TPU v7x, 128 devices: a whole 4x4x4 slice. The times are simulated.
128 devices in a mesh: ex: 32 (over z, x, core), mp: 4 (over y).
Axes of the slice: x: 4, y: 4, z: 4, core: 2. Of those that a mesh axis runs over, the one named last changes fastest.
Arguments:
- tokens: bfloat16 [8192, 1024], P('ex'), may hold values from -6 to 6
- hash_ids: int32 [8192, 1], P('ex'), may hold values from 0 to 63; in each aligned block of 256 rows (0 to 255, 256 to 511, ...) at most 8 rows name the same one
- lengths: int32 [9], replicated, may hold values from 1 to 8064, 8192 in all
- norm1_gain: float32 [1024], replicated, may hold values from 0.5 to 1.5
- qkv_weight: bfloat16 [1024, 3, 1024], P(None, None, 'mp'), may hold values from -0.1875 to 0.1875
- out_weight: bfloat16 [1024, 1024], P('mp'), may hold values from -6 to 6
- norm2_gain: float32 [1024], replicated, may hold values from 0.5 to 1.5
- expert_in: bfloat16 [64, 1024, 4096], P('ex', None, 'mp'), may hold values from -0.1875 to 0.1875
- expert_out: bfloat16 [64, 4096, 1024], P('ex', 'mp'), may hold values from -0.09375 to 0.09375
- cotangent: bfloat16 [8192, 1024], P('ex'), may hold values from -6 to 6
Outputs:
- out: bfloat16 [8192, 1024], P('ex', 'mp')
- input_grad: bfloat16 [8192, 1024], P('ex')
- norm1_gain_grad: float32 [1024], replicated
- qkv_grad: float32 [1024, 3, 1024], P(None, None, 'mp')
- out_weight_grad: float32 [1024, 1024], P('mp')
- norm2_gain_grad: float32 [1024], replicated
- expert_in_grad: float32 [64, 1024, 4096], P('ex', None, 'mp')
- expert_out_grad: float32 [64, 4096, 1024], P('ex', 'mp')
Inputs may be any that keep to these rules, and one draw needn't show every extreme that they name: `hash_ids`: among the 256 rows of one device no expert is named more than 8 times, a bound that some block reaches. The documents lie end to end in the order given, so the lengths sum to 8192; the longest has exactly 8064 tokens.
All inputs are finite; a program needn't handle non-finite values.
Results may differ from a plain program's by a relative error of at most 0.03.
Values may be sent and summed in bfloat16 or wider, within the bound.
A program may use at most 128 MiB of HBM per device.

v0:
```python
import jax
import jax.numpy as jnp
from jax import lax
from jax.sharding import PartitionSpec as P

HEAD_DIM = 64


epsilon = 1e-05
negative_fill = -1e30


def doc_numbers(lengths, first, count):
    doc_ends = jnp.cumsum(lengths)
    positions = first + jnp.arange(count, dtype=jnp.int32)
    return jnp.sum((positions[:, None] >= doc_ends[None, :]).astype(jnp.int32), axis=1)


def norm_forward(inputs, gain_row):
    row_mean = jnp.mean(inputs, axis=-1, keepdims=True)
    centred = inputs - row_mean
    inverse = lax.rsqrt(jnp.mean(centred * centred, axis=-1, keepdims=True) + epsilon)
    normalized = centred * inverse
    return (normalized * gain_row, normalized, inverse)


def norm_backward(grad_out, gain_row, normalized, inverse):
    scaled = grad_out * gain_row
    centred_grad = scaled - jnp.mean(scaled, axis=-1, keepdims=True)
    grad_in = inverse * (
        centred_grad - normalized * jnp.mean(scaled * normalized, axis=-1, keepdims=True)
    )
    return (grad_in, jnp.sum(grad_out * normalized, axis=0))


def over_blocks(state_now, shard_rows, first_row, last_query, step_fn):
    row_count = shard_rows.shape[0]
    block_size = 512
    block_count = row_count // block_size
    stacked = shard_rows.reshape(block_count, block_size, shard_rows.shape[1])

    def visit(state_in, entry_pair):
        key_block = entry_pair[0]
        key_start = first_row + entry_pair[1] * block_size
        state_out = lax.cond(
            key_start <= last_query,
            lambda held_state: step_fn(held_state, key_block, key_start),
            lambda held_state: held_state,
            state_in,
        )
        return (state_out, None)

    state_end, unused = lax.scan(
        visit, state_now, (stacked, jnp.arange(block_count, dtype=jnp.int32))
    )
    return state_end


def on_device(
    tokens,
    hash_ids,
    lengths,
    norm1_gain,
    qkv_weight,
    out_weight,
    norm2_gain,
    expert_in,
    expert_out,
    cotangent,
):
    ex_count = lax.axis_size("ex")
    ex_index = lax.axis_index("ex")
    mp_count = lax.axis_size("mp")
    tok_count = tokens.shape[0]
    model_width = tokens.shape[1]
    head_width = qkv_weight.shape[2]
    head_count = head_width // HEAD_DIM
    scaling = HEAD_DIM ** (-0.5)
    first_query = ex_index * tok_count
    last_query = first_query + tok_count - 1
    query_docs = doc_numbers(lengths, first_query, tok_count)
    query_pos = first_query + jnp.arange(tok_count, dtype=jnp.int32)
    inputs_f = tokens.astype(jnp.float32)
    normed_one, unit_one, inverse_one = norm_forward(inputs_f, norm1_gain)
    normed_low = normed_one.astype(jnp.bfloat16)
    weight_qkv = qkv_weight.reshape(model_width, 3 * head_width)
    projected = jnp.dot(normed_low, weight_qkv, preferred_element_type=jnp.float32).astype(
        jnp.bfloat16
    )
    query_heads = projected[:, :head_width].reshape(tok_count, head_count, HEAD_DIM)
    key_value = projected[:, head_width:]

    def block_scores(key_block, key_start):
        row_count = key_block.shape[0]
        key_heads = key_block[:, :head_width].reshape(row_count, head_count, HEAD_DIM)
        scores = (
            jnp.einsum("qhd,khd->hqk", query_heads, key_heads, preferred_element_type=jnp.float32)
            * scaling
        )
        key_pos = key_start + jnp.arange(row_count, dtype=jnp.int32)
        key_docs = doc_numbers(lengths, key_start, row_count)
        allowed = (key_pos[None, :] <= query_pos[:, None]) & (
            key_docs[None, :] == query_docs[:, None]
        )
        return (scores, allowed[None], key_heads)

    def forward_step(state_in, key_block, key_start):
        row_peak, total_weight, accumulated = state_in
        scores, allowed, key_heads = block_scores(key_block, key_start)
        row_count = key_block.shape[0]
        value_heads = key_block[:, head_width:].reshape(row_count, head_count, HEAD_DIM)
        masked = jnp.where(allowed, scores, negative_fill)
        new_peak = jnp.maximum(row_peak, jnp.max(masked, axis=2))
        factor = jnp.exp(row_peak - new_peak)
        weights = jnp.where(allowed, jnp.exp(masked - new_peak[:, :, None]), 0.0)
        added = jnp.einsum(
            "hqk,khd->qhd",
            weights.astype(jnp.bfloat16),
            value_heads,
            preferred_element_type=jnp.float32,
        )
        accumulated = accumulated * factor.T[:, :, None] + added
        return (new_peak, total_weight * factor + jnp.sum(weights, axis=2), accumulated)

    start_state = (
        jnp.full((head_count, tok_count), negative_fill, jnp.float32),
        jnp.zeros((head_count, tok_count), jnp.float32),
        jnp.zeros((tok_count, head_count, HEAD_DIM), jnp.float32),
    )
    gathered = lax.all_gather(key_value, "ex", axis=0, tiled=True)
    row_peak, total_weight, accumulated = over_blocks(
        start_state, gathered, 0, last_query, forward_step
    )
    attended = accumulated / total_weight.T[:, :, None]
    log_total = row_peak + jnp.log(total_weight)
    attended_low = attended.reshape(tok_count, head_width).astype(jnp.bfloat16)
    branch_part = jnp.dot(attended_low, out_weight, preferred_element_type=jnp.float32)
    residual = inputs_f + lax.psum(branch_part.astype(jnp.bfloat16), "mp").astype(jnp.float32)
    normed_two, unit_two, inverse_two = norm_forward(residual, norm2_gain)
    local_experts = expert_in.shape[0]
    expert_count = local_experts * ex_count
    capacity = 2 * tok_count // expert_count
    chosen = hash_ids[:, 0]
    one_hot = (chosen[:, None] == jnp.arange(expert_count, dtype=jnp.int32)[None, :]).astype(
        jnp.int32
    )
    slot_rank = jnp.sum((jnp.cumsum(one_hot, axis=0) - one_hot) * one_hot, axis=1)
    target = chosen * capacity + slot_rank
    placer = (
        jnp.arange(expert_count * capacity, dtype=jnp.int32)[:, None] == target[None, :]
    ).astype(jnp.bfloat16)
    outgoing = jnp.dot(
        placer, normed_two.astype(jnp.bfloat16), preferred_element_type=jnp.float32
    ).astype(jnp.bfloat16)
    arrived = lax.all_to_all(
        outgoing.reshape(ex_count, local_experts, capacity, model_width),
        "ex",
        split_axis=0,
        concat_axis=2,
        tiled=True,
    )
    expert_rows = arrived.reshape(local_experts, ex_count * capacity, model_width)
    hidden_pre = jnp.einsum(
        "erd,edf->erf", expert_rows, expert_in, preferred_element_type=jnp.float32
    )
    hidden_act, gelu_pull = jax.vjp(jax.nn.gelu, hidden_pre)
    hidden_low = hidden_act.astype(jnp.bfloat16)
    expert_part = jnp.einsum(
        "erf,efd->erd", hidden_low, expert_out, preferred_element_type=jnp.float32
    )
    summed = lax.psum(expert_part.astype(jnp.bfloat16), "mp").astype(jnp.float32)
    columns = summed.shape[2]
    returned = lax.all_to_all(
        summed.astype(jnp.bfloat16).reshape(local_experts, ex_count, capacity, columns),
        "ex",
        split_axis=1,
        concat_axis=0,
        tiled=True,
    )
    branch_rows = jnp.einsum(
        "st,sc->tc",
        placer,
        returned.reshape(expert_count * capacity, columns),
        preferred_element_type=jnp.float32,
    )
    out_width = model_width // mp_count
    out_start = lax.axis_index("mp") * out_width
    output = lax.dynamic_slice_in_dim(residual + branch_rows, out_start, out_width, 1)
    grad_sent = jnp.dot(placer, cotangent, preferred_element_type=jnp.float32).astype(jnp.bfloat16)
    grad_arrived = lax.all_to_all(
        grad_sent.reshape(ex_count, local_experts, capacity, model_width),
        "ex",
        split_axis=0,
        concat_axis=2,
        tiled=True,
    )
    grad_arrived = grad_arrived.reshape(local_experts, ex_count * capacity, model_width)
    grad_hidden = jnp.einsum(
        "erd,efd->erf", grad_arrived, expert_out, preferred_element_type=jnp.float32
    )
    grad_pre = gelu_pull(grad_hidden)[0].astype(jnp.bfloat16)
    expert_out_grad = jnp.einsum(
        "erf,erd->efd", hidden_low, grad_arrived, preferred_element_type=jnp.float32
    )
    expert_in_grad = jnp.einsum(
        "erd,erf->edf", expert_rows, grad_pre, preferred_element_type=jnp.float32
    )
    grad_rows_part = jnp.einsum(
        "erf,edf->erd", grad_pre, expert_in, preferred_element_type=jnp.float32
    )
    grad_rows = lax.psum(grad_rows_part.astype(jnp.bfloat16), "mp")
    grad_back = lax.all_to_all(
        grad_rows.reshape(local_experts, ex_count, capacity, model_width),
        "ex",
        split_axis=1,
        concat_axis=0,
        tiled=True,
    )
    grad_normed_two = jnp.einsum(
        "st,sc->tc",
        placer,
        grad_back.reshape(expert_count * capacity, model_width),
        preferred_element_type=jnp.float32,
    )
    grad_from_two, gain_two_grad = norm_backward(grad_normed_two, norm2_gain, unit_two, inverse_two)
    grad_residual = cotangent.astype(jnp.float32) + grad_from_two
    grad_branch = grad_residual.astype(jnp.bfloat16)
    out_grad_part = jnp.einsum(
        "tc,td->cd", attended_low, grad_branch, preferred_element_type=jnp.float32
    )
    grad_attended = jnp.einsum(
        "td,cd->tc", grad_branch, out_weight, preferred_element_type=jnp.float32
    ).astype(jnp.bfloat16)
    grad_heads = grad_attended.reshape(tok_count, head_count, HEAD_DIM)
    delta_row = jnp.einsum("qhd,qhd->hq", grad_heads.astype(jnp.float32), attended)

    def block_grads(key_block, key_start):
        scores, allowed, key_heads = block_scores(key_block, key_start)
        row_count = key_block.shape[0]
        value_heads = key_block[:, head_width:].reshape(row_count, head_count, HEAD_DIM)
        weights = jnp.exp(jnp.where(allowed, scores - log_total[:, :, None], negative_fill))
        grad_values = jnp.einsum(
            "hqk,qhd->khd",
            weights.astype(jnp.bfloat16),
            grad_heads,
            preferred_element_type=jnp.float32,
        )
        grad_weights = jnp.einsum(
            "qhd,khd->hqk", grad_heads, value_heads, preferred_element_type=jnp.float32
        )
        grad_scores = (weights * (grad_weights - delta_row[:, :, None])).astype(jnp.bfloat16)
        query_added = (
            jnp.einsum("hqk,khd->qhd", grad_scores, key_heads, preferred_element_type=jnp.float32)
            * scaling
        )
        grad_key_rows = (
            jnp.einsum("hqk,qhd->khd", grad_scores, query_heads, preferred_element_type=jnp.float32)
            * scaling
        )
        key_terms = jnp.concatenate(
            [
                grad_key_rows.reshape(row_count, head_width),
                grad_values.reshape(row_count, head_width),
            ],
            axis=1,
        )
        return (query_added, key_terms)

    query_zero = jnp.zeros((tok_count, head_count, HEAD_DIM), jnp.float32)

    def backward_step(state_in, key_block, key_start):
        grad_query_in, grad_keys_in = state_in
        query_added, key_terms = block_grads(key_block, key_start)
        return (
            grad_query_in + query_added,
            lax.dynamic_update_slice_in_dim(grad_keys_in, key_terms, key_start, 0),
        )

    back_state = (query_zero, jnp.zeros((tok_count * ex_count, 2 * head_width), jnp.float32))
    grad_query, grad_keys = over_blocks(back_state, gathered, 0, last_query, backward_step)
    own_keys = lax.psum_scatter(
        grad_keys.astype(jnp.bfloat16), "ex", scatter_dimension=0, tiled=True
    ).astype(jnp.float32)
    grad_projected = jnp.concatenate(
        [grad_query.reshape(tok_count, head_width), own_keys], axis=1
    ).astype(jnp.bfloat16)
    qkv_grad_part = jnp.einsum(
        "td,tc->dc", normed_low, grad_projected, preferred_element_type=jnp.float32
    )
    grad_normed_part = jnp.einsum(
        "tc,dc->td", grad_projected, weight_qkv, preferred_element_type=jnp.float32
    )
    grad_normed_one = lax.psum(grad_normed_part.astype(jnp.bfloat16), "mp").astype(jnp.float32)
    grad_from_one, gain_one_grad = norm_backward(grad_normed_one, norm1_gain, unit_one, inverse_one)
    input_grad = (grad_residual + grad_from_one).astype(jnp.bfloat16)
    qkv_grad, out_weight_grad, norm1_grad, norm2_grad = (
        lax.psum(qkv_grad_part.astype(jnp.bfloat16), "ex").astype(jnp.float32),
        lax.psum(out_grad_part.astype(jnp.bfloat16), "ex").astype(jnp.float32),
        lax.psum(gain_one_grad.astype(jnp.bfloat16), "ex").astype(jnp.float32),
        lax.psum(gain_two_grad.astype(jnp.bfloat16), "ex").astype(jnp.float32),
    )
    return (
        output.astype(jnp.bfloat16),
        input_grad,
        norm1_grad,
        qkv_grad.reshape(model_width, 3, head_width),
        out_weight_grad,
        norm2_grad,
        expert_in_grad,
        expert_out_grad,
    )


def solution(mesh):
    placed = (
        P("ex", None),
        P("ex", None),
        P(),
        P(),
        P(None, None, "mp"),
        P("mp", None),
        P(),
        P("ex", None, "mp"),
        P("ex", "mp", None),
        P("ex", None),
    )
    return jax.shard_map(
        on_device,
        mesh=mesh,
        in_specs=placed,
        out_specs=(
            P("ex", "mp"),
            P("ex", None),
            P(),
            P(None, None, "mp"),
            P("mp", None),
            P(),
            P("ex", None, "mp"),
            P("ex", "mp", None),
        ),
        check_vma=False,
    )
```

profile of v0, /device:TPU:1, one launch (start us, length us, event | category | flops | bytes accessed | tf_op | source)
XLA Modules:
  0.0 845.6 jit_solution(8930775985964746006)
XLA Ops:
  7.3 1.8 copy.51
  9.6 0.7 convolution_convert_fusion.8
  10.3 0.7 slice.36
  11.5 56.3 %all-gather.2.cloned.1.call-done = bf16[8192,512]{1,0:T(8,128)(2,1)} async-done(((bf16[256,512]{1,0:T(8,128)(2,1)}), bf16[8192,512]{1,0:T(8,128)(2,1)}) %all-gather.2.cloned.1.call-update) | async-done | bytes 8388624 | tf_op jit(solution)/shard_map/all_gather | solution.py:130
  67.9 12.3 %copy.53 = bf16[16,512,512]{1,2,0:T(8,128)(2,1)} copy(bf16[16,512,512]{2,1,0:T(8,128)(2,1)} %bitcast.170) | data formatting | bytes 16777216
  80.1 24.2 %while.28 = (s32[]{:T(128)}, f32[4,256]{1,0:T(4,128)S(1)}, f32[4,256]{1,0:T(4,128)S(1)}, f32[256,4,64]{0,2,1:T(8,128)S(1)}, s32[16]{0:T(128)S(1)}, /*index=5*/s3...) while((s32[]{:T(128)}, f32[4,256]{1,0:T(4,128)S(1)}, ...), condition=%wide.region_11.12_spmd.clone, body=%wide.region_4.11_spmd.clone.sunk | while | flops 141574976 | bytes 10173879 | solution.py:53
  80.2 0.6 dynamic_slice.34
  81.4 3.5 conditional.6
  81.9 1.1 dynamic-slice_bitcast_fusion
  84.2 0.7 fusion.7
  87.5 0.6 dynamic_slice.34
  88.8 0.6 dynamic_slice.34
  90.1 0.6 dynamic_slice.34
  91.4 0.6 dynamic_slice.34
  92.7 0.6 dynamic_slice.34
  94.0 0.6 dynamic_slice.34
  95.3 0.6 dynamic_slice.34
  104.4 0.6 copy-done.10
  105.1 1.1 convolution_convert_fusion.6
  106.2 0.6 reduce-window.35
  107.2 90.0 %all-reduce.8.cloned.1.call-done = bf16[256,1024]{1,0:T(8,128)(2,1)} async-done(((bf16[256,1024]{1,0:T(8,128)(2,1)}), bf16[256,1024]{1,0:T(8,128)(2,1)}) %all-reduce.8.cloned.1.call-update) | async-done | bytes 524304 | tf_op jit(solution)/shard_map/psum | solution.py:138
  197.2 1.3 fusion.83
  198.5 1.3 multiply_reduce_fusion.2
  199.9 1.6 convolution_convert_fusion.4
  201.5 9.7 %all-to-all-start = ((bf16[32,2,8,1024]{3,2,1,0:T(8,128)(2,1)}), bf16[32,2,8,1024]{3,2,1,0:T(8,128)(2,1)S(1)}, u32[]{:S(2)}, u32[]{:S(2)}) async-start(bf16[32,2,8,1024]{3,2,1,0:T(8,128)(2,1)} %bitcast.179), calls=%async_computation | async-start | bytes 2097152 | tf_op jit(solution)/shard_map/all_to_all | solution.py:155
  211.2 2.0 convolution_convert_fusion.2
  213.2 15.1 %all-to-all-done = bf16[32,2,8,1024]{3,2,1,0:T(8,128)(2,1)S(1)} async-done(((bf16[32,2,8,1024]{3,2,1,0:T(8,128)(2,1)}), bf16[32,2,8,1024]{3,2,1,0:T(8,128)(2,1)S(1)}, u32[]{:S(2)}, u32[]{:S(2)}) %all-to-all-start) | async-done | bytes 1048608 | tf_op jit(solution)/shard_map/all_to_all | solution.py:155
  228.4 4.6 all-to-all-start.2
  233.1 4.8 fusion.55
  237.8 12.5 %all-to-all-done.2 = bf16[32,2,8,1024]{3,2,1,0:T(8,128)(2,1)} async-done(((bf16[32,2,8,1024]{3,2,1,0:T(8,128)(2,1)}), bf16[32,2,8,1024]{3,2,1,0:T(8,128)(2,1)}, u32[]{:S(2)}, u32[]{:S(2)}) %all-to-all-start.2) | async-done | bytes 1048608 | tf_op jit(solution)/shard_map/all_to_all | solution.py:190
  250.4 5.6 fusion.29
  256.0 1.3 fusion.31
  257.3 1.1 copy.58
  258.4 41.2 %all-reduce.10.cloned.1.call-done = bf16[2,32,8,1024]{3,2,0,1:T(8,128)(2,1)} async-done(((bf16[2,32,8,1024]{3,2,0,1:T(8,128)(2,1)}), bf16[2,32,8,1024]{3,2,0,1:T(8,128)(2,1)}) %all-reduce.10.cloned.1.call-update) | async-done | bytes 1048592 | tf_op jit(solution)/shard_map/psum | solution.py:211
  299.7 9.1 %all-to-all-start.3 = ((bf16[2,32,8,1024]{3,2,0,1:T(8,128)(2,1)}), bf16[2,32,8,1024]{3,2,0,1:T(8,128)(2,1)S(1)}, u32[]{:S(2)}, u32[]{:S(2)}) async-start(bf16[2,32,8,1024]{3,2,0,1:T(8,128)(2,1)} %all-reduce.10.cloned.1.call-done), calls=%async_computation.3 | async-start | bytes 2097152 | tf_op jit(solution)/shard_map/all_to_all | solution.py:212
  308.8 0.6 log_add_fusion
  309.4 16.5 %all-to-all-done.3 = bf16[2,32,8,1024]{3,2,0,1:T(8,128)(2,1)S(1)} async-done(((bf16[2,32,8,1024]{3,2,0,1:T(8,128)(2,1)}), bf16[2,32,8,1024]{3,2,0,1:T(8,128)(2,1)S(1)}, u32[]{:S(2)}, u32[]{:S(2)}) %all-to-all-start.3) | async-done | bytes 1048608 | tf_op jit(solution)/shard_map/all_to_all | solution.py:212
  325.9 3.0 multiply_reduce_fusion
  329.9 4.4 broadcast_in_dim.50
  334.3 30.3 %while.29 = (s32[]{:T(128)}, f32[256,4,64]{0,2,1:T(8,128)S(1)}, bf16[8192,512]{0,1:T(8,128)(2,1)}, s32[16]{0:T(128)S(1)}, s32[]{:T(128)}, /*index=5*/s32[9]{0:T(...) while((s32[]{:T(128)}, f32[256,4,64]{0,2,1:T(8,128)S(1)}, ...), condition=%wide.region_27.28_spmd.clone, body=%wide.region_22.27_spmd.clone.sunk | while | flops 341063488 | bytes 16276973 | solution.py:53
  335.5 9.6 %conditional.7 = ((f32[256,4,64]{0,2,1:T(8,128)S(1)}, bf16[8192,512]{0,1:T(8,128)(2,1)})) conditional(s32[]{:T(128)} %convert_element_type.284, (f32[256,4,64]{0,2,1:T(8,128)S(1)}, bf16[8192,512]{0,1:T(8,128)(2,1)}) %tuple.89, (s32[]{:T(128)}, s32[]{:T(128)}, s32[9]{0:T(128)S(1)}, s32[256]{0:T(256)S(1)}, bf16[16,512,512]{1,2,0:T(8,128)(2,1)}, ...), branch_computations={%region_23.23_spmd, %region_24.26_spmd} | conditional | flops 341063488 | bytes 16275642 | solution.py:45
  335.6 1.1 dynamic-slice_bitcast_fusion.1
  337.2 0.7 fusion.18
  339.6 5.5 dynamic_update_slice.3
  364.6 4.2 fusion.30
  368.9 1.1 copy.56
  370.0 225.6 %reduce-scatter.2.cloned.1.call-done = bf16[256,512]{0,1:T(8,128)(2,1)} async-done(((bf16[8192,512]{0,1:T(8,128)(2,1)}), bf16[256,512]{0,1:T(8,128)(2,1)}) %reduce-scatter.2.cloned.1.call-update) | async-done | bytes 262160 | tf_op jit(solution)/shard_map/reduce_scatter | solution.py:281
  595.5 2.9 convolution_convert_fusion.7
  598.5 1.2 convolution_convert_fusion.5
  599.7 1.8 convolution_convert_fusion
  601.6 2.6 copy.60
  604.2 6.7 fusion.47
  610.9 39.2 %all-reduce.14.cloned.1.call-done = (bf16[2,32,8,1024]{3,2,0,1:T(8,128)(2,1)}, bf16[256,1024]{1,0:T(8,128)(2,1)}) async-done(((bf16[2,32,8,1024]{3,2,0,1:T(8,128)(2,1)}, bf16[256,1024]{1,0:T(8,128)(2,1)}), (bf16[2,32,8,1024]{3,2,0,1:T(8,128)(2,1)}, bf16[256,1024]{1,0:T(8,128)(2,1)})) %all-reduce.14.cloned.1.call-update) | async-done | bytes 1572880 | tf_op jit(solution)/shard_map/psum | solution.py:171
  650.1 7.9 all-to-all-start.1
  658.0 5.9 fusion.53
  663.9 101.2 %all-reduce.12.cloned.1.call-done = (bf16[1024,3,256]{2,0,1:T(8,128)(2,1)}, bf16[256,1024]{1,0:T(8,128)(2,1)}) async-done(((bf16[1024,3,256]{2,0,1:T(8,128)(2,1)}, bf16[256,1024]{1,0:T(8,128)(2,1)}), (bf16[1024,3,256]{2,0,1:T(8,128)(2,1)}, bf16[256,1024]{1,0:T(8,128)(2,1)})) %all-reduce.12.cloned.1.call-update) | async-done | bytes 2097168 | tf_op jit(solution)/shard_map/psum | solution.py:297
  765.1 3.4 reshape.389
  768.5 1.1 convert_element_type.159
  770.2 62.8 %all-reduce = (bf16[1024]{0:T(1024)(128)(2,1)S(1)}, bf16[1024]{0:T(1024)(128)(2,1)S(1)}) all-reduce(bf16[1024]{0:T(1024)(128)(2,1)S(1)} %get-tuple-element.411, bf16[1024]{0:T(1024)(128)(2,1)S(1)} %copy-done.28), channel_id=1, replica_groups=mesh['ex'=32,'mp'=4] {'ex'}, use_global_device_ids=true, to_apply=%region_33.34 | all-reduce | flops 2048 | bytes 8192 | tf_op jit(solution)/shard_map/psum | solution.py:299
  832.9 0.6 convert_element_type.156
  833.5 0.6 convert_element_type.161
  834.1 1.2 fusion.43
  835.4 1.7 fusion.65
  837.1 1.6 fusion.66
  (215 shorter events, 21.8 us)
Async XLA Ops:
  7.2 97.9 %copy-start = (bf16[256,1024]{1,0:T(8,128)(2,1)S(1)}, bf16[256,1024]{1,0:T(8,128)(2,1)}, u32[]{:S(2)}) copy-start(bf16[256,1024]{1,0:T(8,128)(2,1)} %param.23) | copy-start | bytes 1572868
  7.2 1.9 copy-start.2
  7.2 2.3 copy-start.15
  7.2 60.6 %all-gather.2.cloned.1.call-start = ((), (), s32[]{:S(2)}) async-start(), calls=%async_computation.5 | async-start | bytes 8650752 | tf_op jit(solution)/shard_map/all_gather | solution.py:130
  9.1 1.2 copy-start.6
  9.5 1.6 copy-start.23
  9.5 1.6 copy-start.30
  11.0 186.1 %all-reduce.8.cloned.1.call-start = ((), (), s32[]{:S(2)}) async-start(), calls=%async_computation.6 | async-start | bytes 1048576 | tf_op jit(solution)/shard_map/psum | solution.py:138
  104.3 1.9 copy-start.25
  104.4 0.7 copy-start.10
  104.4 95.5 %copy-start.21 = (f32[1024]{0:T(1024)S(1)}, f32[1024]{0:T(1024)}, u32[]{:S(2)}) copy-start(f32[1024]{0:T(1024)} %param.24) | copy-start | bytes 12292
  107.2 94.3 %copy-start.17 = (s32[256]{0:T(256)}, s32[256]{0:T(256)S(1)}, u32[]{:S(2)}) copy-start(s32[256]{0:T(256)S(1)} %multiply_add_fusion.2) | copy-start | bytes 3076
  197.2 2.7 copy-start.5
  198.5 3.0 copy-start.19
  199.9 1.6 copy-start.26
  199.9 11.3 %copy-start.9 = (bf16[256,1024]{1,0:T(8,128)(2,1)S(1)}, bf16[256,1024]{1,0:T(8,128)(2,1)}, u32[]{:S(2)}) copy-start(bf16[256,1024]{1,0:T(8,128)(2,1)} %param.27) | copy-start | bytes 1572868
  201.5 26.9 %all-to-all-start = ((bf16[32,2,8,1024]{3,2,1,0:T(8,128)(2,1)}), bf16[32,2,8,1024]{3,2,1,0:T(8,128)(2,1)S(1)}, u32[]{:S(2)}, u32[]{:S(2)}) async-start(bf16[32,2,8,1024]{3,2,1,0:T(8,128)(2,1)} %bitcast.179), calls=%async_computation | async-start | bytes 2097152 | tf_op jit(solution)/shard_map/all_to_all | solution.py:155
  228.4 9.5 %copy-start.3 = (bf16[32,2,8,1024]{3,2,1,0:T(8,128)(2,1)}, bf16[32,2,8,1024]{3,2,1,0:T(8,128)(2,1)S(1)}, u32[]{:S(2)}) copy-start(bf16[32,2,8,1024]{3,2,1,0:T(8,128)(2,1)S(1)} %all-to-all-done) | copy-start | bytes 3145732
  228.4 22.0 %all-to-all-start.2 = ((bf16[32,2,8,1024]{3,2,1,0:T(8,128)(2,1)}), bf16[32,2,8,1024]{3,2,1,0:T(8,128)(2,1)}, u32[]{:S(2)}, u32[]{:S(2)}) async-start(bf16[32,2,8,1024]{3,2,1,0:T(8,128)(2,1)} %bitcast.174), calls=%async_computation.2 | async-start | bytes 2097152 | tf_op jit(solution)/shard_map/all_to_all | solution.py:190
  233.0 66.6 %all-reduce.10.cloned.1.call-start = ((), (), s32[]{:S(2)}) async-start(), calls=%async_computation.7 | async-start | bytes 2097152 | tf_op jit(solution)/shard_map/psum | solution.py:211
  250.4 5.7 copy-start.7
  256.0 1.3 copy-start.12
  299.7 26.3 %all-to-all-start.3 = ((bf16[2,32,8,1024]{3,2,0,1:T(8,128)(2,1)}), bf16[2,32,8,1024]{3,2,0,1:T(8,128)(2,1)S(1)}, u32[]{:S(2)}, u32[]{:S(2)}) async-start(bf16[2,32,8,1024]{3,2,0,1:T(8,128)(2,1)} %all-reduce.10.cloned.1.call-done), calls=%async_computation.3 | async-start | bytes 2097152 | tf_op jit(solution)/shard_map/all_to_all | solution.py:212
  308.7 286.8 %reduce-scatter.2.cloned.1.call-start = ((), (), s32[]{:S(2)}) async-start(), calls=%async_computation.8 | async-start | bytes 8650752 | tf_op jit(solution)/shard_map/reduce_scatter | solution.py:281
  325.9 3.0 copy-start.20
  325.9 3.0 copy-start.22
  325.9 3.0 copy-start.27
  329.9 4.4 copy-start.29
  329.9 4.4 copy-start.31
  364.6 285.5 %all-reduce.14.cloned.1.call-start = ((), (), s32[]{:S(2)}) async-start(), calls=%async_computation.10 | async-start | bytes 3145728 | tf_op jit(solution)/shard_map/psum | solution.py:171
  370.0 228.6 %copy-start.11 = (bf16[256,4,64]{0,2,1:T(8,128)(2,1)S(1)}, bf16[256,4,64]{0,2,1:T(8,128)(2,1)}, u32[]{:S(2)}) copy-start(bf16[256,4,64]{0,2,1:T(8,128)(2,1)} %copy-done.10) | copy-start | bytes 393220
  598.5 1.3 copy-start.14
  598.5 1.3 copy-start.16
  598.5 1.3 copy-start.24
  598.5 166.6 %all-reduce.12.cloned.1.call-start = ((), (), s32[]{:S(2)}) async-start(), calls=%async_computation.9 | async-start | bytes 4194304 | tf_op jit(solution)/shard_map/psum | solution.py:297
  610.9 47.1 %copy-start.4 = (bf16[32,2,8,1024]{3,2,1,0:T(8,128)(2,1)S(1)}, bf16[32,2,8,1024]{3,2,1,0:T(8,128)(2,1)}, u32[]{:S(2)}) copy-start(bf16[32,2,8,1024]{3,2,1,0:T(8,128)(2,1)} %copy-done.3) | copy-start | bytes 3145732
  650.1 185.3 %all-to-all-start.1 = ((bf16[2,32,8,1024]{3,2,0,1:T(8,128)(2,1)}), bf16[2,32,8,1024]{3,2,0,1:T(8,128)(2,1)}, u32[]{:S(2)}, u32[]{:S(2)}) async-start(bf16[2,32,8,1024]{3,2,0,1:T(8,128)(2,1)} %get-tuple-element.466), calls=%async_computation.1 | async-start | bytes 2097152 | tf_op jit(solution)/shard_map/all_to_all | solution.py:173
  765.1 3.4 copy-start.13
  765.1 4.5 copy-start.8
  768.5 1.7 copy-start.28
  769.6 65.8 %copy-start.18 = (s32[256]{0:T(256)S(1)}, s32[256]{0:T(256)}, u32[]{:S(2)}) copy-start(s32[256]{0:T(256)} %copy-done.17) | copy-start | bytes 3076
  834.1 4.6 copy-start.1
Sparse Core Ops, SparseCore 0:
  11.2 56.6 all-gather.1
  106.3 90.8 all-reduce.7
  258.6 41.0 all-reduce.9
  364.7 230.7 reduce-scatter.1
  598.6 51.4 all-reduce.13
  653.3 111.7 all-reduce.11
where the time goes:
time: 853 us; the launch traced here: 846 us
  waiting for transfers between devices  598 us (70%)
  blocking collectives  62.8 us (7%)
  local copies, waits for them, and re-layouts  51.7 us (6%)
  matrix products  48.5 us (6%)
  starting transfers between devices  31.5 us (4%)
  loops' own time  22.7 us (3%)
  other arithmetic  16 us (2%)
  between operations  14.6 us (2%)
    reduce_scatter x1, waiting for transfers between devices, on_device(): lax.psum_scatter(grad_keys.astype(jnp.bfloat16), 'ex', scatter_dimension=...  226 us
    psum x1, waiting for transfers between devices, on_device(): lax.psum(qkv_grad_part.astype(jnp.bfloat16), 'ex').astype(jnp.float32)  101 us
    psum x1, waiting for transfers between devices, on_device(): lax.psum(branch_part.astype(jnp.bfloat16), 'mp').astype(jnp.float32)  90 us
    psum x1, blocking collectives, on_device(): lax.psum(gain_one_grad.astype(jnp.bfloat16), 'ex').astype(jnp.float32)  62.8 us
    all_gather x1, waiting for transfers between devices, on_device(): gathered = lax.all_gather(key_value, 'ex', axis=0, tiled=True)  56.3 us
    psum x1, waiting for transfers between devices, on_device(): grad_rows = lax.psum(grad_rows_part.astype(jnp.bfloat16), 'mp')  41.2 us
    psum x1, waiting for transfers between devices, on_device(): lax.psum(expert_part.astype(jnp.bfloat16), 'mp').astype(jnp.float32)  39.2 us
    another operation x2, loops' own time, over_blocks(): lax.scan(visit, state_now, (stacked, jnp.arange(block_count, dtype=jnp.in...  22.1 us
  transfers between devices with their start and end apart: 10, of which 9 were waited for; matrix products, arithmetic and copies ran while one was open for 5% of the time, Pallas kernels for 0%

commit v1 on v0

v1 whole, which is shorter than its diff:
```python
import functools

import jax
import jax.numpy as jnp
from jax import lax
from jax.experimental import pallas as pl
from jax.experimental.pallas import tpu as pltpu
from jax.sharding import PartitionSpec as P

HEAD_DIM = 64
epsilon = 1e-05
negative_fill = -1e30
MESH = pl.DeviceIdType.MESH
bf16, f32 = jnp.bfloat16, jnp.float32
EX, MP = 32, 4


def dot(a, b, ca=1, cb=0):
    return lax.dot_general(a, b, (((ca,), (cb,)), ((), ())), preferred_element_type=f32)


def place():
    ex, mp = lax.axis_index("ex"), lax.axis_index("mp")
    z, x, c = ex // 8, (ex // 2) % 4, ex % 2
    return ex, mp, z, x, c


def send(src, dst, ssem, rsem, device):
    copy = pltpu.make_async_remote_copy(
        src_ref=src, dst_ref=dst, send_sem=ssem, recv_sem=rsem, device_id=device, device_id_type=MESH
    )
    copy.start()
    return copy


def greet(ex, mp):
    bar = pltpu.get_barrier_semaphore()

    def one(d, carry):
        pl.semaphore_signal(bar, inc=1, device_id=(lax.rem(ex + d, EX), mp), device_id_type=MESH)
        return carry

    lax.fori_loop(1, EX, one, 0)
    for d in range(1, MP):
        pl.semaphore_signal(bar, inc=1, device_id=(ex, lax.rem(mp + d, MP)), device_id_type=MESH)
    return bar


def greeted(bar):
    pl.semaphore_wait(bar, EX - 1 + MP - 1)


def slot_matrix(chosen_row):
    tok = chosen_row.shape[1]
    experts = lax.broadcasted_iota(jnp.int32, (64, tok), 0)
    hot = (experts == chosen_row).astype(f32)
    rows = lax.broadcasted_iota(jnp.int32, (tok, tok), 0)
    cols = lax.broadcasted_iota(jnp.int32, (tok, tok), 1)
    before = (rows < cols).astype(bf16)
    earlier = dot(hot.astype(bf16), before)
    rank = jnp.sum(earlier * hot, axis=0, keepdims=True)
    target = chosen_row * 8 + rank.astype(jnp.int32)
    slots = lax.broadcasted_iota(jnp.int32, (512, tok), 0)
    return (slots == target).astype(f32).astype(bf16)


def doc_row(ends, first, count):
    pos = first + lax.broadcasted_iota(jnp.int32, (1, count), 1)
    row = jnp.zeros((1, count), jnp.int32)
    for end in ends:
        row = row + (pos >= end).astype(jnp.int32)
    return row


def doc_ends(lengths_ref):
    ends, total = [], 0
    for i in range(9):
        total = total + lengths_ref[i]
        ends.append(total)
    return ends


def norm_parts(v):
    mean = jnp.mean(v, axis=-1, keepdims=True)
    centred = v - mean
    inverse = lax.rsqrt(jnp.mean(centred * centred, axis=-1, keepdims=True) + epsilon)
    return centred * inverse, inverse


def transposed(v):
    return v.T


def front_kernel(
    lengths, tokens, gain, chosen, wqkv_hbm, wout, cot,
    normed_out, kvt, q_out, ot_out, lse_out, att, cot_rows, wfull,
    wqkv, q_s, kv_s, qaug, kaug, vt1, acc, peak, o_s, outgoing,
    wsem, az_s, az_r, ag_s, ag_r, cot_s, cot_r, oz_s, oz_r, oy_s, oy_r, wf_s, wf_r,
):
    ex, mp, z, x, c = place()
    d = 1 - 2 * c
    j = x * 2 + c
    bar = greet(ex, mp)
    wcopy = pltpu.make_async_copy(wqkv_hbm, wqkv, wsem)
    wcopy.start()
    unit, _ = norm_parts(tokens[...].astype(f32))
    normed = (unit * gain[...]).astype(bf16)
    normed_out[...] = normed
    wcopy.wait()
    qt = transposed((dot(normed, wqkv[0]).astype(bf16) * HEAD_DIM ** (-0.5)).astype(bf16))
    kt = transposed(dot(normed, wqkv[1]).astype(bf16))
    vt = transposed(dot(normed, wqkv[2]).astype(bf16))
    for h in range(4):
        q_s[h] = qt[64 * h:64 * h + 64]
        kv_s[h, 0:64] = kt[64 * h:64 * h + 64]
        kv_s[h, 64:128] = vt[64 * h:64 * h + 64]
    greeted(bar)
    zsends = []
    for i in range(1, 4):
        zp = lax.rem(z + i, 4)
        to = (zp * 8 + j, mp)
        zsends.append(send(kv_s.at[zp], kvt.at[0, z], az_s.at[i - 1], az_r.at[i - 1], to))
        zsends.append(send(q_s.at[zp], q_out.at[z], az_s.at[i + 2], az_r.at[i + 2], to))
    wsends = []
    for i in range(1, 4):
        wsends.append(
            send(wout, wfull.at[mp], wf_s.at[i - 1], wf_r.at[i - 1], (ex, lax.rem(mp + i, MP)))
        )
    kvt[0, z] = kv_s[z]
    q_out[z] = q_s[z]
    wfull[mp] = wout[...]
    vt1[64:80, :] = jnp.ones((16, 1024), bf16)
    ends = doc_ends(lengths)
    experts_rows = dot(slot_matrix(chosen[...]), cot[...]).astype(bf16)
    outgoing[...] = experts_rows.reshape(EX, 16, 1024)
    cot_rows[ex] = outgoing[ex]
    feature = lax.broadcasted_iota(jnp.int32, (64, 256), 0)
    for i in range(1, 4):
        zp = lax.rem(z + 4 - i, 4)
        pltpu.make_async_remote_copy(
            src_ref=kv_s.at[zp], dst_ref=kvt.at[0, zp], send_sem=az_s.at[i - 1], recv_sem=az_r.at[i - 1],
            device_id=(zp * 8 + j, mp), device_id_type=MESH).wait_recv()
    sib = (ex + d, mp)
    ahead = (z * 8 + lax.rem(x + d + 4, 4) * 2 + c, mp)
    behind = (z * 8 + lax.rem(x - d + 4, 4) * 2 + c, mp)
    asends = [
        send(kvt.at[0], kvt.at[2], ag_s.at[1], ag_r.at[2], ahead),
        send(kvt.at[0], kvt.at[6], ag_s.at[2], ag_r.at[6], behind),
        send(kvt.at[0], kvt.at[1], ag_s.at[0], ag_r.at[1], sib),
    ]

    def came(slot):
        pltpu.make_async_remote_copy(
            src_ref=kvt.at[0], dst_ref=kvt.at[slot], send_sem=ag_s.at[0], recv_sem=ag_r.at[slot],
            device_id=sib, device_id_type=MESH).wait_recv()

    for i in range(1, 4):
        zp = lax.rem(z + 4 - i, 4)
        pltpu.make_async_remote_copy(
            src_ref=q_s.at[zp], dst_ref=q_out.at[zp], send_sem=az_s.at[i + 2], recv_sem=az_r.at[i + 2],
            device_id=(zp * 8 + j, mp), device_id_type=MESH).wait_recv()
    for b in range(4):
        docs = doc_row(ends, (b * 8 + j) * 256, 256)
        qaug[b, 0:64] = q_out[b]
        qaug[b, 64:128] = jnp.where(feature == docs, 0.0, negative_fill).astype(bf16)
        peak[b] = jnp.full((1, 256), negative_fill, f32)
        acc[b] = jnp.zeros((80, 256), f32)

    def load_chunk(slot, jp):
        for b in range(4):
            docs = doc_row(ends, (b * 8 + jp) * 256, 256)
            hot = (feature == docs).astype(f32).astype(bf16)
            block = kvt[slot, b]
            kaug[256 * b:256 * b + 256, :] = transposed(jnp.concatenate([block[0:64], hot], axis=0))
            vt1[0:64, 256 * b:256 * b + 256] = block[64:128]

    def update(b, n, causal):
        s = dot(kaug[0:n, :], qaug[b])
        if causal:
            rows = lax.broadcasted_iota(jnp.int32, (n, 256), 0)
            cols = lax.broadcasted_iota(jnp.int32, (n, 256), 1)
            s = jnp.where(rows - 256 * b <= cols, s, negative_fill)
        old = peak[b]
        new = jnp.maximum(old, jnp.max(s, axis=0, keepdims=True))
        p = jnp.exp(s - new).astype(bf16)
        acc[b] = acc[b] * jnp.exp(old - new) + dot(vt1[:, 0:n], p)
        peak[b] = new

    load_chunk(0, j)
    for b in range(4):
        update(b, 256 * b + 256, True)

    def chunk(i, carry):
        t = i + (i // 4) * (2 - 4 * ((i // 2) % 2))
        jp = ((x - d * (t // 2) + 8) % 4) * 2 + (c + t) % 2

        @pl.when(i == 1)
        def _():
            came(1)

        @pl.when(i == 2)
        def _():
            came(2)
            send(kvt.at[2], kvt.at[4], ag_s.at[3], ag_r.at[4], ahead)
            send(kvt.at[2], kvt.at[7], ag_s.at[4], ag_r.at[7], sib)
            came(6)
            send(kvt.at[6], kvt.at[3], ag_s.at[5], ag_r.at[3], sib)

        @pl.when(i == 3)
        def _():
            came(3)

        @pl.when(i == 4)
        def _():
            came(4)
            send(kvt.at[4], kvt.at[5], ag_s.at[6], ag_r.at[5], sib)

            def cot_send(k, carry):
                to = lax.rem(ex + k, EX)
                send(outgoing.at[to], cot_rows.at[ex], cot_s.at[k - 1], cot_r.at[k - 1], (to, mp))
                return carry

            lax.fori_loop(1, EX, cot_send, 0)

        @pl.when(i == 5)
        def _():
            came(7)

        @pl.when(i == 7)
        def _():
            came(5)

        load_chunk(t, jp)

        @pl.when(jp < j)
        def _():
            for b in range(4):
                update(b, 256 * b + 256, False)

        @pl.when(jp > j)
        def _():
            for b in range(1, 4):
                update(b, 256 * b, False)

        return carry

    lax.fori_loop(1, 8, chunk, 0)
    for b in range(4):
        total = acc[b, 64:65]
        ot = acc[b, 0:64] / total
        ot_out[b] = ot
        lse_out[b] = peak[b] + jnp.log(total)
        o_s[b] = ot.astype(bf16)
    osends = []
    for i in range(1, 4):
        zp = lax.rem(z + i, 4)
        osends.append(send(o_s.at[zp], att.at[mp, z], oz_s.at[i - 1], oz_r.at[i - 1], (zp * 8 + j, mp)))
    att[mp, z] = o_s[z]
    for i in range(1, 4):
        zp = lax.rem(z + 4 - i, 4)
        pltpu.make_async_remote_copy(
            src_ref=o_s.at[zp], dst_ref=att.at[mp, zp], send_sem=oz_s.at[i - 1], recv_sem=oz_r.at[i - 1],
            device_id=(zp * 8 + j, mp), device_id_type=MESH).wait_recv()
    ysends = []
    for i in range(1, 4):
        ysends.append(send(att.at[mp], att.at[mp], oy_s.at[i - 1], oy_r.at[i - 1], (ex, lax.rem(mp + i, MP))))
    for i in range(1, 4):
        ym = lax.rem(mp + 4 - i, MP)
        pltpu.make_async_remote_copy(
            src_ref=att.at[mp], dst_ref=att.at[ym], send_sem=oy_s.at[i - 1], recv_sem=oy_r.at[i - 1],
            device_id=(ex, ym), device_id_type=MESH).wait_recv()
        pltpu.make_async_remote_copy(
            src_ref=wout, dst_ref=wfull.at[ym], send_sem=wf_s.at[i - 1], recv_sem=wf_r.at[i - 1],
            device_id=(ex, ym), device_id_type=MESH).wait_recv()

    def cot_wait(k, carry):
        to, back = lax.rem(ex + k, EX), lax.rem(ex + EX - k, EX)
        copy = pltpu.make_async_remote_copy(
            src_ref=outgoing.at[to], dst_ref=cot_rows.at[back], send_sem=cot_s.at[k - 1],
            recv_sem=cot_r.at[k - 1], device_id=(to, mp), device_id_type=MESH)
        copy.wait_send()
        copy.wait_recv()
        return carry

    lax.fori_loop(1, EX, cot_wait, 0)
    for copy in zsends + wsends + asends + osends + ysends:
        copy.wait_send()
    for i in range(3, 7):
        pltpu.make_async_remote_copy(
            src_ref=kvt.at[0], dst_ref=kvt.at[1], send_sem=ag_s.at[i], recv_sem=ag_r.at[1],
            device_id=sib, device_id_type=MESH).wait_send()


VM = pl.BlockSpec(memory_space=pltpu.VMEM)
SM = pl.BlockSpec(memory_space=pltpu.SMEM)
ANY = pl.BlockSpec(memory_space=pl.ANY)
DMA = pltpu.SemaphoreType.DMA


def front(lengths, tokens, gain, chosen, wqkv, wout, cot):
    outs = [
        ((256, 1024), bf16), ((8, 4, 128, 256), bf16), ((4, 64, 256), bf16), ((4, 64, 256), f32),
        ((4, 1, 256), f32), ((4, 4, 64, 256), bf16), ((32, 16, 1024), bf16), ((4, 256, 1024), bf16),
    ]
    return pl.pallas_call(
        front_kernel,
        out_shape=[jax.ShapeDtypeStruct(s, t) for s, t in outs],
        in_specs=[SM, VM, VM, VM, ANY, VM, VM],
        out_specs=[VM] * 8,
        scratch_shapes=[
            pltpu.VMEM((3, 1024, 256), bf16), pltpu.VMEM((4, 64, 256), bf16), pltpu.VMEM((4, 128, 256), bf16),
            pltpu.VMEM((4, 128, 256), bf16), pltpu.VMEM((1024, 128), bf16), pltpu.VMEM((80, 1024), bf16),
            pltpu.VMEM((4, 80, 256), f32), pltpu.VMEM((4, 1, 256), f32), pltpu.VMEM((4, 64, 256), bf16),
            pltpu.VMEM((32, 16, 1024), bf16),
            DMA, DMA((6,)), DMA((6,)), DMA((7,)), DMA((8,)), DMA((31,)), DMA((31,)),
            DMA((3,)), DMA((3,)), DMA((3,)), DMA((3,)), DMA((3,)), DMA((3,)),
        ],
        name="front",
        compiler_params=pltpu.CompilerParams(
            collective_id=0, has_side_effects=True, vmem_limit_bytes=56 << 20),
    )(lengths, tokens, gain, chosen, wqkv, wout, cot)
def norm_back(grad_out, gain_row, unit, inverse):
    scaled = grad_out * gain_row
    centred = scaled - jnp.mean(scaled, axis=-1, keepdims=True)
    grad_in = inverse * (centred - unit * jnp.mean(scaled * unit, axis=-1, keepdims=True))
    return grad_in, jnp.sum(grad_out * unit, axis=0, keepdims=True)


def gelu_parts(pre):
    k = 0.7978845608028654
    square = pre * pre
    t = jnp.tanh(k * pre * (1.0 + 0.044715 * square))
    half = 0.5 * (1.0 + t)
    slope = half + 0.5 * pre * (1.0 - t * t) * (k * (1.0 + 3 * 0.044715 * square))
    return pre * half, slope


def one_expert(rows, le):
    wide = rows.astype(f32)
    return wide[:, 8 * le:8 * le + 8].reshape(256, rows.shape[2]).astype(bf16)


def both_experts(first, second):
    width = first.shape[1]
    return jnp.concatenate([first.reshape(32, 8, width), second.reshape(32, 8, width)], axis=1).astype(bf16)


def middle_kernel(
    att, wfull, tokens, cot, gain, chosen, cot_hbm, win_hbm, wex_hbm,
    x_out, c_out, hid_out, gpre_out, branch_out, rescol_out, gres_out, dot_out, wgrad_out, ggrad_out,
    win, wex, cot_rows, outgoing, arrived, gh, part, rs, back_s, back, gn, resid,
    csem, wsem, di_s, di_r, rs_s, rs_r, ba_s, ba_r, gy_s, gy_r,
):
    ex, mp, z, x, c = place()
    bar = greet(ex, mp)
    copies = [
        pltpu.make_async_copy(cot_hbm, cot_rows, csem),
        pltpu.make_async_copy(wex_hbm, wex, wsem.at[0]),
        pltpu.make_async_copy(win_hbm, win, wsem.at[1]),
    ]
    for copy in copies:
        copy.start()
    placer = slot_matrix(chosen[...])
    branch = dot(att[...].reshape(1024, 256), wfull[...].reshape(1024, 1024), 0, 0)
    value = tokens[...].astype(f32) + branch
    resid[...] = value
    for q in range(4):
        @pl.when(mp == q)
        def _():
            rescol_out[...] = value[:, 256 * q:256 * q + 256]
    unit, inverse = norm_parts(value)
    outgoing[...] = dot(placer, (unit * gain[...]).astype(bf16)).astype(bf16).reshape(EX, 16, 1024)
    greeted(bar)

    def dispatch(k, carry):
        to = lax.rem(ex + k, EX)
        send(outgoing.at[to], arrived.at[ex], di_s.at[k - 1], di_r.at[k - 1], (to, mp))
        return carry

    lax.fori_loop(1, EX, dispatch, 0)
    arrived[ex] = outgoing[ex]
    copies[0].wait()
    copies[1].wait()
    for le in range(2):
        rows = one_expert(cot_rows[...], le)
        c_out[le] = rows
        gh[le] = dot(rows, wex[le], 1, 1)
    copies[2].wait()

    def dispatched(k, carry):
        to, source = lax.rem(ex + k, EX), lax.rem(ex + EX - k, EX)
        copy = pltpu.make_async_remote_copy(
            src_ref=outgoing.at[to], dst_ref=arrived.at[source], send_sem=di_s.at[k - 1],
            recv_sem=di_r.at[k - 1], device_id=(to, mp), device_id_type=MESH)
        copy.wait_send()
        copy.wait_recv()
        return carry

    lax.fori_loop(1, EX, dispatched, 0)
    sends = []
    for le in range(2):
        rows = one_expert(arrived[...], le)
        x_out[le] = rows
        hidden, slope = gelu_parts(dot(rows, win[le]))
        hid_out[le] = hidden.astype(bf16)
        gpre = (gh[le] * slope).astype(bf16)
        gpre_out[le] = gpre
        for q in range(4):
            part[le, q] = dot(gpre, win[le, 256 * q:256 * q + 256, :], 1, 1).astype(bf16)
        for i in range(1, 4):
            ym = lax.rem(mp + i, MP)
            sends.append(
                send(part.at[le, ym], rs.at[le, i - 1], rs_s.at[3 * le + i - 1], rs_r.at[3 * le + i - 1], (ex, ym)))
    firsts = dot(hid_out[0], wex[0])
    branch_out[...] = both_experts(firsts, dot(hid_out[1], wex[1]))
    sums = []
    for le in range(2):
        total = part[le, mp].astype(f32)
        for i in range(1, 4):
            sends[3 * le + i - 1].wait_recv()
            total = total + rs[le, i - 1].astype(f32)
        sums.append(total)
    back_s[...] = both_experts(sums[0], sums[1])

    def give(k, carry):
        to = lax.rem(ex + k, EX)
        send(back_s.at[to], back.at[ex], ba_s.at[k - 1], ba_r.at[k - 1], (to, mp))
        return carry

    lax.fori_loop(1, EX, give, 0)
    back[ex] = back_s[ex]

    def given(k, carry):
        to, source = lax.rem(ex + k, EX), lax.rem(ex + EX - k, EX)
        copy = pltpu.make_async_remote_copy(
            src_ref=back_s.at[to], dst_ref=back.at[source], send_sem=ba_s.at[k - 1],
            recv_sem=ba_r.at[k - 1], device_id=(to, mp), device_id_type=MESH)
        copy.wait_send()
        copy.wait_recv()
        return carry

    lax.fori_loop(1, EX, given, 0)
    gn[mp] = dot(slot_matrix(chosen[...]), back[...].reshape(512, 256), 0, 0).astype(bf16)
    ysends = []
    for i in range(1, 4):
        ysends.append(send(gn.at[mp], gn.at[mp], gy_s.at[i - 1], gy_r.at[i - 1], (ex, lax.rem(mp + i, MP))))
    unit, inverse = norm_parts(resid[...])
    for i in range(1, 4):
        ym = lax.rem(mp + 4 - i, MP)
        pltpu.make_async_remote_copy(
            src_ref=gn.at[mp], dst_ref=gn.at[ym], send_sem=gy_s.at[i - 1], recv_sem=gy_r.at[i - 1],
            device_id=(ex, ym), device_id_type=MESH).wait_recv()
    grad = jnp.concatenate([gn[q] for q in range(4)], axis=1).astype(f32)
    grad_in, ggrad = norm_back(grad, gain[...], unit, inverse)
    ggrad_out[...] = ggrad
    gres = cot[...].astype(f32) + grad_in
    gres_out[...] = gres
    low = gres.astype(bf16)
    dot_out[...] = dot(wfull[mp], low, 1, 1).astype(bf16).reshape(4, 64, 256)
    wgrad_out[...] = dot(att[mp].reshape(256, 256), low).astype(bf16)
    for copy in sends + ysends:
        copy.wait_send()


def middle(att, wfull, tokens, cot, gain, chosen, cot_rows, win, wex):
    rows = ((2, 256, 1024), bf16)
    outs = [
        rows, rows, rows, rows, ((32, 16, 1024), bf16), ((256, 256), f32), ((256, 1024), f32),
        ((4, 64, 256), bf16), ((256, 1024), bf16), ((1, 1024), f32),
    ]
    slots = pltpu.VMEM((32, 16, 1024), bf16)
    return pl.pallas_call(
        middle_kernel,
        out_shape=[jax.ShapeDtypeStruct(s, t) for s, t in outs],
        in_specs=[VM, VM, VM, VM, VM, VM, ANY, ANY, ANY],
        out_specs=[VM] * 10,
        scratch_shapes=[
            pltpu.VMEM((2, 1024, 1024), bf16), pltpu.VMEM((2, 1024, 1024), bf16), slots, slots, slots,
            pltpu.VMEM((2, 256, 1024), f32), pltpu.VMEM((2, 4, 256, 256), bf16),
            pltpu.VMEM((2, 3, 256, 256), bf16), pltpu.VMEM((32, 16, 256), bf16), pltpu.VMEM((32, 16, 256), bf16),
            pltpu.VMEM((4, 256, 256), bf16), pltpu.VMEM((256, 1024), f32),
            DMA, DMA((2,)), DMA((31,)), DMA((31,)), DMA((6,)), DMA((6,)), DMA((31,)), DMA((31,)), DMA((3,)), DMA((3,)),
        ],
        name="middle",
        compiler_params=pltpu.CompilerParams(
            collective_id=1, has_side_effects=True, vmem_limit_bytes=56 << 20),
    )(att, wfull, tokens, cot, gain, chosen, cot_rows, win, wex)
def last_kernel(
    lengths, dot_in, kvt, q_in, ot, lse, normed, wqkv_hbm, tokens, gain, gres, branch, rescol, chosen, ggrad,
    out, igrad, gains_out, wgrad_out,
    wqkv, dob, nall, brs, bs, bret, qaug, dopad, qd, delta, kaug, kvn, kt, dkv, dq,
    sb, sr, xs, xr, zs, zr, wp, wr, pieces, gnp, ry, small, smally, smalle,
    wsem, dz_s, dz_r, na_s, na_r, br_s, br_r, sb_s, sb_r, xs_s, xs_r, ba_s, ba_r, zq_s, zq_r,
    wp_s, wp_r, ag_s, ag_r, fw_s, fw_r, ry_s, ry_r, ay_s, ay_r, gy_s, gy_r, ge_s, ge_r,
):
    ex, mp, z, x, c = place()
    d = 1 - 2 * c
    j = x * 2 + c
    sib = (ex + d, mp)
    bar = greet(ex, mp)
    wcopy = pltpu.make_async_copy(wqkv_hbm, wqkv, wsem)
    wcopy.start()

    def zpeer(i):
        zp = lax.rem(z + i, 4)
        return zp, (zp * 8 + j, mp)

    def ypeer(i):
        ym = lax.rem(mp + i, MP)
        return ym, (ex, ym)

    greeted(bar)
    waits = []
    for i in range(1, 4):
        zp, to = zpeer(i)
        waits.append(send(dot_in.at[zp], dob.at[z], dz_s.at[i - 1], dz_r.at[i - 1], to))
    late = []
    for i in range(1, 4):
        ym, to = ypeer(i)
        late.append(send(
            branch.at[:, :, pl.ds(pl.multiple_of(256 * ym, 256), 256)], brs.at[i - 1],
            br_s.at[i - 1], br_r.at[i - 1], to))
    nsends = []
    for i in range(1, 4):
        zp, to = zpeer(i)
        nsends.append(send(normed, nall.at[z], na_s.at[i - 1], na_r.at[i - 1], to))
    dob[z] = dot_in[z]
    nall[z] = normed[...]
    ends = doc_ends(lengths)
    feature = lax.broadcasted_iota(jnp.int32, (64, 256), 0)
    zero = jnp.zeros((64, 256), bf16)

    def zcame(copy, dst, ssem, rsem, i):
        zp, to = zpeer(4 - i)
        pltpu.make_async_remote_copy(
            src_ref=copy, dst_ref=dst.at[zp], send_sem=ssem.at[i - 1], recv_sem=rsem.at[i - 1],
            device_id=to, device_id_type=MESH).wait_recv()

    for i in range(1, 4):
        zcame(dot_in.at[0], dob, dz_s, dz_r, i)
    for b in range(4):
        docs = doc_row(ends, (b * 8 + j) * 256, 256)
        mask = jnp.where(feature == docs, 0.0, negative_fill).astype(bf16)
        qaug[b, 0:64] = q_in[b]
        qaug[b, 64:128] = mask
        dopad[b, 0:64] = zero
        dopad[b, 64:128] = dob[b]
        qd[b, 0:256] = transposed(jnp.concatenate([q_in[b], zero], axis=0))
        qd[b, 256:512] = transposed(jnp.concatenate([zero, dob[b]], axis=0))
        delta[b] = jnp.sum(dob[b].astype(f32) * ot[b], axis=0, keepdims=True)
        dq[b] = jnp.zeros((64, 256), f32)

    def load_chunk(slot, jp):
        for b in range(4):
            docs = doc_row(ends, (b * 8 + jp) * 256, 256)
            hot = (feature == docs).astype(f32).astype(bf16)
            block = kvt[slot, b]
            kaug[256 * b:256 * b + 256, :] = transposed(jnp.concatenate([block[0:64], hot], axis=0))
            kvn[256 * b:256 * b + 256, :] = transposed(block)
            kt[:, 256 * b:256 * b + 256] = block[0:64]

    def update(b, n, causal):
        s = dot(kaug[0:n, :], qaug[b])
        if causal:
            rows = lax.broadcasted_iota(jnp.int32, (n, 256), 0)
            cols = lax.broadcasted_iota(jnp.int32, (n, 256), 1)
            s = jnp.where(rows - 256 * b <= cols, s, negative_fill)
        p = jnp.exp(s - lse[b])
        dp = dot(kvn[0:n, :], dopad[b])
        ds = (p * (dp - delta[b])).astype(bf16)
        added = dot(ds, qd[b, 0:256]) + dot(p.astype(bf16), qd[b, 256:512])
        if b == 3:
            dkv[0:n] = added
        else:
            dkv[0:n] = dkv[0:n] + added
        dq[b] = dq[b] + dot(kt[:, 0:n], ds)

    def sib_came(p):
        pltpu.make_async_remote_copy(
            src_ref=sb.at[p], dst_ref=sr.at[p], send_sem=sb_s.at[p], recv_sem=sb_r.at[p],
            device_id=sib, device_id_type=MESH).wait_recv()

    def chunk(i, carry):
        p = i // 2
        w = p + (p // 2) * (1 - 2 * (p % 2))
        g = (2 + d * w + 4) % 4
        t = 2 * g + 1 - i % 2
        xp = (x - d * g + 8) % 4
        jp = xp * 2 + (c + t) % 2
        load_chunk(t, jp)

        @pl.when(jp < j)
        def _():
            for b in range(3, -1, -1):
                update(b, 256 * b + 256, False)

        @pl.when(jp > j)
        def _():
            dkv[768:1024] = jnp.zeros((256, 128), f32)
            for b in range(3, 0, -1):
                update(b, 256 * b, False)

        @pl.when(i % 2 == 0)
        def _():
            sb[p] = dkv[...].astype(bf16)
            send(sb.at[p], sr.at[p], sb_s.at[p], sb_r.at[p], sib)

        @pl.when(i % 2 == 1)
        def _():
            sib_came(p)
            xs[p] = (dkv[...] + sr[p].astype(f32)).astype(bf16)
            send(xs.at[p], xr.at[p], xs_s.at[p], xs_r.at[p], (z * 8 + xp * 2 + c, mp))

        @pl.when(i == 4)
        def _():
            total = branch[:, :, pl.ds(pl.multiple_of(256 * mp, 256), 256)].astype(f32)
            for k in range(3):
                late[k].wait_recv()
                total = total + brs[k].astype(f32)
            bs[...] = total.astype(bf16)

            def give(k, carry):
                to = lax.rem(ex + k, EX)
                send(bs.at[to], bret.at[ex], ba_s.at[k - 1], ba_r.at[k - 1], (to, mp))
                return carry

            lax.fori_loop(1, EX, give, 0)
            bret[ex] = bs[ex]

        return carry

    lax.fori_loop(0, 7, chunk, 0)
    load_chunk(0, j)
    for b in range(3, -1, -1):
        update(b, 256 * b + 256, True)
    sib_came(3)
    total = dkv[...] + sr[3].astype(f32)
    for p in range(3):
        pltpu.make_async_remote_copy(
            src_ref=xs.at[p], dst_ref=xr.at[p], send_sem=xs_s.at[p], recv_sem=xs_r.at[p],
            device_id=sib, device_id_type=MESH).wait_recv()
        total = total + xr[p].astype(f32)
    low = total.astype(bf16)
    for b in range(4):
        zs[b, 0:64] = (dq[b] * HEAD_DIM ** (-0.5)).astype(bf16)
        zs[b, 64:192] = transposed(low[256 * b:256 * b + 256])
    for i in range(1, 4):
        zp, to = zpeer(i)
        waits.append(send(zs.at[zp], zr.at[z], zq_s.at[i - 1], zq_r.at[i - 1], to))
    zr[z] = zs[z]
    for i in range(1, 4):
        zcame(normed, nall, na_s, na_r, i)
    wt = dot(zs[0], nall[0])
    for b in range(1, 4):
        wt = wt + dot(zs[b], nall[b])
    wt = wt.astype(bf16)
    for k in range(8):
        wp[k] = wt[:, 128 * k:128 * k + 128]
    for i in range(1, 8):
        jt = lax.rem(j + i, 8)
        waits.append(send(wp.at[jt], wr.at[i - 1], wp_s.at[i - 1], wp_r.at[i - 1], (z * 8 + jt, mp)))
    for i in range(1, 4):
        zcame(zs.at[0], zr, zq_s, zq_r, i)
    wcopy.wait()
    part = None
    for k in range(3):
        heads = transposed(jnp.concatenate([zr[h, 64 * k:64 * k + 64] for h in range(4)], axis=0))
        term = dot(heads, wqkv[k], 1, 1)
        part = term if part is None else part + term
    gnp[...] = part.astype(bf16).reshape(4, 64, 1024)
    rsends = []
    for i in range(1, 4):
        ym, to = ypeer(i)
        rsends.append(send(gnp.at[ym], ry.at[i - 1], ry_s.at[i - 1], ry_r.at[i - 1], to))
    summed = wp[j].astype(f32)
    for i in range(7):
        waits[6 + i].wait_recv()
        summed = summed + wr[i].astype(f32)
    pieces[ex] = summed.astype(bf16)
    chip = ex // 2

    def spread(k, carry):
        to = lax.rem(chip + k, 16) * 2 + c
        send(pieces.at[ex], pieces.at[ex], ag_s.at[k - 1], ag_r.at[k - 1], (to, mp))
        return carry

    lax.fori_loop(1, 16, spread, 0)
    send(pieces.at[ex], pieces.at[ex], fw_s.at[0], fw_r.at[0], sib)
    grad = gnp[mp].astype(f32)
    for i in range(3):
        rsends[i].wait_recv()
        grad = grad + ry[i].astype(f32)
    mine = pl.ds(pl.multiple_of(64 * mp, 64), 64)
    unit, inverse = norm_parts(tokens[mine, :].astype(f32))
    grad_in, one_gain = norm_back(grad, gain[...], unit, inverse)
    igrad[mine, :] = (gres[mine, :] + grad_in).astype(bf16)
    small[...] = one_gain
    asends = []
    for i in range(1, 4):
        ym, to = ypeer(i)
        asends.append(send(small, smally.at[i - 1], gy_s.at[i - 1], gy_r.at[i - 1], to))
        asends.append(send(igrad.at[mine, :], igrad.at[mine, :], ay_s.at[i - 1], ay_r.at[i - 1], to))
    one_gain = small[...]
    for i in range(3):
        asends[2 * i].wait_recv()
        one_gain = one_gain + smally[i]
    smalle[ex, 0:1] = one_gain
    smalle[ex, 1:2] = ggrad[...]

    def gain_send(k, carry):
        to = lax.rem(ex + k, EX)
        send(smalle.at[ex], smalle.at[ex], ge_s.at[k - 1], ge_r.at[k - 1], (to, mp))
        return carry

    lax.fori_loop(1, EX, gain_send, 0)

    def given(k, carry):
        to, source = lax.rem(ex + k, EX), lax.rem(ex + EX - k, EX)
        copy = pltpu.make_async_remote_copy(
            src_ref=bs.at[to], dst_ref=bret.at[source], send_sem=ba_s.at[k - 1], recv_sem=ba_r.at[k - 1],
            device_id=(to, mp), device_id_type=MESH)
        copy.wait_send()
        copy.wait_recv()
        return carry

    lax.fori_loop(1, EX, given, 0)
    rows = dot(slot_matrix(chosen[...]), bret[...].reshape(512, 256), 0, 0)
    out[...] = (rescol[...] + rows).astype(bf16)

    def pass_on(k, carry):
        to = lax.rem(chip + k, 16) * 2 + c
        source = lax.rem(chip + 16 - k, 16) * 2 + c
        copy = pltpu.make_async_remote_copy(
            src_ref=pieces.at[ex], dst_ref=pieces.at[source], send_sem=ag_s.at[k - 1], recv_sem=ag_r.at[k - 1],
            device_id=(to, mp), device_id_type=MESH)
        copy.wait_send()
        copy.wait_recv()
        send(pieces.at[source], pieces.at[source], fw_s.at[k], fw_r.at[k], sib)
        return carry

    lax.fori_loop(1, 16, pass_on, 0)

    def passed(k, carry):
        source = lax.rem(chip + 16 - k, 16) * 2 + 1 - c
        copy = pltpu.make_async_remote_copy(
            src_ref=pieces.at[ex], dst_ref=pieces.at[source], send_sem=fw_s.at[k], recv_sem=fw_r.at[k],
            device_id=sib, device_id_type=MESH)
        copy.wait_send()
        copy.wait_recv()
        return carry

    lax.fori_loop(0, 16, passed, 0)
    for k in range(3):
        for r in range(8):
            block = jnp.concatenate([pieces[8 * h + r, 64 * k:64 * k + 64] for h in range(4)], axis=0)
            wgrad_out[k, 128 * r:128 * r + 128] = transposed(block)

    def gain_wait(k, carry):
        to, source = lax.rem(ex + k, EX), lax.rem(ex + EX - k, EX)
        copy = pltpu.make_async_remote_copy(
            src_ref=smalle.at[ex], dst_ref=smalle.at[source], send_sem=ge_s.at[k - 1], recv_sem=ge_r.at[k - 1],
            device_id=(to, mp), device_id_type=MESH)
        copy.wait_send()
        copy.wait_recv()
        return carry

    lax.fori_loop(1, EX, gain_wait, 0)
    gains_out[...] = jnp.sum(smalle[...], axis=0)
    for i in range(1, 4):
        ym, to = ypeer(4 - i)
        other = pl.ds(pl.multiple_of(64 * ym, 64), 64)
        pltpu.make_async_remote_copy(
            src_ref=igrad.at[mine, :], dst_ref=igrad.at[other, :], send_sem=ay_s.at[i - 1], recv_sem=ay_r.at[i - 1],
            device_id=to, device_id_type=MESH).wait_recv()
    for copy in waits + late + nsends + rsends + asends:
        copy.wait_send()
    for p in range(4):
        pltpu.make_async_remote_copy(
            src_ref=sb.at[p], dst_ref=sr.at[p], send_sem=sb_s.at[p], recv_sem=sb_r.at[p],
            device_id=sib, device_id_type=MESH).wait_send()
    for p in range(3):
        pltpu.make_async_remote_copy(
            src_ref=xs.at[p], dst_ref=xr.at[p], send_sem=xs_s.at[p], recv_sem=xs_r.at[p],
            device_id=sib, device_id_type=MESH).wait_send()


def last(lengths, dot_in, kvt, q_in, ot, lse, normed, wqkv, tokens, gain, gres, branch, rescol, chosen, ggrad):
    outs = [((256, 256), bf16), ((256, 1024), bf16), ((2, 1024), f32), ((3, 1024, 256), bf16)]

    def vmem(kind, *shape):
        return pltpu.VMEM(shape, kind)

    scratch = [
        vmem(bf16, 3, 1024, 256), vmem(bf16, 4, 64, 256), vmem(bf16, 4, 256, 1024), vmem(bf16, 3, 32, 16, 256),
        vmem(bf16, 32, 16, 256), vmem(bf16, 32, 16, 256), vmem(bf16, 4, 128, 256), vmem(bf16, 4, 128, 256),
        vmem(bf16, 4, 512, 128), vmem(f32, 4, 1, 256), vmem(bf16, 1024, 128), vmem(bf16, 1024, 128),
        vmem(bf16, 64, 1024), vmem(f32, 1024, 128), vmem(f32, 4, 64, 256),
        vmem(bf16, 4, 1024, 128), vmem(bf16, 4, 1024, 128), vmem(bf16, 3, 1024, 128), vmem(bf16, 3, 1024, 128),
        vmem(bf16, 4, 192, 256), vmem(bf16, 4, 192, 256), vmem(bf16, 8, 192, 128), vmem(bf16, 7, 192, 128),
        vmem(bf16, 32, 192, 128), vmem(bf16, 4, 64, 1024), vmem(bf16, 3, 64, 1024),
        vmem(f32, 1, 1024), vmem(f32, 3, 1, 1024), vmem(f32, 32, 2, 1024), DMA,
    ]
    for n in (3, 3, 3, 4, 3, 31, 3, 7, 15, 16, 3, 3, 3, 31):
        scratch += [DMA((n,)), DMA((n,))]
    return pl.pallas_call(
        last_kernel,
        out_shape=[jax.ShapeDtypeStruct(s, t) for s, t in outs],
        in_specs=[SM, VM, VM, VM, VM, VM, VM, ANY] + [VM] * 7,
        out_specs=[VM] * 4,
        scratch_shapes=scratch,
        name="last",
        compiler_params=pltpu.CompilerParams(
            collective_id=2, has_side_effects=True, vmem_limit_bytes=56 << 20),
    )(lengths, dot_in, kvt, q_in, ot, lse, normed, wqkv, tokens, gain, gres, branch, rescol, chosen, ggrad)
def expert_grads_kernel(x, gpre, hidden, cots, in_grad, out_grad):
    in_grad[0] = dot(x[0], gpre[0], 0, 0)
    out_grad[0] = dot(hidden[0], cots[0], 0, 0)


def expert_grads(x, gpre, hidden, cots):
    shape = jax.ShapeDtypeStruct((2, 1024, 1024), f32)
    width = 256
    tall = pl.BlockSpec((1, 256, width), lambda e, i: (e, 0, i))
    whole = pl.BlockSpec((1, 256, 1024), lambda e, i: (e, 0, 0))
    made = pl.BlockSpec((1, width, 1024), lambda e, i: (e, i, 0))
    return pl.pallas_call(
        expert_grads_kernel,
        grid=(2, 1024 // width),
        out_shape=[shape, shape],
        in_specs=[tall, whole, tall, whole],
        out_specs=[made, made],
        name="expert_grads",
        compiler_params=pltpu.CompilerParams(vmem_limit_bytes=48 << 20),
        cost_estimate=pl.CostEstimate(flops=2 * 2 * 2 * 256 * 1024 * 1024, bytes_accessed=20 << 20, transcendentals=0),
    )(x, gpre, hidden, cots)


def on_device(
    tokens, hash_ids, lengths, norm1_gain, qkv_weight, out_weight, norm2_gain, expert_in, expert_out, cotangent,
):
    chosen = hash_ids.reshape(1, 256)
    gain1, gain2 = norm1_gain.reshape(1, 1024), norm2_gain.reshape(1, 1024)
    wqkv = jnp.transpose(qkv_weight, (1, 0, 2))
    normed, kvt, q, ot, lse, att, cot_rows, wfull = front(
        lengths, tokens, gain1, chosen, wqkv, out_weight, cotangent)
    x, cots, hidden, gpre, branch, rescol, gres, dheads, wout_part, ggrad = middle(
        att, wfull, tokens, cotangent, gain2, chosen, cot_rows, expert_in, expert_out)
    wout_grad = lax.psum(wout_part, "ex").astype(f32)
    in_grad, out_grad = expert_grads(x, gpre, hidden, cots)
    out, igrad, gains, wgrad = last(
        lengths, dheads, kvt, q, ot, lse, normed, wqkv, tokens, gain1, gres, branch, rescol, chosen, ggrad)
    qkv_grad = jnp.transpose(wgrad.astype(f32), (1, 0, 2))
    return out, igrad, gains[0], qkv_grad, wout_grad, gains[1], in_grad, out_grad


def solution(mesh):
    placed = (
        P("ex", None), P("ex", None), P(), P(), P(None, None, "mp"), P("mp", None), P(),
        P("ex", None, "mp"), P("ex", "mp", None), P("ex", None),
    )
    return jax.shard_map(
        on_device,
        mesh=mesh,
        in_specs=placed,
        out_specs=(
            P("ex", "mp"), P("ex", None), P(), P(None, None, "mp"), P("mp", None), P(),
            P("ex", None, "mp"), P("ex", "mp", None),
        ),
        check_vma=False,
    )
```

time: 853 us -> 254 us (0.30)
  waiting for transfers between devices: 598 us -> 41.1 us
  Pallas kernels: 0 us -> 191 us
  blocking collectives: 62.8 us -> 0 us
  local copies, waits for them, and re-layouts: 51.7 us -> 2.08 us
  matrix products: 48.5 us -> 0 us
  starting transfers between devices: 31.5 us -> 0.04 us
  loops' own time: 22.7 us -> 0 us
  other arithmetic: 16 us -> 5.61 us
    psum x4 -> x1, waiting for transfers between devices: 272 us -> 41 us  [on_device(): wout_grad = lax.psum(wout_part, 'ex').astype(f32)]
    reduce_scatter x1 -> x0, waiting for transfers between devices: 226 us -> none  [on_device(): lax.psum_scatter(grad_keys.astype(jnp.bfloat16), 'ex', scatter_dimension=...]
    pallas_call x0 -> x4, Pallas kernels: none -> 191 us  [the longest x1 71.3 us: last(): pl.pallas_call(last_kernel, out_shape=[jax.ShapeDtypeStruct(s, t) for s,...]
    psum x1 -> x0, blocking collectives: 62.8 us -> none  [on_device(): lax.psum(gain_one_grad.astype(jnp.bfloat16), 'ex').astype(jnp.float32)]
    all_gather x1 -> x0, waiting for transfers between devices: 56.3 us -> none  [on_device(): gathered = lax.all_gather(key_value, 'ex', axis=0, tiled=True)]
    dot_general x23 -> x0, matrix products: 48.5 us -> none  [the longest x1 6.73 us: on_device(): jnp.einsum('erf,erd->efd', hidden_low, grad_arrived, preferred_element_ty...]
    all_to_all x4 -> x0, waiting for transfers between devices: 44.2 us -> none  [the longest x1 16.5 us: on_device(): lax.all_to_all(grad_rows.reshape(local_experts, ex_count, capacity, model...]
    all_to_all x4 -> x0, starting transfers between devices: 31.3 us -> none  [the longest x1 9.67 us: on_device(): lax.all_to_all(outgoing.reshape(ex_count, local_experts, capacity, model_...]
  transfers between devices with their start and end apart: 10 -> 1, of which waited for: 9 -> 1; matrix products, arithmetic and copies ran while one was open for 5% -> 2% of each run, Pallas kernels for 0% -> 31%
where the time goes in v1:
time: 254 us
  Pallas kernels  191 us (75%)
  waiting for transfers between devices  41.1 us (16%)
  between operations  14.1 us (6%)
  other arithmetic  5.61 us (2%)
    pallas_call x1, Pallas kernels, last(): pl.pallas_call(last_kernel, out_shape=[jax.ShapeDtypeStruct(s, t) for s,...  71.3 us
    pallas_call x1, Pallas kernels, middle(): pl.pallas_call(middle_kernel, out_shape=[jax.ShapeDtypeStruct(s, t) for s...  60.2 us
    pallas_call x1, Pallas kernels, front(): pl.pallas_call(front_kernel, out_shape=[jax.ShapeDtypeStruct(s, t) for s,...  52.1 us
    psum x1, waiting for transfers between devices, on_device(): wout_grad = lax.psum(wout_part, 'ex').astype(f32)  41 us
    pallas_call x1, Pallas kernels, expert_grads(): pl.pallas_call(expert_grads_kernel, grid=(2, 1024 // width), out_shape=[s...  7.34 us
  transfers between devices with their start and end apart: 1, of which 1 were waited for; matrix products, arithmetic and copies ran while one was open for 2% of the time, Pallas kernels for 31%

profile of v1, /device:TPU:1, one launch (start us, length us, event | category | flops | bytes accessed | tf_op | source)
XLA Modules:
  0.0 253.9 jit_solution(5736726359804590660)
XLA Ops:
  7.2 0.0 all-reduce.2.cloned.1.call-start
  7.2 52.1 %front.1 = (bf16[256,1024]{1,0:T(8,128)(2,1)}, bf16[8,4,128,256]{3,2,1,0:T(8,128)(2,1)}, bf16[4,64,256]{2,1,0:T(8,128)(2,1)}, f32[4,64,256]{2,1,0:T(8,128)}, f32...) custom-call(s32[9]{0:T(128)} %lengths.3, ...), custom_call_target="tpu_custom_call" | custom-call | tf_op jit(solution)/shard_map/front/pallas_call | solution.py:305
  59.3 60.2 %middle.1 = (bf16[2,256,1024]{2,1,0:T(8,128)(2,1)}, bf16[2,256,1024]{2,1,0:T(8,128)(2,1)}, bf16[2,256,1024]{2,1,0:T(8,128)(2,1)}, bf16[2,256,1024]{2,1,0:T(8,128...) custom-call(bf16[4,4,64,256]{3,2,1,0:T(8,128)(2,1)} %get-tuple-eleme, ...), custom_call_target="tpu_custom_call" | custom-call | tf_op jit(solution)/shard_map/middle/pallas_call | solution.py:472
  119.5 0.0 all-reduce.2.cloned.1.call-update
  119.5 71.3 %last.1 = (bf16[256,256]{1,0:T(8,128)(2,1)}, bf16[256,1024]{1,0:T(8,128)(2,1)}, f32[2,1024]{1,0:T(2,128)}, bf16[3,1024,256]{2,1,0:T(8,128)(2,1)}) custom-call(s32[9]{0:T(128)} %lengths.3, bf16[4,64,256]{2,1,0:T(8,128)(2,1)} %get-tuple-element.35.dot_in, bf16[8,4,128,256]{3,2,1,0:T(8,128)(2,1)} %get-tuple-element.36.kvt, ...), custom_call_target="tpu_custom_call" | custom-call | tf_op jit(solution)/shard_map/last/pallas_call | solution.py:805
  190.9 0.0 copy-start
  190.9 0.0 copy-start.1
  190.9 0.0 copy-start.2
  190.9 0.0 copy-start.3
  190.9 3.5 %convert_bitcast_fusion = f32[1024,3,256]{2,0,1:T(8,128)} fusion(bf16[3,1024,256]{2,1,0:T(8,128)(2,1)} %get-tuple-element.48), kind=kLoop, calls=%fused_computation | loop fusion | flops 786432 | bytes 4718592 | tf_op jit(solution)/shard_map/transpose | solution.py:852
  194.4 0.0 copy-done
  194.4 0.0 copy-done.1
  194.4 0.0 copy-done.2
  194.4 0.0 copy-done.3
  194.4 0.0 copy-start.6
  194.5 0.0 copy-start.5
  194.5 0.0 copy-start.4
  194.5 7.3 %expert_grads.1 = (f32[2,1024,1024]{2,1,0:T(8,128)}, f32[2,1024,1024]{2,1,0:T(8,128)}) custom-call(bf16[2,256,1024]{2,1,0:T(8,128)(2,1)S(1)} %copy-done, bf16[2,256,1024]{2,1,0:T(8,128)(2,1)S(1)} %copy-done.3, bf16[2,256,1024]{2,1,0:T(8,128)(2,1)S(1)} %copy-done.2, bf16[2,256,1024]{2,1,0:T(8,128)(2,1)S(1)} %copy-done.1), custom_call_target="tpu_custom_call" | custom-call | flops 2147483648 | bytes 20971520 | tf_op jit(solution)/shard_map/expert_grads/pallas_call | solution.py:826
  201.8 0.0 copy-done.6
  201.8 0.6 fusion
  202.4 41.0 %all-reduce.2.cloned.1.call-done = bf16[256,1024]{1,0:T(8,128)(2,1)} async-done(((bf16[256,1024]{1,0:T(8,128)(2,1)}), bf16[256,1024]{1,0:T(8,128)(2,1)}) %all-reduce.2.cloned.1.call-update) | async-done | bytes 524304 | tf_op jit(solution)/shard_map/psum | solution.py:848
  243.5 2.1 convert_element_type.4
  245.6 0.0 copy-done.5
  245.6 0.7 copy.21
  246.2 0.0 copy-done.4
  246.2 0.8 copy.22
Async XLA Ops:
  7.2 236.3 %all-reduce.2.cloned.1.call-start = ((), (), s32[]{:S(2)}) async-start(), calls=%async_computation | async-start | bytes 1048576 | tf_op jit(solution)/shard_map/psum | solution.py:848
  190.9 3.5 %copy-start = (bf16[2,256,1024]{2,1,0:T(8,128)(2,1)S(1)}, bf16[2,256,1024]{2,1,0:T(8,128)(2,1)}, u32[]{:S(2)}) copy-start(bf16[2,256,1024]{2,1,0:T(8,128)(2,1)} %get-tuple-element.50.x) | copy-start | bytes 3145732
  190.9 3.5 %copy-start.1 = (bf16[2,256,1024]{2,1,0:T(8,128)(2,1)S(1)}, bf16[2,256,1024]{2,1,0:T(8,128)(2,1)}, u32[]{:S(2)}) copy-start(bf16[2,256,1024]{2,1,0:T(8,128)(2,1)} %get-tuple-element.53.cots) | copy-start | bytes 3145732
  190.9 3.5 %copy-start.2 = (bf16[2,256,1024]{2,1,0:T(8,128)(2,1)S(1)}, bf16[2,256,1024]{2,1,0:T(8,128)(2,1)}, u32[]{:S(2)}) copy-start(bf16[2,256,1024]{2,1,0:T(8,128)(2,1)} %get-tuple-element.52.hidden) | copy-start | bytes 3145732
  190.9 3.5 %copy-start.3 = (bf16[2,256,1024]{2,1,0:T(8,128)(2,1)S(1)}, bf16[2,256,1024]{2,1,0:T(8,128)(2,1)}, u32[]{:S(2)}) copy-start(bf16[2,256,1024]{2,1,0:T(8,128)(2,1)} %get-tuple-element.51.gpre) | copy-start | bytes 3145732
  194.4 7.4 %copy-start.6 = (f32[2,1024]{1,0:T(2,128)S(1)}, f32[2,1024]{1,0:T(2,128)}, u32[]{:S(2)}) copy-start(f32[2,1024]{1,0:T(2,128)} %get-tuple-element.47) | copy-start | bytes 24580
  194.5 51.1 %copy-start.5 = (bf16[256,256]{1,0:T(8,128)(2,1)S(1)}, bf16[256,256]{1,0:T(8,128)(2,1)}, u32[]{:S(2)}) copy-start(bf16[256,256]{1,0:T(8,128)(2,1)} %get-tuple-element.66) | copy-start | bytes 393220
  194.5 51.8 %copy-start.4 = (bf16[256,1024]{1,0:T(8,128)(2,1)S(1)}, bf16[256,1024]{1,0:T(8,128)(2,1)}, u32[]{:S(2)}) copy-start(bf16[256,1024]{1,0:T(8,128)(2,1)} %get-tuple-element.67) | copy-start | bytes 1572868
Sparse Core Ops, SparseCore 0:
  119.7 123.7 all-reduce.1

commit v2 on v0

v2 whole, which is shorter than its diff:
```python
import functools

import jax
import jax.numpy as jnp
from jax import lax
from jax.experimental import pallas as pl
from jax.experimental.pallas import tpu as pltpu
from jax.sharding import PartitionSpec as P

HEAD_DIM = 64
epsilon = 1e-05
negative_fill = -1e30
MESH = pl.DeviceIdType.MESH
bf16, f32 = jnp.bfloat16, jnp.float32
EX, MP = 32, 4
VMEM_BYTES = 60 << 20


def dot(a, b, ca=1, cb=0):
    return lax.dot_general(a, b, (((ca,), (cb,)), ((), ())), preferred_element_type=f32)


def place():
    ex, mp = lax.axis_index("ex"), lax.axis_index("mp")
    z, x, c = ex // 8, (ex // 2) % 4, ex % 2
    return ex, mp, z, x, c


def send(src, dst, ssem, rsem, device):
    copy = pltpu.make_async_remote_copy(
        src_ref=src, dst_ref=dst, send_sem=ssem, recv_sem=rsem, device_id=device, device_id_type=MESH
    )
    copy.start()
    return copy


def greet(ex, mp):
    bar = pltpu.get_barrier_semaphore()

    def one(d, carry):
        pl.semaphore_signal(bar, inc=1, device_id=(lax.rem(ex + d, EX), mp), device_id_type=MESH)
        return carry

    lax.fori_loop(1, EX, one, 0)
    for d in range(1, MP):
        pl.semaphore_signal(bar, inc=1, device_id=(ex, lax.rem(mp + d, MP)), device_id_type=MESH)
    return bar


def greeted(bar):
    pl.semaphore_wait(bar, EX - 1 + MP - 1)


def slot_matrix(chosen_row):
    tok = chosen_row.shape[1]
    experts = lax.broadcasted_iota(jnp.int32, (64, tok), 0)
    hot = (experts == chosen_row).astype(f32)
    rows = lax.broadcasted_iota(jnp.int32, (tok, tok), 0)
    cols = lax.broadcasted_iota(jnp.int32, (tok, tok), 1)
    before = (rows < cols).astype(bf16)
    earlier = dot(hot.astype(bf16), before)
    rank = jnp.sum(earlier * hot, axis=0, keepdims=True)
    target = chosen_row * 8 + rank.astype(jnp.int32)
    slots = lax.broadcasted_iota(jnp.int32, (512, tok), 0)
    return (slots == target).astype(f32).astype(bf16)


def doc_row(ends, first, count):
    pos = first + lax.broadcasted_iota(jnp.int32, (1, count), 1)
    row = jnp.zeros((1, count), jnp.int32)
    for end in ends:
        row = row + (pos >= end).astype(jnp.int32)
    return row


def doc_ends(lengths_ref):
    ends, total = [], 0
    for i in range(9):
        total = total + lengths_ref[i]
        ends.append(total)
    return ends


def norm_parts(v):
    mean = jnp.mean(v, axis=-1, keepdims=True)
    centred = v - mean
    inverse = lax.rsqrt(jnp.mean(centred * centred, axis=-1, keepdims=True) + epsilon)
    return centred * inverse, inverse


def transposed(v):
    return v.T


def norm_back(grad_out, gain_row, unit, inverse):
    scaled = grad_out * gain_row
    centred = scaled - jnp.mean(scaled, axis=-1, keepdims=True)
    grad_in = inverse * (centred - unit * jnp.mean(scaled * unit, axis=-1, keepdims=True))
    return grad_in, jnp.sum(grad_out * unit, axis=0, keepdims=True)


def gelu_parts(pre):
    k = 0.7978845608028654
    square = pre * pre
    t = jnp.tanh(k * pre * (1.0 + 0.044715 * square))
    half = 0.5 * (1.0 + t)
    slope = half + 0.5 * pre * (1.0 - t * t) * (k * (1.0 + 3 * 0.044715 * square))
    return pre * half, slope


def one_expert(rows, le):
    wide = rows.astype(f32)
    return wide[:, 8 * le:8 * le + 8].reshape(256, rows.shape[2]).astype(bf16)


def both_experts(first, second):
    width = first.shape[1]
    return jnp.concatenate([first.reshape(32, 8, width), second.reshape(32, 8, width)], axis=1).astype(bf16)


VM = pl.BlockSpec(memory_space=pltpu.VMEM)
SM = pl.BlockSpec(memory_space=pltpu.SMEM)
ANY = pl.BlockSpec(memory_space=pl.ANY)
DMA = pltpu.SemaphoreType.DMA
ROWS = (2, 256, 1024)

ARGS = ["lengths", "tokens", "gain1", "gain2", "chosen", "wqkv_hbm", "wout_hbm", "cot_hbm", "win_hbm", "wex_hbm"]
OUTS = {
    "x_hbm": (ROWS, bf16), "c_hbm": (ROWS, bf16), "hid_hbm": (ROWS, bf16), "gpre_hbm": (ROWS, bf16),
    "out": ((256, 256), bf16), "igrad": ((256, 1024), bf16), "gains": ((2, 1024), f32),
    "qkv_out": ((3, 1024, 256), bf16), "wout_out": ((256, 1024), bf16),
}
BUFFERS = {
    "wqkv": ((3, 1024, 256), bf16), "wout": ((256, 1024), bf16), "cot": ((256, 1024), bf16),
    "win": ((2, 1024, 1024), bf16), "wex": ((2, 1024, 1024), bf16), "normed": ((256, 1024), bf16),
    "nall": ((4, 256, 1024), bf16), "wfull": ((4, 256, 1024), bf16),
    "q_s": ((4, 64, 256), bf16), "kv_s": ((4, 128, 256), bf16), "q": ((4, 64, 256), bf16),
    "kvt": ((8, 4, 128, 256), bf16), "qaug": ((4, 128, 256), bf16), "kaug": ((1024, 128), bf16),
    "vt1": ((80, 1024), bf16), "acc": ((4, 80, 256), f32), "peak": ((4, 1, 256), f32),
    "ot": ((4, 64, 256), f32), "lse": ((4, 1, 256), f32), "o_s": ((4, 64, 256), bf16),
    "att": ((4, 4, 64, 256), bf16), "cotq_s": ((32, 16, 256), bf16), "cotq": ((4, 32, 16, 256), bf16),
    "outgoing": ((32, 16, 1024), bf16), "arrived": ((32, 16, 1024), bf16),
    "xrows": (ROWS, bf16), "crows": (ROWS, bf16), "hid": (ROWS, bf16), "gpre": (ROWS, bf16), "gh": (ROWS, f32),
    "part": ((2, 4, 256, 256), bf16), "rs": ((2, 3, 256, 256), bf16), "back_s": ((32, 16, 256), bf16),
    "back": ((32, 16, 256), bf16), "gn": ((4, 256, 256), bf16), "resid": ((256, 1024), f32),
    "rescol": ((256, 256), f32), "gres": ((256, 1024), f32), "branch": ((32, 16, 1024), bf16),
    "wgp": ((2, 16, 16, 512), bf16), "wgs": ((16, 16, 512), bf16), "wgq": ((16, 16, 512), bf16),
    "wgr": ((15, 16, 512), bf16), "wgf": ((32, 16, 512), bf16),
    "dheads": ((4, 64, 256), bf16), "dob": ((4, 64, 256), bf16), "brs": ((3, 32, 16, 256), bf16),
    "bs": ((32, 16, 256), bf16), "bret": ((32, 16, 256), bf16), "dopad": ((4, 128, 256), bf16),
    "qd": ((4, 512, 128), bf16), "delta": ((4, 1, 256), f32), "kvn": ((1024, 128), bf16),
    "kt": ((64, 1024), bf16), "dkv": ((1024, 128), f32), "dq": ((4, 64, 256), f32),
    "sb": ((4, 1024, 128), bf16), "sr": ((4, 1024, 128), bf16), "xs": ((3, 1024, 128), bf16),
    "xr": ((3, 1024, 128), bf16), "zs": ((4, 192, 256), bf16), "zr": ((4, 192, 256), bf16),
    "wp": ((8, 192, 128), bf16), "wr": ((7, 192, 128), bf16), "pieces": ((32, 192, 128), bf16),
    "gnp": ((4, 64, 1024), bf16), "ry": ((3, 64, 1024), bf16), "small": ((1, 1024), f32),
    "smally": ((3, 1, 1024), f32), "smalle": ((32, 2, 1024), f32), "ggrad": ((1, 1024), f32),
}
LOCAL = {"load": (5,), "store": (4,)}
SENT = {
    "az": (6,), "ag": (28,), "wf": (3,), "wd": (3,), "co": (31,), "cy": (3,), "na": (3,), "oz": (3,), "oy": (3,),
    "di": (31,), "rs": (6,), "ba": (31,), "gy": (3,), "dz": (3,), "br": (3,), "bb": (31,), "sb": (4,), "xs": (3,),
    "wg": (1,), "wq": (15,), "wa": (15,), "wb": (16,), "zq": (3,), "wp": (7,), "pa": (15,), "pb": (16,),
    "ry": (3,), "ay": (3,), "sy": (3,), "se": (31,),
}
TAKEN = dict(SENT, ag=(32,))


class Refs:
    pass


def layer_kernel(*refs):
    r, ls, ss, rr = Refs(), Refs(), Refs(), Refs()
    names = [(r, k) for k in ARGS + list(OUTS) + list(BUFFERS)] + [(ls, k) for k in LOCAL]
    names += [(ss, k) for k in SENT] + [(rr, k) for k in TAKEN]
    for (group, name), ref in zip(names, refs, strict=True):
        setattr(group, name, ref)
    ex, mp, z, x, c = place()
    d = 1 - 2 * c
    j = x * 2 + c
    chip = ex // 2
    sib = (ex + d, mp)
    ahead = (z * 8 + lax.rem(x + d + 4, 4) * 2 + c, mp)
    behind = (z * 8 + lax.rem(x - d + 4, 4) * 2 + c, mp)
    pending = []

    def zpeer(i):
        zp = lax.rem(z + i, 4)
        return zp, (zp * 8 + j, mp)

    def ypeer(i):
        ym = lax.rem(mp + i, MP)
        return ym, (ex, ym)

    def remote(src, dst, ssem, rsem, device):
        return pltpu.make_async_remote_copy(
            src_ref=src, dst_ref=dst, send_sem=ssem, recv_sem=rsem, device_id=device, device_id_type=MESH)

    def push(src, dst, ssem, rsem, device):
        remote(src, dst, ssem, rsem, device).start()
        pending.append((src, ssem))

    def arrive(dst, rsem):
        remote(dst, dst, rsem, rsem, sib).wait_recv()

    def left(src, ssem):
        remote(src, src, ssem, ssem, sib).wait_send()

    def to_all(src_of, dst, name):
        def one(k, carry):
            to = lax.rem(ex + k, EX)
            remote(src_of(to), dst, getattr(ss, name).at[k - 1], getattr(rr, name).at[k - 1], (to, mp)).start()
            return carry

        lax.fori_loop(1, EX, one, 0)

    def from_all(src, dst_of, name):
        def one(k, carry):
            left(src, getattr(ss, name).at[k - 1])
            arrive(dst_of(lax.rem(ex + EX - k, EX)), getattr(rr, name).at[k - 1])
            return carry

        lax.fori_loop(1, EX, one, 0)

    def spread(buf, far, near):
        def one(k, carry):
            to = lax.rem(chip + k, 16) * 2 + c
            remote(buf.at[ex], buf.at[ex], getattr(ss, far).at[k - 1], getattr(rr, far).at[k - 1], (to, mp)).start()
            return carry

        lax.fori_loop(1, 16, one, 0)
        remote(buf.at[ex], buf.at[ex], getattr(ss, near).at[0], getattr(rr, near).at[0], sib).start()

    def pass_on(buf, far, near):
        def one(k, carry):
            source = lax.rem(chip + 16 - k, 16) * 2 + c
            left(buf.at[ex], getattr(ss, far).at[k - 1])
            arrive(buf.at[source], getattr(rr, far).at[k - 1])
            remote(buf.at[source], buf.at[source], getattr(ss, near).at[k], getattr(rr, near).at[k], sib).start()
            return carry

        lax.fori_loop(1, 16, one, 0)

    def passed(buf, near):
        def one(k, carry):
            source = lax.rem(chip + 16 - k, 16) * 2 + 1 - c
            left(buf.at[ex], getattr(ss, near).at[k])
            arrive(buf.at[source], getattr(rr, near).at[k])
            return carry

        lax.fori_loop(0, 16, one, 0)

    bar = greet(ex, mp)
    loads = [
        pltpu.make_async_copy(src, dst, ls.load.at[i])
        for i, (src, dst) in enumerate([
            (r.wqkv_hbm, r.wqkv), (r.wout_hbm, r.wout), (r.cot_hbm, r.cot), (r.wex_hbm, r.wex), (r.win_hbm, r.win)])
    ]
    for copy in loads:
        copy.start()
    unit, _ = norm_parts(r.tokens[...].astype(f32))
    normed = (unit * r.gain1[...]).astype(bf16)
    r.normed[...] = normed
    loads[0].wait()
    kt = transposed(dot(normed, r.wqkv[1]).astype(bf16))
    vt = transposed(dot(normed, r.wqkv[2]).astype(bf16))
    qt = transposed((dot(normed, r.wqkv[0]).astype(bf16) * HEAD_DIM ** (-0.5)).astype(bf16))
    for h in range(4):
        r.q_s[h] = qt[64 * h:64 * h + 64]
        r.kv_s[h, 0:64] = kt[64 * h:64 * h + 64]
        r.kv_s[h, 64:128] = vt[64 * h:64 * h + 64]
    greeted(bar)
    for i in (1, 3, 2):
        zp, to = zpeer(i)
        push(r.kv_s.at[zp], r.kvt.at[0, z], ss.az.at[i - 1], rr.az.at[i - 1], to)
    r.kvt[0, z] = r.kv_s[z]

    def own_piece(k):
        zq = lax.rem(z + 4 - k, 4)
        remote(r.kvt.at[0, zq], r.kvt.at[2, zq], ss.ag.at[4 * 1 + k], rr.ag.at[4 * 2 + k], ahead).start()
        remote(r.kvt.at[0, zq], r.kvt.at[3, zq], ss.ag.at[4 * 2 + k], rr.ag.at[4 * 3 + k], behind).start()
        remote(r.kvt.at[0, zq], r.kvt.at[1, zq], ss.ag.at[k], rr.ag.at[4 * 1 + k], sib).start()

    def came(slot, k):
        arrive(r.kvt.at[slot, lax.rem(z + 4 - k, 4)], rr.ag.at[4 * slot + k])

    def from_sides(k):
        zq = lax.rem(z + 4 - k, 4)
        came(2, k)
        remote(r.kvt.at[2, zq], r.kvt.at[6, zq], ss.ag.at[4 * 3 + k], rr.ag.at[4 * 6 + k], ahead).start()
        remote(r.kvt.at[2, zq], r.kvt.at[5, zq], ss.ag.at[4 * 4 + k], rr.ag.at[4 * 5 + k], sib).start()
        came(3, k)
        remote(r.kvt.at[3, zq], r.kvt.at[4, zq], ss.ag.at[4 * 5 + k], rr.ag.at[4 * 4 + k], sib).start()

    def from_far(k):
        zq = lax.rem(z + 4 - k, 4)
        came(6, k)
        remote(r.kvt.at[6, zq], r.kvt.at[7, zq], ss.ag.at[4 * 6 + k], rr.ag.at[4 * 7 + k], sib).start()

    own_piece(0)
    for i in (1, 3, 2):
        zp, to = zpeer(i)
        push(r.q_s.at[zp], r.q.at[z], ss.az.at[i + 2], rr.az.at[i + 2], to)
    r.q[z] = r.q_s[z]
    loads[1].wait()
    half = pl.ds(pl.multiple_of(128 * c, 128), 128)
    for i in range(1, 4):
        ym, to = ypeer(i)
        push(r.wout.at[half, :], r.wfull.at[mp, half, :], ss.wf.at[i - 1], rr.wf.at[i - 1], to)
    r.wfull[mp] = r.wout[...]
    r.vt1[64:80, :] = jnp.ones((16, 1024), bf16)
    ends = doc_ends(r.lengths)
    feature = lax.broadcasted_iota(jnp.int32, (64, 256), 0)
    loads[2].wait()
    mine = pl.ds(pl.multiple_of(256 * mp, 256), 256)
    r.cotq_s[...] = dot(slot_matrix(r.chosen[...]), r.cot[:, mine]).astype(bf16).reshape(EX, 16, 256)
    r.cotq[mp, ex] = r.cotq_s[ex]
    arrive(r.kvt.at[0, lax.rem(z + 3, 4)], rr.az.at[0])
    own_piece(1)
    arrive(r.kvt.at[0, lax.rem(z + 1, 4)], rr.az.at[2])
    own_piece(3)
    from_sides(0)
    arrive(r.kvt.at[0, lax.rem(z + 2, 4)], rr.az.at[1])
    own_piece(2)
    zp, to = zpeer(2)
    push(r.normed, r.nall.at[z], ss.na.at[1], rr.na.at[1], to)
    r.nall[z] = r.normed[...]
    for i in range(1, 4):
        arrive(r.q.at[lax.rem(z + 4 - i, 4)], rr.az.at[i + 2])
    for b in range(4):
        docs = doc_row(ends, (b * 8 + j) * 256, 256)
        r.qaug[b, 0:64] = r.q[b]
        r.qaug[b, 64:128] = jnp.where(feature == docs, 0.0, negative_fill).astype(bf16)
        r.peak[b] = jnp.full((1, 256), negative_fill, f32)
        r.acc[b] = jnp.zeros((80, 256), f32)

    def load_keys(slot, jp):
        for b in range(4):
            docs = doc_row(ends, (b * 8 + jp) * 256, 256)
            hot = (feature == docs).astype(f32).astype(bf16)
            r.kaug[256 * b:256 * b + 256, :] = transposed(
                jnp.concatenate([r.kvt[slot, b, 0:64], hot], axis=0))

    def scores(b, n, causal):
        s = dot(r.kaug[0:n, :], r.qaug[b])
        if causal:
            rows = lax.broadcasted_iota(jnp.int32, (n, 256), 0)
            cols = lax.broadcasted_iota(jnp.int32, (n, 256), 1)
            s = jnp.where(rows - 256 * b <= cols, s, negative_fill)
        return s

    def load_chunk(slot, jp):
        load_keys(slot, jp)
        for b in range(4):
            r.vt1[0:64, 256 * b:256 * b + 256] = r.kvt[slot, b, 64:128]

    def update(b, n, causal):
        s = scores(b, n, causal)
        old = r.peak[b]
        new = jnp.maximum(old, jnp.max(s, axis=0, keepdims=True))
        p = jnp.exp(s - new).astype(bf16)
        r.acc[b] = r.acc[b] * jnp.exp(old - new) + dot(r.vt1[:, 0:n], p)
        r.peak[b] = new

    load_chunk(0, j)
    for b in range(4):
        update(b, 256 * b + 256, True)

    def chunk(i, carry):
        u = i // 2
        side = ((u + 1) // 2) % 2
        xp = (x + d * (2 * (i % 2) - 1) * side + 2 * (u // 3) + 8) % 4
        jp = xp * 2 + (c + (1 - side) * (i % 2) + side * (u // 2)) % 2

        @pl.when(i == 1)
        def _():
            from_sides(1)
            from_far(0)
            for k in range(4):
                came(1, k)

        @pl.when(i == 2)
        def _():
            from_sides(3)
            from_far(1)
            from_sides(2)

        @pl.when(i == 3)
        def _():
            from_far(3)

        @pl.when(i == 4)
        def _():
            from_far(2)
            for k in range(4):
                came(4, k)
            to_all(lambda to: r.cotq_s.at[to], r.cotq.at[mp, ex], "co")

        @pl.when(i == 5)
        def _():
            for k in range(4):
                came(5, k)
            for i in range(1, 4):
                ym, to = ypeer(4 - i)
                arrive(r.wfull.at[ym, half, :], rr.wf.at[i - 1])
                remote(
                    r.wfull.at[ym, half, :], r.wfull.at[ym, half, :], ss.wd.at[i - 1], rr.wd.at[i - 1], sib).start()

        @pl.when(i == 7)
        def _():
            for k in range(4):
                came(7, k)

        load_chunk(i, jp)

        @pl.when(jp < j)
        def _():
            for b in range(4):
                update(b, 256 * b + 256, False)

        @pl.when(jp > j)
        def _():
            for b in range(1, 4):
                update(b, 256 * b, False)

        return carry

    lax.fori_loop(1, 8, chunk, 0)
    for b in range(4):
        total = r.acc[b, 64:65]
        ot = r.acc[b, 0:64] / total
        r.ot[b] = ot
        r.lse[b] = r.peak[b] + jnp.log(total)
        r.o_s[b] = ot.astype(bf16)
    for i in (1, 3, 2):
        zp, to = zpeer(i)
        push(r.o_s.at[zp], r.att.at[mp, z], ss.oz.at[i - 1], rr.oz.at[i - 1], to)
    r.att[mp, z] = r.o_s[z]
    for i in range(1, 4):
        zp, _ = zpeer(4 - i)
        arrive(r.att.at[mp, zp], rr.oz.at[i - 1])
    for i in (1, 3, 2):
        ym, to = ypeer(i)
        push(r.att.at[mp], r.att.at[mp], ss.oy.at[i - 1], rr.oy.at[i - 1], to)
    from_all(r.cotq_s.at[ex], lambda source: r.cotq.at[mp, source], "co")
    other = pl.ds(pl.multiple_of(128 - 128 * c, 128), 128)
    for i in range(1, 4):
        ym, _ = ypeer(4 - i)
        arrive(r.wfull.at[ym, other, :], rr.wd.at[i - 1])
    for i in range(1, 4):
        ym, _ = ypeer(4 - i)
        arrive(r.att.at[ym], rr.oy.at[i - 1])
    for i in (1, 3, 2):
        ym, to = ypeer(i)
        push(r.cotq.at[mp], r.cotq.at[mp], ss.cy.at[i - 1], rr.cy.at[i - 1], to)
    value = r.tokens[...].astype(f32) + dot(r.att[...].reshape(1024, 256), r.wfull[...].reshape(1024, 1024), 0, 0)
    r.resid[...] = value
    for k in range(4):
        @pl.when(mp == k)
        def _():
            r.rescol[...] = value[:, 256 * k:256 * k + 256]
    unit, _ = norm_parts(value)
    r.outgoing[...] = dot(slot_matrix(r.chosen[...]), (unit * r.gain2[...]).astype(bf16)).astype(bf16).reshape(
        EX, 16, 1024)
    to_all(lambda to: r.outgoing.at[to], r.arrived.at[ex], "di")
    r.arrived[ex] = r.outgoing[ex]
    loads[3].wait()
    for i in range(1, 4):
        ym, _ = ypeer(4 - i)
        arrive(r.cotq.at[ym], rr.cy.at[i - 1])
    for le in range(2):
        rows = jnp.concatenate([one_expert(r.cotq[k], le) for k in range(4)], axis=1)
        r.crows[le] = rows
        r.gh[le] = dot(rows, r.wex[le], 1, 1)
    loads[4].wait()
    from_all(r.outgoing.at[ex], lambda source: r.arrived.at[source], "di")
    for le in range(2):
        rows = one_expert(r.arrived[...], le)
        r.xrows[le] = rows
        hidden, slope = gelu_parts(dot(rows, r.win[le]))
        r.hid[le] = hidden.astype(bf16)
        gpre = (r.gh[le] * slope).astype(bf16)
        r.gpre[le] = gpre
        for k in range(4):
            r.part[le, k] = dot(gpre, r.win[le, 256 * k:256 * k + 256, :], 1, 1).astype(bf16)
        for i in (1, 3, 2):
            ym, to = ypeer(i)
            push(r.part.at[le, ym], r.rs.at[le, i - 1], ss.rs.at[3 * le + i - 1], rr.rs.at[3 * le + i - 1], to)
    stores = [
        pltpu.make_async_copy(src, dst, ls.store.at[i])
        for i, (src, dst) in enumerate([
            (r.xrows, r.x_hbm), (r.crows, r.c_hbm), (r.hid, r.hid_hbm), (r.gpre, r.gpre_hbm)])
    ]
    for copy in stores:
        copy.start()
    first = dot(r.hid[0], r.wex[0])
    r.branch[...] = both_experts(first, dot(r.hid[1], r.wex[1]))
    sums = []
    for le in range(2):
        total = r.part[le, mp].astype(f32)
        for i in range(3):
            arrive(r.rs.at[le, i], rr.rs.at[3 * le + i])
            total = total + r.rs[le, i].astype(f32)
        sums.append(total)
    r.back_s[...] = both_experts(sums[0], sums[1])
    to_all(lambda to: r.back_s.at[to], r.back.at[ex], "ba")
    r.back[ex] = r.back_s[ex]
    from_all(r.back_s.at[ex], lambda source: r.back.at[source], "ba")
    r.gn[mp] = dot(slot_matrix(r.chosen[...]), r.back[...].reshape(512, 256), 0, 0).astype(bf16)
    for i in (1, 3, 2):
        ym, to = ypeer(i)
        push(r.gn.at[mp], r.gn.at[mp], ss.gy.at[i - 1], rr.gy.at[i - 1], to)
    unit, inverse = norm_parts(r.resid[...])
    for i in range(1, 4):
        ym, _ = ypeer(4 - i)
        arrive(r.gn.at[ym], rr.gy.at[i - 1])
    grad = jnp.concatenate([r.gn[k] for k in range(4)], axis=1).astype(f32)
    grad_in, ggrad = norm_back(grad, r.gain2[...], unit, inverse)
    r.ggrad[...] = ggrad
    gres = r.cot[...].astype(f32) + grad_in
    r.gres[...] = gres
    low = gres.astype(bf16)
    r.dheads[...] = dot(r.wfull[mp], low, 1, 1).astype(bf16).reshape(4, 64, 256)
    for i in (1, 3, 2):
        zp, to = zpeer(i)
        push(r.dheads.at[zp], r.dob.at[z], ss.dz.at[i - 1], rr.dz.at[i - 1], to)
    r.dob[z] = r.dheads[z]
    wgrad = dot(r.att[mp].reshape(256, 256), low).astype(bf16)
    r.wgp[0] = wgrad[:, 0:512].reshape(16, 16, 512)
    r.wgp[1] = wgrad[:, 512:1024].reshape(16, 16, 512)
    push(r.wgp.at[1 - c], r.wgs, ss.wg.at[0], rr.wg.at[0], sib)
    for i in range(1, 4):
        ym, to = ypeer(i)
        push(
            r.branch.at[:, :, pl.ds(pl.multiple_of(256 * ym, 256), 256)], r.brs.at[i - 1],
            ss.br.at[i - 1], rr.br.at[i - 1], to)
    zero = jnp.zeros((64, 256), bf16)
    for i in range(1, 4):
        zp, _ = zpeer(4 - i)
        arrive(r.dob.at[zp], rr.dz.at[i - 1])
    for i in (1, 3):
        zp, to = zpeer(i)
        push(r.normed, r.nall.at[z], ss.na.at[i - 1], rr.na.at[i - 1], to)
    for b in range(4):
        r.dopad[b, 0:64] = zero
        r.dopad[b, 64:128] = r.dob[b]
        r.qd[b, 0:256] = transposed(jnp.concatenate([r.q[b], zero], axis=0))
        r.qd[b, 256:512] = transposed(jnp.concatenate([zero, r.dob[b]], axis=0))
        r.delta[b] = jnp.sum(r.dob[b].astype(f32) * r.ot[b], axis=0, keepdims=True)
        r.dq[b] = jnp.zeros((64, 256), f32)

    def load_back(slot, jp):
        load_keys(slot, jp)
        for b in range(4):
            r.kvn[256 * b:256 * b + 256, :] = transposed(r.kvt[slot, b])
            r.kt[:, 256 * b:256 * b + 256] = r.kvt[slot, b, 0:64]

    def back_update(b, n, causal):
        p = jnp.exp(scores(b, n, causal) - r.lse[b])
        dp = dot(r.kvn[0:n, :], r.dopad[b])
        ds = (p * (dp - r.delta[b])).astype(bf16)
        added = dot(ds, r.qd[b, 0:256]) + dot(p.astype(bf16), r.qd[b, 256:512])
        if b == 3:
            r.dkv[0:n] = added
        else:
            r.dkv[0:n] = r.dkv[0:n] + added
        r.dq[b] = r.dq[b] + dot(r.kt[:, 0:n], ds)

    def back_chunk(i, carry):
        p = i // 2
        w = p + (p // 2) * (1 - 2 * (p % 2))
        g = (2 + d * w + 4) % 4
        flip = 1 - i % 2
        odd = g % 2
        slot = odd * (2 + g // 2 + 2 * flip) + (1 - odd) * (3 * g + flip)
        xp = (x - d * g + 8) % 4
        jp = xp * 2 + (c + flip) % 2
        load_back(slot, jp)

        @pl.when(jp < j)
        def _():
            for b in range(3, -1, -1):
                back_update(b, 256 * b + 256, False)

        @pl.when(jp > j)
        def _():
            r.dkv[768:1024] = jnp.zeros((256, 128), f32)
            for b in range(3, 0, -1):
                back_update(b, 256 * b, False)

        @pl.when(i % 2 == 0)
        def _():
            r.sb[p] = r.dkv[...].astype(bf16)
            remote(r.sb.at[p], r.sr.at[p], ss.sb.at[p], rr.sb.at[p], sib).start()

        @pl.when(i % 2 == 1)
        def _():
            arrive(r.sr.at[p], rr.sb.at[p])
            r.xs[p] = (r.dkv[...] + r.sr[p].astype(f32)).astype(bf16)
            remote(r.xs.at[p], r.xr.at[p], ss.xs.at[p], rr.xs.at[p], (z * 8 + xp * 2 + c, mp)).start()

        @pl.when(i == 1)
        def _():
            arrive(r.wgs, rr.wg.at[0])
            r.wgq[...] = (r.wgp[c].astype(f32) + r.wgs[...].astype(f32)).astype(bf16)

            def one(k, carry):
                to = lax.rem(chip + k, 16)
                remote(r.wgq.at[to], r.wgr.at[k - 1], ss.wq.at[k - 1], rr.wq.at[k - 1], (to * 2 + c, mp)).start()
                return carry

            lax.fori_loop(1, 16, one, 0)

        @pl.when(i == 4)
        def _():
            total = r.branch[:, :, mine].astype(f32)
            for k in range(3):
                arrive(r.brs.at[k], rr.br.at[k])
                total = total + r.brs[k].astype(f32)
            r.bs[...] = total.astype(bf16)
            to_all(lambda to: r.bs.at[to], r.bret.at[ex], "bb")
            r.bret[ex] = r.bs[ex]

        @pl.when(i == 5)
        def _():
            total = r.wgq[chip].astype(f32)
            for k in range(15):
                arrive(r.wgr.at[k], rr.wq.at[k])
                total = total + r.wgr[k].astype(f32)
            r.wgf[ex] = total.astype(bf16)
            spread(r.wgf, "wa", "wb")

        return carry

    lax.fori_loop(0, 7, back_chunk, 0)
    load_back(0, j)
    for b in range(3, -1, -1):
        back_update(b, 256 * b + 256, True)
    arrive(r.sr.at[3], rr.sb.at[3])
    total = r.dkv[...] + r.sr[3].astype(f32)
    pass_on(r.wgf, "wa", "wb")
    for p in range(3):
        arrive(r.xr.at[p], rr.xs.at[p])
        total = total + r.xr[p].astype(f32)
    low = total.astype(bf16)
    for b in range(4):
        r.zs[b, 0:64] = (r.dq[b] * HEAD_DIM ** (-0.5)).astype(bf16)
        r.zs[b, 64:192] = transposed(low[256 * b:256 * b + 256])
    for i in (1, 3, 2):
        zp, to = zpeer(i)
        push(r.zs.at[zp], r.zr.at[z], ss.zq.at[i - 1], rr.zq.at[i - 1], to)
    r.zr[z] = r.zs[z]
    for i in range(1, 4):
        zp, _ = zpeer(4 - i)
        arrive(r.nall.at[zp], rr.na.at[i - 1])
    wt = dot(r.zs[0], r.nall[0])
    for b in range(1, 4):
        wt = wt + dot(r.zs[b], r.nall[b])
    wt = wt.astype(bf16)
    for k in range(8):
        r.wp[k] = wt[:, 128 * k:128 * k + 128]
    for i in range(1, 8):
        jt = lax.rem(j + i, 8)
        push(r.wp.at[jt], r.wr.at[i - 1], ss.wp.at[i - 1], rr.wp.at[i - 1], (z * 8 + jt, mp))
    for i in range(1, 4):
        zp, _ = zpeer(4 - i)
        arrive(r.zr.at[zp], rr.zq.at[i - 1])
    part = None
    for k in range(3):
        heads = transposed(jnp.concatenate([r.zr[h, 64 * k:64 * k + 64] for h in range(4)], axis=0))
        term = dot(heads, r.wqkv[k], 1, 1)
        part = term if part is None else part + term
    r.gnp[...] = part.astype(bf16).reshape(4, 64, 1024)
    for i in (1, 3, 2):
        ym, to = ypeer(i)
        push(r.gnp.at[ym], r.ry.at[i - 1], ss.ry.at[i - 1], rr.ry.at[i - 1], to)
    summed = r.wp[j].astype(f32)
    for i in range(7):
        arrive(r.wr.at[i], rr.wp.at[i])
        summed = summed + r.wr[i].astype(f32)
    r.pieces[ex] = summed.astype(bf16)
    spread(r.pieces, "pa", "pb")
    from_all(r.bs.at[ex], lambda source: r.bret.at[source], "bb")
    rows = dot(slot_matrix(r.chosen[...]), r.bret[...].reshape(512, 256), 0, 0)
    r.out[...] = (r.rescol[...] + rows).astype(bf16)
    passed(r.wgf, "wb")
    for k in range(32):
        r.wout_out[16 * (k // 2):16 * (k // 2) + 16, 512 * (k % 2):512 * (k % 2) + 512] = r.wgf[k]
    grad = r.gnp[mp].astype(f32)
    for i in range(3):
        arrive(r.ry.at[i], rr.ry.at[i])
        grad = grad + r.ry[i].astype(f32)
    here = pl.ds(pl.multiple_of(64 * mp, 64), 64)
    unit, inverse = norm_parts(r.tokens[here, :].astype(f32))
    grad_in, one_gain = norm_back(grad, r.gain1[...], unit, inverse)
    r.small[...] = one_gain
    for i in (1, 3, 2):
        ym, to = ypeer(i)
        push(r.small, r.smally.at[i - 1], ss.sy.at[i - 1], rr.sy.at[i - 1], to)
    r.igrad[here, :] = (r.gres[here, :] + grad_in).astype(bf16)
    for i in (1, 3, 2):
        ym, to = ypeer(i)
        push(r.igrad.at[here, :], r.igrad.at[here, :], ss.ay.at[i - 1], rr.ay.at[i - 1], to)
    for i in range(3):
        arrive(r.smally.at[i], rr.sy.at[i])
        one_gain = one_gain + r.smally[i]
    r.smalle[ex, 0:1] = one_gain
    r.smalle[ex, 1:2] = r.ggrad[...]
    to_all(lambda to: r.smalle.at[ex], r.smalle.at[ex], "se")
    pass_on(r.pieces, "pa", "pb")
    passed(r.pieces, "pb")
    for k in range(3):
        for row in range(8):
            block = jnp.concatenate([r.pieces[8 * h + row, 64 * k:64 * k + 64] for h in range(4)], axis=0)
            r.qkv_out[k, 128 * row:128 * row + 128] = transposed(block)
    from_all(r.smalle.at[ex], lambda source: r.smalle.at[source], "se")
    r.gains[...] = jnp.sum(r.smalle[...], axis=0)
    for i in range(1, 4):
        ym, _ = ypeer(4 - i)
        there = pl.ds(pl.multiple_of(64 * ym, 64), 64)
        arrive(r.igrad.at[there, :], rr.ay.at[i - 1])
    for src, ssem in pending:
        left(src, ssem)
    for k in range(28):
        left(r.kvt.at[0, 0], ss.ag.at[k])
    for k in range(3):
        left(r.wfull.at[0, half, :], ss.wd.at[k])
    for p in range(4):
        left(r.sb.at[p], ss.sb.at[p])
    for p in range(3):
        left(r.xs.at[p], ss.xs.at[p])
    for k in range(15):
        left(r.wgq.at[0], ss.wq.at[k])
    for copy in stores:
        copy.wait()


def layer(*args):
    spaces = {"x_hbm": ANY, "c_hbm": ANY, "hid_hbm": ANY, "gpre_hbm": ANY}
    return pl.pallas_call(
        layer_kernel,
        out_shape=[jax.ShapeDtypeStruct(s, t) for s, t in OUTS.values()],
        in_specs=[SM, VM, VM, VM, VM, ANY, ANY, ANY, ANY, ANY],
        out_specs=[spaces.get(name, VM) for name in OUTS],
        scratch_shapes=[pltpu.VMEM(s, t) for s, t in BUFFERS.values()]
        + [DMA(s) for group in (LOCAL, SENT, TAKEN) for s in group.values()],
        name="layer",
        compiler_params=pltpu.CompilerParams(
            collective_id=0, has_side_effects=True, vmem_limit_bytes=VMEM_BYTES),
    )(*args)


def finish_kernel(x, gpre, hid, cots, qkv, wout, out, igrad, in_grad, out_grad, qkv_o, wout_o, out_o, igrad_o):
    in_grad[0] = dot(x[0], gpre[0], 0, 0)
    out_grad[0] = dot(hid[0], cots[0], 0, 0)
    qkv_o[...] = qkv[...].astype(f32)
    wout_o[...] = wout[...].astype(f32)
    out_o[...] = out[...]
    igrad_o[...] = igrad[...]


def finish(x, gpre, hid, cots, qkv, wout, out, igrad):
    width, steps = 256, 4
    n = 2 * steps
    tall = pl.BlockSpec((1, 256, width), lambda e, i: (e, 0, i))
    whole = pl.BlockSpec((1, 256, 1024), lambda e, i: (e, 0, 0))
    made = pl.BlockSpec((1, width, 1024), lambda e, i: (e, i, 0))

    def rows(shape):
        if len(shape) == 3:
            return pl.BlockSpec((shape[0], shape[1] // n, shape[2]), lambda e, i: (0, e * steps + i, 0))
        return pl.BlockSpec((shape[0] // n, shape[1]), lambda e, i: (e * steps + i, 0))

    plain = [rows(v.shape) for v in (qkv, wout, out, igrad)]
    big = jax.ShapeDtypeStruct((2, 1024, 1024), f32)
    return pl.pallas_call(
        finish_kernel,
        grid=(2, steps),
        out_shape=[
            big, big, jax.ShapeDtypeStruct(qkv.shape, f32), jax.ShapeDtypeStruct(wout.shape, f32),
            jax.ShapeDtypeStruct(out.shape, bf16), jax.ShapeDtypeStruct(igrad.shape, bf16)],
        in_specs=[tall, whole, tall, whole] + plain,
        out_specs=[made, made] + plain,
        name="finish",
        compiler_params=pltpu.CompilerParams(vmem_limit_bytes=48 << 20),
        cost_estimate=pl.CostEstimate(flops=2 * 2 * 2 * 256 * 1024 * 1024, bytes_accessed=28 << 20, transcendentals=0),
    )(x, gpre, hid, cots, qkv, wout, out, igrad)


def on_device(
    tokens, hash_ids, lengths, norm1_gain, qkv_weight, out_weight, norm2_gain, expert_in, expert_out, cotangent,
):
    x, cots, hid, gpre, out, igrad, gains, qkv, wout = layer(
        lengths, tokens, norm1_gain.reshape(1, 1024), norm2_gain.reshape(1, 1024), hash_ids.reshape(1, 256),
        jnp.transpose(qkv_weight, (1, 0, 2)), out_weight, cotangent, expert_in, expert_out)
    in_grad, out_grad, qkv, wout, out, igrad = finish(x, gpre, hid, cots, qkv, wout, out, igrad)
    return out, igrad, gains[0], jnp.transpose(qkv, (1, 0, 2)), wout, gains[1], in_grad, out_grad


def solution(mesh):
    placed = (
        P("ex", None), P("ex", None), P(), P(), P(None, None, "mp"), P("mp", None), P(),
        P("ex", None, "mp"), P("ex", "mp", None), P("ex", None),
    )
    return jax.shard_map(
        on_device,
        mesh=mesh,
        in_specs=placed,
        out_specs=(
            P("ex", "mp"), P("ex", None), P(), P(None, None, "mp"), P("mp", None), P(),
            P("ex", None, "mp"), P("ex", "mp", None),
        ),
        check_vma=False,
    )
```

time: 853 us -> 177 us (0.21)
  waiting for transfers between devices: 598 us -> 0 us
  Pallas kernels: 0 us -> 166 us
  blocking collectives: 62.8 us -> 0 us
  matrix products: 48.5 us -> 0 us
  local copies, waits for them, and re-layouts: 51.7 us -> 9.26 us
  starting transfers between devices: 31.5 us -> 0 us
  loops' own time: 22.7 us -> 0 us
  other arithmetic: 16 us -> 0 us
  between operations: 14.6 us -> 0.77 us
    psum x4 -> x0, waiting for transfers between devices: 272 us -> none  [the longest x1 101 us: on_device(): lax.psum(qkv_grad_part.astype(jnp.bfloat16), 'ex').astype(jnp.float32)]
    reduce_scatter x1 -> x0, waiting for transfers between devices: 226 us -> none  [on_device(): lax.psum_scatter(grad_keys.astype(jnp.bfloat16), 'ex', scatter_dimension=...]
    pallas_call x0 -> x2, Pallas kernels: none -> 166 us  [the longest x1 156 us: layer(): pl.pallas_call(layer_kernel, out_shape=[jax.ShapeDtypeStruct(s, t) for s,...]
    psum x1 -> x0, blocking collectives: 62.8 us -> none  [on_device(): lax.psum(gain_one_grad.astype(jnp.bfloat16), 'ex').astype(jnp.float32)]
    all_gather x1 -> x0, waiting for transfers between devices: 56.3 us -> none  [on_device(): gathered = lax.all_gather(key_value, 'ex', axis=0, tiled=True)]
    dot_general x23 -> x0, matrix products: 48.5 us -> none  [the longest x1 6.73 us: on_device(): jnp.einsum('erf,erd->efd', hidden_low, grad_arrived, preferred_element_ty...]
    all_to_all x4 -> x0, waiting for transfers between devices: 44.2 us -> none  [the longest x1 16.5 us: on_device(): lax.all_to_all(grad_rows.reshape(local_experts, ex_count, capacity, model...]
    all_to_all x4 -> x0, starting transfers between devices: 31.3 us -> none  [the longest x1 9.67 us: on_device(): lax.all_to_all(outgoing.reshape(ex_count, local_experts, capacity, model_...]
  transfers between devices with their start and end apart: 10 -> 0, of which waited for: 9 -> 0; matrix products, arithmetic and copies ran while one was open for 5% -> 0% of each run, Pallas kernels for 0% -> 0%
where the time goes in v2:
time: 177 us; the launch traced here: 176 us
  Pallas kernels  166 us (94%)
  local copies, waits for them, and re-layouts  9.26 us (5%)
    pallas_call x1, Pallas kernels, layer(): pl.pallas_call(layer_kernel, out_shape=[jax.ShapeDtypeStruct(s, t) for s,...  156 us
    pallas_call x1, Pallas kernels, finish(): pl.pallas_call(finish_kernel, grid=(2, steps), out_shape=[big, big, jax.S...  9.63 us
    unnamed x14, local copies, waits for them, and re-layouts  7.88 us

profile of v2, /device:TPU:1, one launch (start us, length us, event | category | flops | bytes accessed | tf_op | source)
XLA Modules:
  0.0 176.0 jit_solution(15673315721882576050)
XLA Ops:
  0.6 156.3 %layer.1 = (bf16[2,256,1024]{2,1,0:T(8,128)(2,1)}, bf16[2,256,1024]{2,1,0:T(8,128)(2,1)}, bf16[2,256,1024]{2,1,0:T(8,128)(2,1)}, bf16[2,256,1024]{2,1,0:T(8,128)...) custom-call(s32[9]{0:T(128)} %refs_0_.1, ...), custom_call_target="tpu_custom_call" | custom-call | tf_op jit(solution)/shard_map/layer/pallas_call | solution.py:741
  157.0 1.4 fusion
  158.4 0.0 copy-start
  158.4 1.2 copy-done
  159.6 0.0 copy-start.1
  159.6 1.2 copy-done.1
  160.8 0.0 copy-start.2
  160.8 1.2 copy-done.2
  162.0 0.0 copy-start.3
  162.0 1.2 copy-done.3
  163.3 0.0 copy-start.4
  163.3 1.0 copy-done.4
  164.3 0.0 copy-start.5
  164.3 1.0 copy-done.5
  165.4 0.0 copy-start.6
  165.4 0.9 copy-done.6
  166.3 9.6 %finish.1 = (f32[2,1024,1024]{2,1,0:T(8,128)}, f32[2,1024,1024]{2,1,0:T(8,128)}, f32[3,1024,256]{2,1,0:T(8,128)}, f32[256,1024]{1,0:T(8,128)}, bf16[256,256]{1,0:T(8,128)(2,1)}, /*index=5*/bf16[256,1024]{1,0:T(8,128)(2,1)}) custom-call(bf16[2,256,1024]{2,1,0:T(8,128)(2,1)S(1)} %copy-done, bf16[2,256,1024]{2,1,0:T(8,128)(2,1)S(1)} %copy-done.3, ...), custom_call_target="tpu_custom_call" | custom-call | flops 2147483648 | bytes 29360128 | tf_op jit(solution)/shard_map/finish/pallas_call | solution.py:777
Async XLA Ops:
  158.4 1.2 copy-start
  159.6 1.2 copy-start.1
  160.8 1.2 copy-start.2
  162.0 1.2 copy-start.3
  163.3 1.0 copy-start.4
  164.3 1.0 copy-start.5
  165.4 0.9 copy-start.6

commit v3 on v2

--- a/solution.py
+++ b/solution.py
@@ -127,7 +127,7 @@
 ARGS = ["lengths", "tokens", "gain1", "gain2", "chosen", "wqkv_hbm", "wout_hbm", "cot_hbm", "win_hbm", "wex_hbm"]
 OUTS = {
     "x_hbm": (ROWS, bf16), "c_hbm": (ROWS, bf16), "hid_hbm": (ROWS, bf16), "gpre_hbm": (ROWS, bf16),
-    "out": ((256, 256), bf16), "igrad": ((256, 1024), bf16), "gains": ((2, 1024), f32),
+    "out": ((256, 256), bf16), "igrad": ((256, 1024), bf16), "gain1_out": ((1, 1024), f32), "gain2_out": ((1, 1024), f32),
     "qkv_out": ((3, 1024, 256), bf16), "wout_out": ((256, 1024), bf16),
 }
 BUFFERS = {
@@ -144,13 +144,14 @@
     "part": ((2, 4, 256, 256), bf16), "rs": ((2, 3, 256, 256), bf16), "back_s": ((32, 16, 256), bf16),
     "back": ((32, 16, 256), bf16), "gn": ((4, 256, 256), bf16), "resid": ((256, 1024), f32),
     "rescol": ((256, 256), f32), "gres": ((256, 1024), f32), "branch": ((32, 16, 1024), bf16),
-    "wgp": ((2, 16, 16, 512), bf16), "wgs": ((16, 16, 512), bf16), "wgq": ((16, 16, 512), bf16),
-    "wgr": ((15, 16, 512), bf16), "wgf": ((32, 16, 512), bf16),
+    "wgp": ((2, 4, 4, 16, 512), bf16), "wgs": ((4, 4, 16, 512), bf16), "wgq": ((4, 4, 16, 512), bf16),
+    "wgz": ((3, 4, 16, 512), bf16), "wgx": ((4, 16, 512), bf16), "wgr": ((3, 16, 512), bf16),
+    "wgf": ((2, 4, 4, 16, 512), bf16),
     "dheads": ((4, 64, 256), bf16), "dob": ((4, 64, 256), bf16), "brs": ((3, 32, 16, 256), bf16),
     "bs": ((32, 16, 256), bf16), "bret": ((32, 16, 256), bf16), "dopad": ((4, 128, 256), bf16),
     "qd": ((4, 512, 128), bf16), "delta": ((4, 1, 256), f32), "kvn": ((1024, 128), bf16),
     "kt": ((64, 1024), bf16), "dkv": ((1024, 128), f32), "dq": ((4, 64, 256), f32),
-    "sb": ((4, 1024, 128), bf16), "sr": ((4, 1024, 128), bf16), "xs": ((3, 1024, 128), bf16),
+    "sb": ((4, 1024, 128), bf16), "sr": ((4, 1024, 128), bf16), "xs": ((4, 1024, 128), bf16),
     "xr": ((3, 1024, 128), bf16), "zs": ((4, 192, 256), bf16), "zr": ((4, 192, 256), bf16),
     "wp": ((8, 192, 128), bf16), "wr": ((7, 192, 128), bf16), "pieces": ((32, 192, 128), bf16),
     "gnp": ((4, 64, 1024), bf16), "ry": ((3, 64, 1024), bf16), "small": ((1, 1024), f32),
@@ -160,7 +161,7 @@
 SENT = {
     "az": (6,), "ag": (28,), "wf": (3,), "wd": (3,), "co": (31,), "cy": (3,), "na": (3,), "oz": (3,), "oy": (3,),
     "di": (31,), "rs": (6,), "ba": (31,), "gy": (3,), "dz": (3,), "br": (3,), "bb": (31,), "sb": (4,), "xs": (3,),
-    "wg": (1,), "wq": (15,), "wa": (15,), "wb": (16,), "zq": (3,), "wp": (7,), "pa": (15,), "pb": (16,),
+    "wg": (1,), "wz": (3,), "wx": (3,), "wa": (3,), "wb": (3,), "wc": (1,), "zq": (6,), "wp": (7,), "pa": (15,), "pb": (16,),
     "ry": (3,), "ay": (3,), "sy": (3,), "se": (31,),
 }
 TAKEN = dict(SENT, ag=(32,))
@@ -192,6 +193,10 @@
     def ypeer(i):
         ym = lax.rem(mp + i, MP)
         return ym, (ex, ym)
+
+    def xpeer(i):
+        xq = lax.rem(x + i, 4)
+        return xq, (z * 8 + xq * 2 + c, mp)
 
     def remote(src, dst, ssem, rsem, device):
         return pltpu.make_async_remote_copy(
@@ -355,17 +360,23 @@
         for b in range(4):
             r.vt1[0:64, 256 * b:256 * b + 256] = r.kvt[slot, b, 64:128]
 
-    def update(b, n, causal):
-        s = scores(b, n, causal)
-        old = r.peak[b]
-        new = jnp.maximum(old, jnp.max(s, axis=0, keepdims=True))
-        p = jnp.exp(s - new).astype(bf16)
-        r.acc[b] = r.acc[b] * jnp.exp(old - new) + dot(r.vt1[:, 0:n], p)
-        r.peak[b] = new
+    def forward(tiles, causal):
+        def gather(b, n, p, factor):
+            r.acc[b] = r.acc[b] * factor + dot(r.vt1[:, 0:n], p)
+
+        held = None
+        for b, n in tiles:
+            s = scores(b, n, causal)
+            if held is not None:
+                gather(*held)
+            old = r.peak[b]
+            new = jnp.maximum(old, jnp.max(s, axis=0, keepdims=True))
+            held = (b, n, jnp.exp(s - new).astype(bf16), jnp.exp(old - new))
+            r.peak[b] = new
+        gather(*held)
 
     load_chunk(0, j)
-    for b in range(4):
-        update(b, 256 * b + 256, True)
+    forward([(b, 256 * b + 256) for b in (3, 2, 1, 0)], True)
 
     def chunk(i, carry):
         u = i // 2
@@ -416,13 +427,11 @@
 
         @pl.when(jp < j)
         def _():
-            for b in range(4):
-                update(b, 256 * b + 256, False)
+            forward([(b, 256 * b + 256) for b in (3, 2, 1, 0)], False)
 
         @pl.when(jp > j)
         def _():
-            for b in range(1, 4):
-                update(b, 256 * b, False)
+            forward([(b, 256 * b) for b in (3, 2, 1)], False)
 
         return carry
 
@@ -527,8 +536,8 @@
         push(r.dheads.at[zp], r.dob.at[z], ss.dz.at[i - 1], rr.dz.at[i - 1], to)
     r.dob[z] = r.dheads[z]
     wgrad = dot(r.att[mp].reshape(256, 256), low).astype(bf16)
-    r.wgp[0] = wgrad[:, 0:512].reshape(16, 16, 512)
-    r.wgp[1] = wgrad[:, 512:1024].reshape(16, 16, 512)
+    r.wgp[0] = wgrad[:, 0:512].reshape(4, 4, 16, 512)
+    r.wgp[1] = wgrad[:, 512:1024].reshape(4, 4, 16, 512)
     push(r.wgp.at[1 - c], r.wgs, ss.wg.at[0], rr.wg.at[0], sib)
     for i in range(1, 4):
         ym, to = ypeer(i)
@@ -539,6 +548,11 @@
     for i in range(1, 4):
         zp, _ = zpeer(4 - i)
         arrive(r.dob.at[zp], rr.dz.at[i - 1])
+    arrive(r.wgs, rr.wg.at[0])
+    r.wgq[...] = (r.wgp[c].astype(f32) + r.wgs[...].astype(f32)).astype(bf16)
+    for i in (1, 3, 2):
+        zp, to = zpeer(i)
+        push(r.wgq.at[zp], r.wgz.at[i - 1], ss.wz.at[i - 1], rr.wz.at[i - 1], to)
     for i in (1, 3):
         zp, to = zpeer(i)
         push(r.normed, r.nall.at[z], ss.na.at[i - 1], rr.na.at[i - 1], to)
@@ -556,16 +570,24 @@
             r.kvn[256 * b:256 * b + 256, :] = transposed(r.kvt[slot, b])
             r.kt[:, 256 * b:256 * b + 256] = r.kvt[slot, b, 0:64]
 
-    def back_update(b, n, causal):
-        p = jnp.exp(scores(b, n, causal) - r.lse[b])
-        dp = dot(r.kvn[0:n, :], r.dopad[b])
-        ds = (p * (dp - r.delta[b])).astype(bf16)
-        added = dot(ds, r.qd[b, 0:256]) + dot(p.astype(bf16), r.qd[b, 256:512])
-        if b == 3:
-            r.dkv[0:n] = added
-        else:
-            r.dkv[0:n] = r.dkv[0:n] + added
-        r.dq[b] = r.dq[b] + dot(r.kt[:, 0:n], ds)
+    def backward(tiles, causal):
+        def gather(b, n, ds, p):
+            added = dot(ds, r.qd[b, 0:256]) + dot(p, r.qd[b, 256:512])
+            if b == 3:
+                r.dkv[0:n] = added
+            else:
+                r.dkv[0:n] = r.dkv[0:n] + added
+            r.dq[b] = r.dq[b] + dot(r.kt[:, 0:n], ds)
+
+        held = None
+        for b, n in tiles:
+            s = scores(b, n, causal)
+            dp = dot(r.kvn[0:n, :], r.dopad[b])
+            if held is not None:
+                gather(*held)
+            p = jnp.exp(s - r.lse[b])
+            held = (b, n, (p * (dp - r.delta[b])).astype(bf16), p.astype(bf16))
+        gather(*held)
 
     def back_chunk(i, carry):
         p = i // 2
@@ -580,14 +602,12 @@
 
         @pl.when(jp < j)
         def _():
-            for b in range(3, -1, -1):
-                back_update(b, 256 * b + 256, False)
+            backward([(b, 256 * b + 256) for b in (3, 2, 1, 0)], False)
 
         @pl.when(jp > j)
         def _():
             r.dkv[768:1024] = jnp.zeros((256, 128), f32)
-            for b in range(3, 0, -1):
-                back_update(b, 256 * b, False)
+            backward([(b, 256 * b) for b in (3, 2, 1)], False)
 
         @pl.when(i % 2 == 0)
         def _():
@@ -598,19 +618,32 @@
         def _():
             arrive(r.sr.at[p], rr.sb.at[p])
             r.xs[p] = (r.dkv[...] + r.sr[p].astype(f32)).astype(bf16)
-            remote(r.xs.at[p], r.xr.at[p], ss.xs.at[p], rr.xs.at[p], (z * 8 + xp * 2 + c, mp)).start()
+
+            @pl.when(p == 0)
+            def _():
+                remote(r.xs.at[0], r.xr.at[0], ss.xs.at[0], rr.xs.at[0], ahead).start()
+
+            @pl.when(p == 2 - c)
+            def _():
+                remote(r.xs.at[p], r.xr.at[1], ss.xs.at[1], rr.xs.at[1], behind).start()
+
+            @pl.when(p == 2)
+            def _():
+                arrive(r.xr.at[0], rr.xs.at[0])
+                r.xs[3] = (r.xs[1 + c].astype(f32) + r.xr[0].astype(f32)).astype(bf16)
+                remote(r.xs.at[3], r.xr.at[2], ss.xs.at[2], rr.xs.at[2], ahead).start()
 
         @pl.when(i == 1)
         def _():
-            arrive(r.wgs, rr.wg.at[0])
-            r.wgq[...] = (r.wgp[c].astype(f32) + r.wgs[...].astype(f32)).astype(bf16)
-
-            def one(k, carry):
-                to = lax.rem(chip + k, 16)
-                remote(r.wgq.at[to], r.wgr.at[k - 1], ss.wq.at[k - 1], rr.wq.at[k - 1], (to * 2 + c, mp)).start()
-                return carry
-
-            lax.fori_loop(1, 16, one, 0)
+            for k in range(3):
+                arrive(r.wgz.at[k], rr.wz.at[k])
+            total = r.wgq[z].astype(f32)
+            for k in range(3):
+                total = total + r.wgz[k].astype(f32)
+            r.wgx[...] = total.astype(bf16)
+            for k in (1, 3, 2):
+                xq, to = xpeer(k)
+                remote(r.wgx.at[xq], r.wgr.at[k - 1], ss.wx.at[k - 1], rr.wx.at[k - 1], to).start()
 
         @pl.when(i == 4)
         def _():
@@ -622,34 +655,39 @@
             to_all(lambda to: r.bs.at[to], r.bret.at[ex], "bb")
             r.bret[ex] = r.bs[ex]
 
-        @pl.when(i == 5)
-        def _():
-            total = r.wgq[chip].astype(f32)
-            for k in range(15):
-                arrive(r.wgr.at[k], rr.wq.at[k])
+        @pl.when(i == 6)
+        def _():
+            total = r.wgx[x].astype(f32)
+            for k in range(3):
+                arrive(r.wgr.at[k], rr.wx.at[k])
                 total = total + r.wgr[k].astype(f32)
-            r.wgf[ex] = total.astype(bf16)
-            spread(r.wgf, "wa", "wb")
+            r.wgf[c, z, x] = total.astype(bf16)
+            for k in (1, 3, 2):
+                _, to = xpeer(k)
+                remote(r.wgf.at[c, z, x], r.wgf.at[c, z, x], ss.wa.at[k - 1], rr.wa.at[k - 1], to).start()
 
         return carry
 
     lax.fori_loop(0, 7, back_chunk, 0)
     load_back(0, j)
-    for b in range(3, -1, -1):
-        back_update(b, 256 * b + 256, True)
+    backward([(b, 256 * b + 256) for b in (3, 2, 1, 0)], True)
+    for b in range(4):
+        r.zs[b, 0:64] = (r.dq[b] * HEAD_DIM ** (-0.5)).astype(bf16)
+    for i in (1, 3, 2):
+        zp, to = zpeer(i)
+        push(r.zs.at[zp, 0:64], r.zr.at[z, 0:64], ss.zq.at[i + 2], rr.zq.at[i + 2], to)
+    r.resid[...] = norm_parts(r.tokens[...].astype(f32))[0]
     arrive(r.sr.at[3], rr.sb.at[3])
     total = r.dkv[...] + r.sr[3].astype(f32)
-    pass_on(r.wgf, "wa", "wb")
-    for p in range(3):
-        arrive(r.xr.at[p], rr.xs.at[p])
-        total = total + r.xr[p].astype(f32)
+    for k in (1, 2):
+        arrive(r.xr.at[k], rr.xs.at[k])
+        total = total + r.xr[k].astype(f32)
     low = total.astype(bf16)
     for b in range(4):
-        r.zs[b, 0:64] = (r.dq[b] * HEAD_DIM ** (-0.5)).astype(bf16)
         r.zs[b, 64:192] = transposed(low[256 * b:256 * b + 256])
     for i in (1, 3, 2):
         zp, to = zpeer(i)
-        push(r.zs.at[zp], r.zr.at[z], ss.zq.at[i - 1], rr.zq.at[i - 1], to)
+        push(r.zs.at[zp, 64:192], r.zr.at[z, 64:192], ss.zq.at[i - 1], rr.zq.at[i - 1], to)
     r.zr[z] = r.zs[z]
     for i in range(1, 4):
         zp, _ = zpeer(4 - i)
@@ -664,14 +702,26 @@
         jt = lax.rem(j + i, 8)
         push(r.wp.at[jt], r.wr.at[i - 1], ss.wp.at[i - 1], rr.wp.at[i - 1], (z * 8 + jt, mp))
     for i in range(1, 4):
+        xq, _ = xpeer(4 - i)
+        arrive(r.wgf.at[c, z, xq], rr.wa.at[i - 1])
+    for i in (1, 3, 2):
+        _, to = zpeer(i)
+        push(r.wgf.at[c, z], r.wgf.at[c, z], ss.wb.at[i - 1], rr.wb.at[i - 1], to)
+    for i in range(1, 4):
         zp, _ = zpeer(4 - i)
-        arrive(r.zr.at[zp], rr.zq.at[i - 1])
+        arrive(r.zr.at[zp, 0:64], rr.zq.at[i + 2])
+        arrive(r.zr.at[zp, 64:192], rr.zq.at[i - 1])
     part = None
     for k in range(3):
         heads = transposed(jnp.concatenate([r.zr[h, 64 * k:64 * k + 64] for h in range(4)], axis=0))
         term = dot(heads, r.wqkv[k], 1, 1)
         part = term if part is None else part + term
     r.gnp[...] = part.astype(bf16).reshape(4, 64, 1024)
+    one_gain = jnp.sum(part * r.resid[...], axis=0, keepdims=True)
+    r.small[...] = one_gain
+    for i in (1, 3, 2):
+        ym, to = ypeer(i)
+        push(r.small, r.smally.at[i - 1], ss.sy.at[i - 1], rr.sy.at[i - 1], to)
     for i in (1, 3, 2):
         ym, to = ypeer(i)
         push(r.gnp.at[ym], r.ry.at[i - 1], ss.ry.at[i - 1], rr.ry.at[i - 1], to)
@@ -681,23 +731,13 @@
         summed = summed + r.wr[i].astype(f32)
     r.pieces[ex] = summed.astype(bf16)
     spread(r.pieces, "pa", "pb")
-    from_all(r.bs.at[ex], lambda source: r.bret.at[source], "bb")
-    rows = dot(slot_matrix(r.chosen[...]), r.bret[...].reshape(512, 256), 0, 0)
-    r.out[...] = (r.rescol[...] + rows).astype(bf16)
-    passed(r.wgf, "wb")
-    for k in range(32):
-        r.wout_out[16 * (k // 2):16 * (k // 2) + 16, 512 * (k % 2):512 * (k % 2) + 512] = r.wgf[k]
     grad = r.gnp[mp].astype(f32)
     for i in range(3):
         arrive(r.ry.at[i], rr.ry.at[i])
         grad = grad + r.ry[i].astype(f32)
     here = pl.ds(pl.multiple_of(64 * mp, 64), 64)
     unit, inverse = norm_parts(r.tokens[here, :].astype(f32))
-    grad_in, one_gain = norm_back(grad, r.gain1[...], unit, inverse)
-    r.small[...] = one_gain
-    for i in (1, 3, 2):
-        ym, to = ypeer(i)
-        push(r.small, r.smally.at[i - 1], ss.sy.at[i - 1], rr.sy.at[i - 1], to)
+    grad_in, _ = norm_back(grad, r.gain1[...], unit, inverse)
     r.igrad[here, :] = (r.gres[here, :] + grad_in).astype(bf16)
     for i in (1, 3, 2):
         ym, to = ypeer(i)
@@ -708,6 +748,17 @@
     r.smalle[ex, 0:1] = one_gain
     r.smalle[ex, 1:2] = r.ggrad[...]
     to_all(lambda to: r.smalle.at[ex], r.smalle.at[ex], "se")
+    from_all(r.bs.at[ex], lambda source: r.bret.at[source], "bb")
+    rows = dot(slot_matrix(r.chosen[...]), r.bret[...].reshape(512, 256), 0, 0)
+    r.out[...] = (r.rescol[...] + rows).astype(bf16)
+    for i in range(1, 4):
+        zp, _ = zpeer(4 - i)
+        arrive(r.wgf.at[c, zp], rr.wb.at[i - 1])
+    push(r.wgf.at[c], r.wgf.at[c], ss.wc.at[0], rr.wc.at[0], sib)
+    arrive(r.wgf.at[1 - c], rr.wc.at[0])
+    for k in range(16):
+        for core in range(2):
+            r.wout_out[16 * k:16 * k + 16, 512 * core:512 * core + 512] = r.wgf[core, k // 4, k % 4]
     pass_on(r.pieces, "pa", "pb")
     passed(r.pieces, "pb")
     for k in range(3):
@@ -715,7 +766,9 @@
             block = jnp.concatenate([r.pieces[8 * h + row, 64 * k:64 * k + 64] for h in range(4)], axis=0)
             r.qkv_out[k, 128 * row:128 * row + 128] = transposed(block)
     from_all(r.smalle.at[ex], lambda source: r.smalle.at[source], "se")
-    r.gains[...] = jnp.sum(r.smalle[...], axis=0)
+    both = jnp.sum(r.smalle[...], axis=0)
+    r.gain1_out[...] = both[0:1]
+    r.gain2_out[...] = both[1:2]
     for i in range(1, 4):
         ym, _ = ypeer(4 - i)
         there = pl.ds(pl.multiple_of(64 * ym, 64), 64)
@@ -730,8 +783,8 @@
         left(r.sb.at[p], ss.sb.at[p])
     for p in range(3):
         left(r.xs.at[p], ss.xs.at[p])
-    for k in range(15):
-        left(r.wgq.at[0], ss.wq.at[k])
+        left(r.wgx.at[0], ss.wx.at[p])
+        left(r.wgf.at[c, z, x], ss.wa.at[p])
     for copy in stores:
         copy.wait()
 
@@ -751,51 +804,68 @@
     )(*args)
 
 
-def finish_kernel(x, gpre, hid, cots, qkv, wout, out, igrad, in_grad, out_grad, qkv_o, wout_o, out_o, igrad_o):
-    in_grad[0] = dot(x[0], gpre[0], 0, 0)
-    out_grad[0] = dot(hid[0], cots[0], 0, 0)
-    qkv_o[...] = qkv[...].astype(f32)
-    wout_o[...] = wout[...].astype(f32)
-    out_o[...] = out[...]
-    igrad_o[...] = igrad[...]
-
-
-def finish(x, gpre, hid, cots, qkv, wout, out, igrad):
-    width, steps = 256, 4
-    n = 2 * steps
-    tall = pl.BlockSpec((1, 256, width), lambda e, i: (e, 0, i))
-    whole = pl.BlockSpec((1, 256, 1024), lambda e, i: (e, 0, 0))
-    made = pl.BlockSpec((1, width, 1024), lambda e, i: (e, i, 0))
-
-    def rows(shape):
-        if len(shape) == 3:
-            return pl.BlockSpec((shape[0], shape[1] // n, shape[2]), lambda e, i: (0, e * steps + i, 0))
-        return pl.BlockSpec((shape[0] // n, shape[1]), lambda e, i: (e * steps + i, 0))
-
-    plain = [rows(v.shape) for v in (qkv, wout, out, igrad)]
-    big = jax.ShapeDtypeStruct((2, 1024, 1024), f32)
+def finish_kernel(*refs):
+    held = 10
+    sources, results = refs[:held], refs[held:held + 8]
+    x, gpre, hid, cots, qkv, wout, out, igrad, gain1, gain2 = refs[held + 8:2 * held + 8]
+    in_buf, out_buf, qkv_buf, wout_buf, load, store, rest = refs[2 * held + 8:]
+    in_grad, out_grad, qkv_o, wout_o, out_o, igrad_o, gain1_o, gain2_o = results
+    buffers = (x, gpre, hid, cots, qkv, wout, out, igrad, gain1, gain2)
+    loads = [pltpu.make_async_copy(a, b, load.at[i]) for i, (a, b) in enumerate(zip(sources, buffers, strict=True))]
+    for copy in loads:
+        copy.start()
+    stores = []
+
+    def put(src, dst, sem):
+        copy = pltpu.make_async_copy(src, dst, sem)
+        copy.start()
+        stores.append(copy)
+
+    for k, (left, right, buf, result) in enumerate(((x, gpre, in_buf, in_grad), (hid, cots, out_buf, out_grad))):
+        loads[2 * k].wait()
+        loads[2 * k + 1].wait()
+        for e in range(2):
+            for t in range(4):
+                rows = pl.ds(256 * t, 256)
+                buf[e, rows, :] = dot(left[e, :, 256 * t:256 * t + 256], right[e], 0, 0)
+                put(buf.at[e, rows, :], result.at[e, rows, :], store.at[8 * k + 4 * e + t])
+    for copy in loads[4:]:
+        copy.wait()
+    qkv_buf[...] = qkv[...].astype(f32)
+    wout_buf[...] = wout[...].astype(f32)
+    plain = ((qkv_buf, qkv_o), (wout_buf, wout_o), (out, out_o), (igrad, igrad_o), (gain1, gain1_o), (gain2, gain2_o))
+    for k, (src, dst) in enumerate(plain):
+        put(src, dst, rest.at[k])
+    for copy in stores:
+        copy.wait()
+
+
+def finish(*args):
+    big = ((2, 1024, 1024), f32)
+    outs = [big, big, ((3, 1024, 256), f32), ((256, 1024), f32), ((256, 256), bf16), ((256, 1024), bf16)]
+    outs += [((1, 1024), f32)] * 2
     return pl.pallas_call(
         finish_kernel,
-        grid=(2, steps),
-        out_shape=[
-            big, big, jax.ShapeDtypeStruct(qkv.shape, f32), jax.ShapeDtypeStruct(wout.shape, f32),
-            jax.ShapeDtypeStruct(out.shape, bf16), jax.ShapeDtypeStruct(igrad.shape, bf16)],
-        in_specs=[tall, whole, tall, whole] + plain,
-        out_specs=[made, made] + plain,
+        out_shape=[jax.ShapeDtypeStruct(s, t) for s, t in outs],
+        in_specs=[ANY] * 10,
+        out_specs=[ANY] * 8,
+        scratch_shapes=[pltpu.VMEM(v.shape, v.dtype) for v in args]
+        + [pltpu.VMEM(s, t) for s, t in outs[:4]] + [DMA((10,)), DMA((16,)), DMA((6,))],
         name="finish",
-        compiler_params=pltpu.CompilerParams(vmem_limit_bytes=48 << 20),
+        compiler_params=pltpu.CompilerParams(vmem_limit_bytes=62 << 20),
         cost_estimate=pl.CostEstimate(flops=2 * 2 * 2 * 256 * 1024 * 1024, bytes_accessed=28 << 20, transcendentals=0),
-    )(x, gpre, hid, cots, qkv, wout, out, igrad)
+    )(*args)
 
 
 def on_device(
     tokens, hash_ids, lengths, norm1_gain, qkv_weight, out_weight, norm2_gain, expert_in, expert_out, cotangent,
 ):
-    x, cots, hid, gpre, out, igrad, gains, qkv, wout = layer(
+    x, cots, hid, gpre, out, igrad, gain1, gain2, qkv, wout = layer(
         lengths, tokens, norm1_gain.reshape(1, 1024), norm2_gain.reshape(1, 1024), hash_ids.reshape(1, 256),
         jnp.transpose(qkv_weight, (1, 0, 2)), out_weight, cotangent, expert_in, expert_out)
-    in_grad, out_grad, qkv, wout, out, igrad = finish(x, gpre, hid, cots, qkv, wout, out, igrad)
-    return out, igrad, gains[0], jnp.transpose(qkv, (1, 0, 2)), wout, gains[1], in_grad, out_grad
+    in_grad, out_grad, qkv, wout, out, igrad, gain1, gain2 = finish(
+        x, gpre, hid, cots, qkv, wout, out, igrad, gain1, gain2)
+    return out, igrad, gain1.reshape(1024), jnp.transpose(qkv, (1, 0, 2)), wout, gain2.reshape(1024), in_grad, out_grad
 
 
 def solution(mesh):

time: 177 us -> 154 us (0.87)
  Pallas kernels: 166 us -> 153 us
  local copies, waits for them, and re-layouts: 9.26 us -> 0 us
    pallas_call x1, Pallas kernels: 156 us -> 143 us  [layer(): pl.pallas_call(layer_kernel, out_shape=[jax.ShapeDtypeStruct(s, t) for s,...]
    unnamed x14 -> x0, local copies, waits for them, and re-layouts: 7.88 us -> none
where the time goes in v3:
time: 154 us
  Pallas kernels  153 us (99%)
    pallas_call x1, Pallas kernels, layer(): pl.pallas_call(layer_kernel, out_shape=[jax.ShapeDtypeStruct(s, t) for s,...  143 us
    pallas_call x1, Pallas kernels, finish(): pl.pallas_call(finish_kernel, out_shape=[jax.ShapeDtypeStruct(s, t) for s...  9.42 us

profile of v3, /device:TPU:1, one launch (start us, length us, event | category | flops | bytes accessed | tf_op | source)
XLA Modules:
  0.0 153.5 jit_solution(3606974829307791657)
XLA Ops:
  0.6 143.3 %layer.1 = (bf16[2,256,1024]{2,1,0:T(8,128)(2,1)}, bf16[2,256,1024]{2,1,0:T(8,128)(2,1)}, bf16[2,256,1024]{2,1,0:T(8,128)(2,1)}, bf16[2,256,1024]{2,1,0:T(8,128)...) custom-call(s32[9]{0:T(128)} %refs_0_.1, ...), custom_call_target="tpu_custom_call" | custom-call | tf_op jit(solution)/shard_map/layer/pallas_call | solution.py:794
  143.9 9.4 %finish.1 = (f32[2,1024,1024]{2,1,0:T(8,128)}, f32[2,1024,1024]{2,1,0:T(8,128)}, f32[3,1024,256]{2,1,0:T(8,128)}, f32[256,1024]{1,0:T(8,128)}, bf16[256,256]{1,0...) custom-call(bf16[2,256,1024]{2,1,0:T(8,128)(2,1)} %get-tuple-element.26.refs_0_, ...), custom_call_target="tpu_custom_call" | custom-call | flops 2147483648 | bytes 29360128 | tf_op jit(solution)/shard_map/finish/pallas_call | solution.py:847

commit v4 on v3

--- a/solution.py
+++ b/solution.py
@@ -13,7 +13,7 @@
 MESH = pl.DeviceIdType.MESH
 bf16, f32 = jnp.bfloat16, jnp.float32
 EX, MP = 32, 4
-VMEM_BYTES = 60 << 20
+VMEM_BYTES = 54 << 20
 
 
 def dot(a, b, ca=1, cb=0):
@@ -126,7 +126,7 @@
 
 ARGS = ["lengths", "tokens", "gain1", "gain2", "chosen", "wqkv_hbm", "wout_hbm", "cot_hbm", "win_hbm", "wex_hbm"]
 OUTS = {
-    "x_hbm": (ROWS, bf16), "c_hbm": (ROWS, bf16), "hid_hbm": (ROWS, bf16), "gpre_hbm": (ROWS, bf16),
+    "xrows": (ROWS, bf16), "crows": (ROWS, bf16), "hid": (ROWS, bf16), "gpre": (ROWS, bf16),
     "out": ((256, 256), bf16), "igrad": ((256, 1024), bf16), "gain1_out": ((1, 1024), f32), "gain2_out": ((1, 1024), f32),
     "qkv_out": ((3, 1024, 256), bf16), "wout_out": ((256, 1024), bf16),
 }
@@ -140,9 +140,10 @@
     "ot": ((4, 64, 256), f32), "lse": ((4, 1, 256), f32), "o_s": ((4, 64, 256), bf16),
     "att": ((4, 4, 64, 256), bf16), "cotq_s": ((32, 16, 256), bf16), "cotq": ((4, 32, 16, 256), bf16),
     "outgoing": ((32, 16, 1024), bf16), "arrived": ((32, 16, 1024), bf16),
-    "xrows": (ROWS, bf16), "crows": (ROWS, bf16), "hid": (ROWS, bf16), "gpre": (ROWS, bf16), "gh": (ROWS, f32),
-    "part": ((2, 4, 256, 256), bf16), "rs": ((2, 3, 256, 256), bf16), "back_s": ((32, 16, 256), bf16),
-    "back": ((32, 16, 256), bf16), "gn": ((4, 256, 256), bf16), "resid": ((256, 1024), f32),
+    "gh": (ROWS, f32),
+    "part": ((2, 4, 256, 128), bf16), "rs": ((2, 3, 256, 128), bf16), "back_s": ((32, 16, 128), bf16),
+    "back": ((32, 16, 128), bf16), "wide_s": ((32, 16, 512), bf16), "wide": ((32, 16, 512), bf16),
+    "gb": ((4, 256, 128), bf16), "gbr": ((3, 256, 128), bf16), "gn": ((2, 4, 256, 128), bf16), "resid": ((256, 1024), f32),
     "rescol": ((256, 256), f32), "gres": ((256, 1024), f32), "branch": ((32, 16, 1024), bf16),
     "wgp": ((2, 4, 4, 16, 512), bf16), "wgs": ((4, 4, 16, 512), bf16), "wgq": ((4, 4, 16, 512), bf16),
     "wgz": ((3, 4, 16, 512), bf16), "wgx": ((4, 16, 512), bf16), "wgr": ((3, 16, 512), bf16),
@@ -153,15 +154,16 @@
     "kt": ((64, 1024), bf16), "dkv": ((1024, 128), f32), "dq": ((4, 64, 256), f32),
     "sb": ((4, 1024, 128), bf16), "sr": ((4, 1024, 128), bf16), "xs": ((4, 1024, 128), bf16),
     "xr": ((3, 1024, 128), bf16), "zs": ((4, 192, 256), bf16), "zr": ((4, 192, 256), bf16),
-    "wp": ((8, 192, 128), bf16), "wr": ((7, 192, 128), bf16), "pieces": ((32, 192, 128), bf16),
+    "wpq": ((8, 64, 128), bf16), "wrq": ((7, 64, 128), bf16), "pieceq": ((32, 64, 128), bf16),
+    "wpk": ((8, 128, 128), bf16), "wrk": ((7, 128, 128), bf16), "piecek": ((32, 128, 128), bf16),
     "gnp": ((4, 64, 1024), bf16), "ry": ((3, 64, 1024), bf16), "small": ((1, 1024), f32),
     "smally": ((3, 1, 1024), f32), "smalle": ((32, 2, 1024), f32), "ggrad": ((1, 1024), f32),
 }
-LOCAL = {"load": (5,), "store": (4,)}
+LOCAL = {"load": (5,)}
 SENT = {
     "az": (6,), "ag": (28,), "wf": (3,), "wd": (3,), "co": (31,), "cy": (3,), "na": (3,), "oz": (3,), "oy": (3,),
-    "di": (31,), "rs": (6,), "ba": (31,), "gy": (3,), "dz": (3,), "br": (3,), "bb": (31,), "sb": (4,), "xs": (3,),
-    "wg": (1,), "wz": (3,), "wx": (3,), "wa": (3,), "wb": (3,), "wc": (1,), "zq": (6,), "wp": (7,), "pa": (15,), "pb": (16,),
+    "di": (31,), "rs": (6,), "ba": (31,), "bc": (31,), "gb": (3,), "gy": (6,), "dz": (3,), "br": (3,), "bb": (31,), "sb": (4,), "xs": (3,),
+    "wg": (1,), "wz": (3,), "wx": (3,), "wa": (3,), "wb": (3,), "wc": (1,), "zq": (6,), "wp": (7,), "wk": (7,), "pa": (15,), "pb": (16,), "pc": (15,), "pd": (16,),
     "ry": (3,), "ay": (3,), "sy": (3,), "se": (31,),
 }
 TAKEN = dict(SENT, ag=(32,))
@@ -484,25 +486,34 @@
         r.gh[le] = dot(rows, r.wex[le], 1, 1)
     loads[4].wait()
     from_all(r.outgoing.at[ex], lambda source: r.arrived.at[source], "di")
-    for le in range(2):
+    def expert_rows(le):
         rows = one_expert(r.arrived[...], le)
         r.xrows[le] = rows
-        hidden, slope = gelu_parts(dot(rows, r.win[le]))
+        return dot(rows, r.win[le])
+
+    def activate(le, pre):
+        hidden, slope = gelu_parts(pre)
         r.hid[le] = hidden.astype(bf16)
         gpre = (r.gh[le] * slope).astype(bf16)
         r.gpre[le] = gpre
+        return gpre
+
+    def give_back(le, gpre):
         for k in range(4):
-            r.part[le, k] = dot(gpre, r.win[le, 256 * k:256 * k + 256, :], 1, 1).astype(bf16)
+            product = dot(gpre, r.win[le, 256 * k:256 * k + 256, :], 1, 1)
+            r.part[le, k] = product[:, 0:128].astype(bf16)
+            r.gh[le, :, 128 * k:128 * k + 128] = product[:, 128:256]
         for i in (1, 3, 2):
             ym, to = ypeer(i)
             push(r.part.at[le, ym], r.rs.at[le, i - 1], ss.rs.at[3 * le + i - 1], rr.rs.at[3 * le + i - 1], to)
-    stores = [
-        pltpu.make_async_copy(src, dst, ls.store.at[i])
-        for i, (src, dst) in enumerate([
-            (r.xrows, r.x_hbm), (r.crows, r.c_hbm), (r.hid, r.hid_hbm), (r.gpre, r.gpre_hbm)])
-    ]
-    for copy in stores:
-        copy.start()
+
+    first, second = expert_rows(0), expert_rows(1)
+    gpre = activate(0, first)
+    give_back(0, gpre)
+    give_back(1, activate(1, second))
+    r.wide_s[...] = both_experts(r.gh[0, :, 0:512], r.gh[1, :, 0:512])
+    to_all(lambda to: r.wide_s.at[to], r.wide.at[ex], "bc")
+    r.wide[ex] = r.wide_s[ex]
     first = dot(r.hid[0], r.wex[0])
     r.branch[...] = both_experts(first, dot(r.hid[1], r.wex[1]))
     sums = []
@@ -515,16 +526,33 @@
     r.back_s[...] = both_experts(sums[0], sums[1])
     to_all(lambda to: r.back_s.at[to], r.back.at[ex], "ba")
     r.back[ex] = r.back_s[ex]
+    placer = slot_matrix(r.chosen[...])
+    from_all(r.wide_s.at[ex], lambda source: r.wide.at[source], "bc")
+    rows = dot(placer, r.wide[...].reshape(512, 512), 0, 0).astype(bf16)
+    for k in range(4):
+        r.gb[k] = rows[:, 128 * k:128 * k + 128]
+    for i in (1, 3, 2):
+        ym, to = ypeer(i)
+        push(r.gb.at[ym], r.gbr.at[i - 1], ss.gb.at[i - 1], rr.gb.at[i - 1], to)
     from_all(r.back_s.at[ex], lambda source: r.back.at[source], "ba")
-    r.gn[mp] = dot(slot_matrix(r.chosen[...]), r.back[...].reshape(512, 256), 0, 0).astype(bf16)
+    r.gn[0, mp] = dot(placer, r.back[...].reshape(512, 128), 0, 0).astype(bf16)
     for i in (1, 3, 2):
         ym, to = ypeer(i)
-        push(r.gn.at[mp], r.gn.at[mp], ss.gy.at[i - 1], rr.gy.at[i - 1], to)
+        push(r.gn.at[0, mp], r.gn.at[0, mp], ss.gy.at[i - 1], rr.gy.at[i - 1], to)
+    total = r.gb[mp].astype(f32)
+    for i in range(3):
+        arrive(r.gbr.at[i], rr.gb.at[i])
+        total = total + r.gbr[i].astype(f32)
+    r.gn[1, mp] = total.astype(bf16)
+    for i in (1, 3, 2):
+        ym, to = ypeer(i)
+        push(r.gn.at[1, mp], r.gn.at[1, mp], ss.gy.at[i + 2], rr.gy.at[i + 2], to)
     unit, inverse = norm_parts(r.resid[...])
     for i in range(1, 4):
         ym, _ = ypeer(4 - i)
-        arrive(r.gn.at[ym], rr.gy.at[i - 1])
-    grad = jnp.concatenate([r.gn[k] for k in range(4)], axis=1).astype(f32)
+        arrive(r.gn.at[0, ym], rr.gy.at[i - 1])
+        arrive(r.gn.at[1, ym], rr.gy.at[i + 2])
+    grad = jnp.concatenate([r.gn[k % 2, k // 2] for k in range(8)], axis=1).astype(f32)
     grad_in, ggrad = norm_back(grad, r.gain2[...], unit, inverse)
     r.ggrad[...] = ggrad
     gres = r.cot[...].astype(f32) + grad_in
@@ -633,7 +661,7 @@
                 r.xs[3] = (r.xs[1 + c].astype(f32) + r.xr[0].astype(f32)).astype(bf16)
                 remote(r.xs.at[3], r.xr.at[2], ss.xs.at[2], rr.xs.at[2], ahead).start()
 
-        @pl.when(i == 1)
+        @pl.when(i == 3)
         def _():
             for k in range(3):
                 arrive(r.wgz.at[k], rr.wz.at[k])
@@ -652,8 +680,6 @@
                 arrive(r.brs.at[k], rr.br.at[k])
                 total = total + r.brs[k].astype(f32)
             r.bs[...] = total.astype(bf16)
-            to_all(lambda to: r.bs.at[to], r.bret.at[ex], "bb")
-            r.bret[ex] = r.bs[ex]
 
         @pl.when(i == 6)
         def _():
@@ -676,6 +702,33 @@
     for i in (1, 3, 2):
         zp, to = zpeer(i)
         push(r.zs.at[zp, 0:64], r.zr.at[z, 0:64], ss.zq.at[i + 2], rr.zq.at[i + 2], to)
+    to_all(lambda to: r.bs.at[to], r.bret.at[ex], "bb")
+    r.bret[ex] = r.bs[ex]
+    for i in range(1, 4):
+        zp, _ = zpeer(4 - i)
+        arrive(r.nall.at[zp], rr.na.at[i - 1])
+
+    def weight_part(first, last, pieces, name):
+        wt = dot(r.zs[0, first:last], r.nall[0])
+        for b in range(1, 4):
+            wt = wt + dot(r.zs[b, first:last], r.nall[b])
+        wt = wt.astype(bf16)
+        for k in range(8):
+            pieces[0][k] = wt[:, 128 * k:128 * k + 128]
+        for i in range(1, 8):
+            jt = lax.rem(j + i, 8)
+            push(
+                pieces[0].at[jt], pieces[1].at[i - 1], getattr(ss, name).at[i - 1], getattr(rr, name).at[i - 1],
+                (z * 8 + jt, mp))
+
+    def weight_sum(pieces, name):
+        summed = pieces[0][j].astype(f32)
+        for i in range(7):
+            arrive(pieces[1].at[i], getattr(rr, name).at[i])
+            summed = summed + pieces[1][i].astype(f32)
+        pieces[2][ex] = summed.astype(bf16)
+
+    weight_part(0, 64, (r.wpq, r.wrq), "wp")
     r.resid[...] = norm_parts(r.tokens[...].astype(f32))[0]
     arrive(r.sr.at[3], rr.sb.at[3])
     total = r.dkv[...] + r.sr[3].astype(f32)
@@ -689,33 +742,25 @@
         zp, to = zpeer(i)
         push(r.zs.at[zp, 64:192], r.zr.at[z, 64:192], ss.zq.at[i - 1], rr.zq.at[i - 1], to)
     r.zr[z] = r.zs[z]
-    for i in range(1, 4):
-        zp, _ = zpeer(4 - i)
-        arrive(r.nall.at[zp], rr.na.at[i - 1])
-    wt = dot(r.zs[0], r.nall[0])
-    for b in range(1, 4):
-        wt = wt + dot(r.zs[b], r.nall[b])
-    wt = wt.astype(bf16)
-    for k in range(8):
-        r.wp[k] = wt[:, 128 * k:128 * k + 128]
-    for i in range(1, 8):
-        jt = lax.rem(j + i, 8)
-        push(r.wp.at[jt], r.wr.at[i - 1], ss.wp.at[i - 1], rr.wp.at[i - 1], (z * 8 + jt, mp))
+    weight_part(64, 192, (r.wpk, r.wrk), "wk")
     for i in range(1, 4):
         xq, _ = xpeer(4 - i)
         arrive(r.wgf.at[c, z, xq], rr.wa.at[i - 1])
     for i in (1, 3, 2):
         _, to = zpeer(i)
         push(r.wgf.at[c, z], r.wgf.at[c, z], ss.wb.at[i - 1], rr.wb.at[i - 1], to)
+
+    def heads(first):
+        return transposed(jnp.concatenate([r.zr[h, first:first + 64] for h in range(4)], axis=0))
+
     for i in range(1, 4):
         zp, _ = zpeer(4 - i)
         arrive(r.zr.at[zp, 0:64], rr.zq.at[i + 2])
+    part = dot(heads(0), r.wqkv[0], 1, 1)
+    for i in range(1, 4):
+        zp, _ = zpeer(4 - i)
         arrive(r.zr.at[zp, 64:192], rr.zq.at[i - 1])
-    part = None
-    for k in range(3):
-        heads = transposed(jnp.concatenate([r.zr[h, 64 * k:64 * k + 64] for h in range(4)], axis=0))
-        term = dot(heads, r.wqkv[k], 1, 1)
-        part = term if part is None else part + term
+    part = part + dot(heads(64), r.wqkv[1], 1, 1) + dot(heads(128), r.wqkv[2], 1, 1)
     r.gnp[...] = part.astype(bf16).reshape(4, 64, 1024)
     one_gain = jnp.sum(part * r.resid[...], axis=0, keepdims=True)
     r.small[...] = one_gain
@@ -725,12 +770,10 @@
     for i in (1, 3, 2):
         ym, to = ypeer(i)
         push(r.gnp.at[ym], r.ry.at[i - 1], ss.ry.at[i - 1], rr.ry.at[i - 1], to)
-    summed = r.wp[j].astype(f32)
-    for i in range(7):
-        arrive(r.wr.at[i], rr.wp.at[i])
-        summed = summed + r.wr[i].astype(f32)
-    r.pieces[ex] = summed.astype(bf16)
-    spread(r.pieces, "pa", "pb")
+    weight_sum((r.wpq, r.wrq, r.pieceq), "wp")
+    spread(r.pieceq, "pa", "pb")
+    weight_sum((r.wpk, r.wrk, r.piecek), "wk")
+    spread(r.piecek, "pc", "pd")
     grad = r.gnp[mp].astype(f32)
     for i in range(3):
         arrive(r.ry.at[i], rr.ry.at[i])
@@ -759,11 +802,14 @@
     for k in range(16):
         for core in range(2):
             r.wout_out[16 * k:16 * k + 16, 512 * core:512 * core + 512] = r.wgf[core, k // 4, k % 4]
-    pass_on(r.pieces, "pa", "pb")
-    passed(r.pieces, "pb")
+    pass_on(r.pieceq, "pa", "pb")
+    pass_on(r.piecek, "pc", "pd")
+    passed(r.pieceq, "pb")
+    passed(r.piecek, "pd")
     for k in range(3):
+        source, first = (r.pieceq, 0) if k == 0 else (r.piecek, 64 * k - 64)
         for row in range(8):
-            block = jnp.concatenate([r.pieces[8 * h + row, 64 * k:64 * k + 64] for h in range(4)], axis=0)
+            block = jnp.concatenate([source[8 * h + row, first:first + 64] for h in range(4)], axis=0)
             r.qkv_out[k, 128 * row:128 * row + 128] = transposed(block)
     from_all(r.smalle.at[ex], lambda source: r.smalle.at[source], "se")
     both = jnp.sum(r.smalle[...], axis=0)
@@ -785,17 +831,14 @@
         left(r.xs.at[p], ss.xs.at[p])
         left(r.wgx.at[0], ss.wx.at[p])
         left(r.wgf.at[c, z, x], ss.wa.at[p])
-    for copy in stores:
-        copy.wait()
 
 
 def layer(*args):
-    spaces = {"x_hbm": ANY, "c_hbm": ANY, "hid_hbm": ANY, "gpre_hbm": ANY}
     return pl.pallas_call(
         layer_kernel,
-        out_shape=[jax.ShapeDtypeStruct(s, t) for s, t in OUTS.values()],
+        out_shape=[pltpu.VMEM(s, t) for s, t in OUTS.values()],
         in_specs=[SM, VM, VM, VM, VM, ANY, ANY, ANY, ANY, ANY],
-        out_specs=[spaces.get(name, VM) for name in OUTS],
+        out_specs=[VM] * len(OUTS),
         scratch_shapes=[pltpu.VMEM(s, t) for s, t in BUFFERS.values()]
         + [DMA(s) for group in (LOCAL, SENT, TAKEN) for s in group.values()],
         name="layer",
@@ -804,16 +847,9 @@
     )(*args)
 
 
-def finish_kernel(*refs):
-    held = 10
-    sources, results = refs[:held], refs[held:held + 8]
-    x, gpre, hid, cots, qkv, wout, out, igrad, gain1, gain2 = refs[held + 8:2 * held + 8]
-    in_buf, out_buf, qkv_buf, wout_buf, load, store, rest = refs[2 * held + 8:]
-    in_grad, out_grad, qkv_o, wout_o, out_o, igrad_o, gain1_o, gain2_o = results
-    buffers = (x, gpre, hid, cots, qkv, wout, out, igrad, gain1, gain2)
-    loads = [pltpu.make_async_copy(a, b, load.at[i]) for i, (a, b) in enumerate(zip(sources, buffers, strict=True))]
-    for copy in loads:
-        copy.start()
+def finish_kernel(x, gpre, hid, cots, qkv, wout, out, igrad, gain1, gain2, *refs):
+    in_grad, out_grad, qkv_o, wout_o, out_o, igrad_o, gain1_o, gain2_o = refs[:8]
+    in_buf, out_buf, qkv_buf, wout_buf, store, rest = refs[8:]
     stores = []
 
     def put(src, dst, sem):
@@ -822,15 +858,11 @@
         stores.append(copy)
 
     for k, (left, right, buf, result) in enumerate(((x, gpre, in_buf, in_grad), (hid, cots, out_buf, out_grad))):
-        loads[2 * k].wait()
-        loads[2 * k + 1].wait()
         for e in range(2):
             for t in range(4):
                 rows = pl.ds(256 * t, 256)
                 buf[e, rows, :] = dot(left[e, :, 256 * t:256 * t + 256], right[e], 0, 0)
                 put(buf.at[e, rows, :], result.at[e, rows, :], store.at[8 * k + 4 * e + t])
-    for copy in loads[4:]:
-        copy.wait()
     qkv_buf[...] = qkv[...].astype(f32)
     wout_buf[...] = wout[...].astype(f32)
     plain = ((qkv_buf, qkv_o), (wout_buf, wout_o), (out, out_o), (igrad, igrad_o), (gain1, gain1_o), (gain2, gain2_o))
@@ -847,12 +879,11 @@
     return pl.pallas_call(
         finish_kernel,
         out_shape=[jax.ShapeDtypeStruct(s, t) for s, t in outs],
-        in_specs=[ANY] * 10,
+        in_specs=[VM] * 10,
         out_specs=[ANY] * 8,
-        scratch_shapes=[pltpu.VMEM(v.shape, v.dtype) for v in args]
-        + [pltpu.VMEM(s, t) for s, t in outs[:4]] + [DMA((10,)), DMA((16,)), DMA((6,))],
+        scratch_shapes=[pltpu.VMEM(s, t) for s, t in outs[:4]] + [DMA((16,)), DMA((6,))],
         name="finish",
-        compiler_params=pltpu.CompilerParams(vmem_limit_bytes=62 << 20),
+        compiler_params=pltpu.CompilerParams(vmem_limit_bytes=36 << 20),
         cost_estimate=pl.CostEstimate(flops=2 * 2 * 2 * 256 * 1024 * 1024, bytes_accessed=28 << 20, transcendentals=0),
     )(*args)
 

time: 154 us -> 142 us (0.922)
  Pallas kernels: 153 us -> 141 us
    pallas_call x1, Pallas kernels: 143 us -> 133 us  [layer(): pl.pallas_call(layer_kernel, out_shape=[pltpu.VMEM(s, t) for s, t in OUTS...]
    pallas_call x1, Pallas kernels: 9.42 us -> 7.8 us  [finish(): pl.pallas_call(finish_kernel, out_shape=[jax.ShapeDtypeStruct(s, t) for s...]
where the time goes in v4:
time: 142 us
  Pallas kernels  141 us (99%)
    pallas_call x1, Pallas kernels, layer(): pl.pallas_call(layer_kernel, out_shape=[pltpu.VMEM(s, t) for s, t in OUTS...  133 us
    pallas_call x1, Pallas kernels, finish(): pl.pallas_call(finish_kernel, out_shape=[jax.ShapeDtypeStruct(s, t) for s...  7.8 us

profile of v4, /device:TPU:1, one launch (start us, length us, event | category | flops | bytes accessed | tf_op | source)
XLA Modules:
  0.0 142.1 jit_solution(1888550386526153075)
XLA Ops:
  0.6 133.4 %layer.1 = (bf16[2,256,1024]{2,1,0:T(8,128)(2,1)S(1)}, bf16[2,256,1024]{2,1,0:T(8,128)(2,1)S(1)}, bf16[2,256,1024]{2,1,0:T(8,128)(2,1)S(1)}, bf16[2,256,1024]{2,...) custom-call(s32[9]{0:T(128)} %refs_0_.1, ...), custom_call_target="tpu_custom_call" | custom-call | tf_op jit(solution)/shard_map/layer/pallas_call | solution.py:837
  134.1 7.8 %finish.1 = (f32[2,1024,1024]{2,1,0:T(8,128)}, f32[2,1024,1024]{2,1,0:T(8,128)}, f32[3,1024,256]{2,1,0:T(8,128)}, f32[256,1024]{1,0:T(8,128)}, bf16[256,256]{1,0...) custom-call(bf16[2,256,1024]{2,1,0:T(8,128)(2,1)S(1)} %get-tuple-element.26.x, ...), custom_call_target="tpu_custom_call" | custom-call | flops 2147483648 | bytes 29360128 | tf_op jit(solution)/shard_map/finish/pallas_call | solution.py:879

commit v5 on v4

--- a/solution.py
+++ b/solution.py
@@ -13,7 +13,7 @@
 MESH = pl.DeviceIdType.MESH
 bf16, f32 = jnp.bfloat16, jnp.float32
 EX, MP = 32, 4
-VMEM_BYTES = 54 << 20
+VMEM_BYTES = 56 << 20
 
 
 def dot(a, b, ca=1, cb=0):
@@ -131,8 +131,8 @@
     "qkv_out": ((3, 1024, 256), bf16), "wout_out": ((256, 1024), bf16),
 }
 BUFFERS = {
-    "wqkv": ((3, 1024, 256), bf16), "wout": ((256, 1024), bf16), "cot": ((256, 1024), bf16),
-    "win": ((2, 1024, 1024), bf16), "wex": ((2, 1024, 1024), bf16), "normed": ((256, 1024), bf16),
+    "wqkv": ((3, 1024, 256), bf16), "cot": ((256, 1024), bf16),
+    "weights": ((7, 1024, 1024), bf16), "placer": ((512, 256), bf16), "normed": ((256, 1024), bf16),
     "nall": ((4, 256, 1024), bf16), "wfull": ((4, 256, 1024), bf16),
     "q_s": ((4, 64, 256), bf16), "kv_s": ((4, 128, 256), bf16), "q": ((4, 64, 256), bf16),
     "kvt": ((8, 4, 128, 256), bf16), "qaug": ((4, 128, 256), bf16), "kaug": ((1024, 128), bf16),
@@ -154,17 +154,18 @@
     "kt": ((64, 1024), bf16), "dkv": ((1024, 128), f32), "dq": ((4, 64, 256), f32),
     "sb": ((4, 1024, 128), bf16), "sr": ((4, 1024, 128), bf16), "xs": ((4, 1024, 128), bf16),
     "xr": ((3, 1024, 128), bf16), "zs": ((4, 192, 256), bf16), "zr": ((4, 192, 256), bf16),
-    "wpq": ((8, 64, 128), bf16), "wrq": ((7, 64, 128), bf16), "pieceq": ((32, 64, 128), bf16),
-    "wpk": ((8, 128, 128), bf16), "wrk": ((7, 128, 128), bf16), "piecek": ((32, 128, 128), bf16),
+    "wpq": ((8, 64, 128), bf16), "wrq": ((7, 64, 128), bf16),
+    "wpk": ((8, 128, 128), bf16), "wrk": ((7, 128, 128), bf16),
+    "pieces": ((3, 2, 4, 4, 64, 128), bf16),
     "gnp": ((4, 64, 1024), bf16), "ry": ((3, 64, 1024), bf16), "small": ((1, 1024), f32),
-    "smally": ((3, 1, 1024), f32), "smalle": ((32, 2, 1024), f32), "ggrad": ((1, 1024), f32),
+    "smally": ((3, 1, 1024), f32), "smalle": ((32, 1, 1024), f32), "smallf": ((32, 1, 1024), f32),
 }
 LOCAL = {"load": (5,)}
 SENT = {
-    "az": (6,), "ag": (28,), "wf": (3,), "wd": (3,), "co": (31,), "cy": (3,), "na": (3,), "oz": (3,), "oy": (3,),
+    "az": (6,), "ag": (28,), "wf": (3,), "wd": (3,), "co": (31,), "cy": (3,), "na": (6,), "oz": (3,), "oy": (12,),
     "di": (31,), "rs": (6,), "ba": (31,), "bc": (31,), "gb": (3,), "gy": (6,), "dz": (3,), "br": (3,), "bb": (31,), "sb": (4,), "xs": (3,),
-    "wg": (1,), "wz": (3,), "wx": (3,), "wa": (3,), "wb": (3,), "wc": (1,), "zq": (6,), "wp": (7,), "wk": (7,), "pa": (15,), "pb": (16,), "pc": (15,), "pd": (16,),
-    "ry": (3,), "ay": (3,), "sy": (3,), "se": (31,),
+    "wg": (1,), "wz": (3,), "wx": (3,), "wa": (3,), "wb": (3,), "wc": (1,), "zq": (6,), "wp": (7,), "wk": (7,), "pa": (9,), "pb": (9,), "pc": (3,),
+    "ry": (3,), "ay": (3,), "sy": (3,), "se": (31,), "sf": (31,),
 }
 TAKEN = dict(SENT, ag=(32,))
 
@@ -230,39 +231,41 @@
 
         lax.fori_loop(1, EX, one, 0)
 
-    def spread(buf, far, near):
-        def one(k, carry):
-            to = lax.rem(chip + k, 16) * 2 + c
-            remote(buf.at[ex], buf.at[ex], getattr(ss, far).at[k - 1], getattr(rr, far).at[k - 1], (to, mp)).start()
-            return carry
-
-        lax.fori_loop(1, 16, one, 0)
-        remote(buf.at[ex], buf.at[ex], getattr(ss, near).at[0], getattr(rr, near).at[0], sib).start()
-
-    def pass_on(buf, far, near):
-        def one(k, carry):
-            source = lax.rem(chip + 16 - k, 16) * 2 + c
-            left(buf.at[ex], getattr(ss, far).at[k - 1])
-            arrive(buf.at[source], getattr(rr, far).at[k - 1])
-            remote(buf.at[source], buf.at[source], getattr(ss, near).at[k], getattr(rr, near).at[k], sib).start()
-            return carry
-
-        lax.fori_loop(1, 16, one, 0)
-
-    def passed(buf, near):
-        def one(k, carry):
-            source = lax.rem(chip + 16 - k, 16) * 2 + 1 - c
-            left(buf.at[ex], getattr(ss, near).at[k])
-            arrive(buf.at[source], getattr(rr, near).at[k])
-            return carry
-
-        lax.fori_loop(0, 16, one, 0)
+    def gather_first(part):
+        for i in (1, 3, 2):
+            _, to = xpeer(i) if part == 1 else zpeer(i)
+            own = r.pieces.at[part, c, z, x]
+            push(own, own, ss.pa.at[3 * part + i - 1], rr.pa.at[3 * part + i - 1], to)
+
+    def gather_second(part):
+        for i in range(1, 4):
+            if part == 1:
+                xq, _ = xpeer(4 - i)
+                arrive(r.pieces.at[part, c, z, xq], rr.pa.at[3 * part + i - 1])
+            else:
+                zp, _ = zpeer(4 - i)
+                arrive(r.pieces.at[part, c, zp, x], rr.pa.at[3 * part + i - 1])
+        row = r.pieces.at[part, c, z] if part == 1 else r.pieces.at[part, c, :, x]
+        for i in (1, 3, 2):
+            _, to = zpeer(i) if part == 1 else xpeer(i)
+            push(row, row, ss.pb.at[3 * part + i - 1], rr.pb.at[3 * part + i - 1], to)
+
+    def gather_third(part):
+        for i in range(1, 4):
+            if part == 1:
+                zp, _ = zpeer(4 - i)
+                arrive(r.pieces.at[part, c, zp], rr.pb.at[3 * part + i - 1])
+            else:
+                xq, _ = xpeer(4 - i)
+                arrive(r.pieces.at[part, c, :, xq], rr.pb.at[3 * part + i - 1])
+        push(r.pieces.at[part, c], r.pieces.at[part, c], ss.pc.at[part], rr.pc.at[part], sib)
 
     bar = greet(ex, mp)
     loads = [
         pltpu.make_async_copy(src, dst, ls.load.at[i])
         for i, (src, dst) in enumerate([
-            (r.wqkv_hbm, r.wqkv), (r.wout_hbm, r.wout), (r.cot_hbm, r.cot), (r.wex_hbm, r.wex), (r.win_hbm, r.win)])
+            (r.wqkv_hbm, r.wqkv), (r.wout_hbm, r.wfull.at[mp]), (r.cot_hbm, r.cot), (r.wex_hbm, r.weights.at[2:4]),
+            (r.win_hbm, r.weights.at[0:2])])
     ]
     for copy in loads:
         copy.start()
@@ -314,14 +317,14 @@
     half = pl.ds(pl.multiple_of(128 * c, 128), 128)
     for i in range(1, 4):
         ym, to = ypeer(i)
-        push(r.wout.at[half, :], r.wfull.at[mp, half, :], ss.wf.at[i - 1], rr.wf.at[i - 1], to)
-    r.wfull[mp] = r.wout[...]
+        push(r.wfull.at[mp, half, :], r.wfull.at[mp, half, :], ss.wf.at[i - 1], rr.wf.at[i - 1], to)
     r.vt1[64:80, :] = jnp.ones((16, 1024), bf16)
     ends = doc_ends(r.lengths)
     feature = lax.broadcasted_iota(jnp.int32, (64, 256), 0)
     loads[2].wait()
     mine = pl.ds(pl.multiple_of(256 * mp, 256), 256)
-    r.cotq_s[...] = dot(slot_matrix(r.chosen[...]), r.cot[:, mine]).astype(bf16).reshape(EX, 16, 256)
+    r.placer[...] = slot_matrix(r.chosen[...])
+    r.cotq_s[...] = dot(r.placer[...], r.cot[:, mine]).astype(bf16).reshape(EX, 16, 256)
     r.cotq[mp, ex] = r.cotq_s[ex]
     arrive(r.kvt.at[0, lax.rem(z + 3, 4)], rr.az.at[0])
     own_piece(1)
@@ -448,23 +451,66 @@
         zp, to = zpeer(i)
         push(r.o_s.at[zp], r.att.at[mp, z], ss.oz.at[i - 1], rr.oz.at[i - 1], to)
     r.att[mp, z] = r.o_s[z]
-    for i in range(1, 4):
-        zp, _ = zpeer(4 - i)
-        arrive(r.att.at[mp, zp], rr.oz.at[i - 1])
-    for i in (1, 3, 2):
-        ym, to = ypeer(i)
-        push(r.att.at[mp], r.att.at[mp], ss.oy.at[i - 1], rr.oy.at[i - 1], to)
+    def normed_half(part):
+        rows = pl.ds(128 * part, 128)
+        for i in (1, 3):
+            zp, to = zpeer(i)
+            push(
+                r.normed.at[rows, :], r.nall.at[z, rows, :], ss.na.at[i - 1 + 3 * part],
+                rr.na.at[i - 1 + 3 * part], to)
+
+    def attended_piece(k):
+        zq = lax.rem(z + 4 - k, 4)
+        for i in (1, 3, 2):
+            ym, to = ypeer(i)
+            push(
+                r.att.at[mp, zq], r.att.at[mp, zq], ss.oy.at[3 * k + i - 1], rr.oy.at[3 * k + i - 1], to)
+
+    attended_piece(0)
+    for k in (1, 3, 2):
+        arrive(r.att.at[mp, lax.rem(z + 4 - k, 4)], rr.oz.at[k - 1])
+        attended_piece(k)
+    normed_half(0)
     from_all(r.cotq_s.at[ex], lambda source: r.cotq.at[mp, source], "co")
     other = pl.ds(pl.multiple_of(128 - 128 * c, 128), 128)
     for i in range(1, 4):
         ym, _ = ypeer(4 - i)
         arrive(r.wfull.at[ym, other, :], rr.wd.at[i - 1])
-    for i in range(1, 4):
-        ym, _ = ypeer(4 - i)
-        arrive(r.att.at[ym], rr.oy.at[i - 1])
+    for k in (0, 1, 3, 2):
+        for i in range(1, 4):
+            ym, _ = ypeer(4 - i)
+            arrive(r.att.at[ym, lax.rem(z + 4 - k, 4)], rr.oy.at[3 * k + i - 1])
     for i in (1, 3, 2):
         ym, to = ypeer(i)
         push(r.cotq.at[mp], r.cotq.at[mp], ss.cy.at[i - 1], rr.cy.at[i - 1], to)
+    def geometry(i):
+        p = i // 2
+        w = p + (p // 2) * (1 - 2 * (p % 2))
+        g = (2 + d * w + 4) % 4
+        flip = 1 - i % 2
+        odd = g % 2
+        slot = odd * (2 + g // 2 + 2 * flip) + (1 - odd) * (3 * g + flip)
+        xp = (x - d * g + 8) % 4
+        return slot, xp, xp * 2 + (c + flip) % 2
+
+    def softmax(i, carry):
+        slot, _, jp = geometry(i)
+        load_keys(slot, jp)
+
+        def keep(tiles):
+            for b, n in tiles:
+                r.weights[i, 0:n, 256 * b:256 * b + 256] = jnp.exp(scores(b, n, False) - r.lse[b]).astype(bf16)
+
+        @pl.when(jp < j)
+        def _():
+            keep([(b, 256 * b + 256) for b in (3, 2, 1, 0)])
+
+        @pl.when(jp > j)
+        def _():
+            keep([(b, 256 * b) for b in (3, 2, 1)])
+
+        return carry
+
     value = r.tokens[...].astype(f32) + dot(r.att[...].reshape(1024, 256), r.wfull[...].reshape(1024, 1024), 0, 0)
     r.resid[...] = value
     for k in range(4):
@@ -472,10 +518,22 @@
         def _():
             r.rescol[...] = value[:, 256 * k:256 * k + 256]
     unit, _ = norm_parts(value)
-    r.outgoing[...] = dot(slot_matrix(r.chosen[...]), (unit * r.gain2[...]).astype(bf16)).astype(bf16).reshape(
-        EX, 16, 1024)
-    to_all(lambda to: r.outgoing.at[to], r.arrived.at[ex], "di")
+    normed = (unit * r.gain2[...]).astype(bf16)
+    for step in (1, 3, 2, 0):
+        plane = lax.rem(z + step, 4)
+        r.outgoing[pl.ds(8 * plane, 8)] = dot(
+            r.placer[pl.ds(pl.multiple_of(128 * plane, 128), 128), :], normed).astype(bf16).reshape(8, 16, 1024)
+
+        def dispatch(k, carry):
+            to = plane * 8 + lax.rem(j + k, 8)
+            remote(
+                r.outgoing.at[to], r.arrived.at[ex], ss.di.at[8 * step + k - 1], rr.di.at[8 * step + k - 1],
+                (to, mp)).start()
+            return carry
+
+        lax.fori_loop(0 if step else 1, 8, dispatch, 0)
     r.arrived[ex] = r.outgoing[ex]
+    lax.fori_loop(4, 7, softmax, 0)
     loads[3].wait()
     for i in range(1, 4):
         ym, _ = ypeer(4 - i)
@@ -483,13 +541,20 @@
     for le in range(2):
         rows = jnp.concatenate([one_expert(r.cotq[k], le) for k in range(4)], axis=1)
         r.crows[le] = rows
-        r.gh[le] = dot(rows, r.wex[le], 1, 1)
+        r.gh[le] = dot(rows, r.weights[2 + le], 1, 1)
     loads[4].wait()
-    from_all(r.outgoing.at[ex], lambda source: r.arrived.at[source], "di")
+
+    def dispatched(k, carry):
+        left(r.outgoing.at[ex], ss.di.at[k - 1])
+        source = lax.rem(z + 4 - k // 8, 4) * 8 + lax.rem(j + 8 - k % 8, 8)
+        arrive(r.arrived.at[source], rr.di.at[k - 1])
+        return carry
+
+    lax.fori_loop(1, EX, dispatched, 0)
     def expert_rows(le):
         rows = one_expert(r.arrived[...], le)
         r.xrows[le] = rows
-        return dot(rows, r.win[le])
+        return dot(rows, r.weights[le])
 
     def activate(le, pre):
         hidden, slope = gelu_parts(pre)
@@ -500,7 +565,7 @@
 
     def give_back(le, gpre):
         for k in range(4):
-            product = dot(gpre, r.win[le, 256 * k:256 * k + 256, :], 1, 1)
+            product = dot(gpre, r.weights[le, 256 * k:256 * k + 256, :], 1, 1)
             r.part[le, k] = product[:, 0:128].astype(bf16)
             r.gh[le, :, 128 * k:128 * k + 128] = product[:, 128:256]
         for i in (1, 3, 2):
@@ -514,8 +579,9 @@
     r.wide_s[...] = both_experts(r.gh[0, :, 0:512], r.gh[1, :, 0:512])
     to_all(lambda to: r.wide_s.at[to], r.wide.at[ex], "bc")
     r.wide[ex] = r.wide_s[ex]
-    first = dot(r.hid[0], r.wex[0])
-    r.branch[...] = both_experts(first, dot(r.hid[1], r.wex[1]))
+    first = dot(r.hid[0], r.weights[2])
+    r.branch[...] = both_experts(first, dot(r.hid[1], r.weights[3]))
+    lax.fori_loop(0, 4, softmax, 0)
     sums = []
     for le in range(2):
         total = r.part[le, mp].astype(f32)
@@ -526,19 +592,19 @@
     r.back_s[...] = both_experts(sums[0], sums[1])
     to_all(lambda to: r.back_s.at[to], r.back.at[ex], "ba")
     r.back[ex] = r.back_s[ex]
-    placer = slot_matrix(r.chosen[...])
     from_all(r.wide_s.at[ex], lambda source: r.wide.at[source], "bc")
-    rows = dot(placer, r.wide[...].reshape(512, 512), 0, 0).astype(bf16)
+    rows = dot(r.placer[...], r.wide[...].reshape(512, 512), 0, 0).astype(bf16)
     for k in range(4):
         r.gb[k] = rows[:, 128 * k:128 * k + 128]
     for i in (1, 3, 2):
         ym, to = ypeer(i)
         push(r.gb.at[ym], r.gbr.at[i - 1], ss.gb.at[i - 1], rr.gb.at[i - 1], to)
     from_all(r.back_s.at[ex], lambda source: r.back.at[source], "ba")
-    r.gn[0, mp] = dot(placer, r.back[...].reshape(512, 128), 0, 0).astype(bf16)
+    r.gn[0, mp] = dot(r.placer[...], r.back[...].reshape(512, 128), 0, 0).astype(bf16)
     for i in (1, 3, 2):
         ym, to = ypeer(i)
         push(r.gn.at[0, mp], r.gn.at[0, mp], ss.gy.at[i - 1], rr.gy.at[i - 1], to)
+    normed_half(1)
     total = r.gb[mp].astype(f32)
     for i in range(3):
         arrive(r.gbr.at[i], rr.gb.at[i])
@@ -554,7 +620,7 @@
         arrive(r.gn.at[1, ym], rr.gy.at[i + 2])
     grad = jnp.concatenate([r.gn[k % 2, k // 2] for k in range(8)], axis=1).astype(f32)
     grad_in, ggrad = norm_back(grad, r.gain2[...], unit, inverse)
-    r.ggrad[...] = ggrad
+    r.smallf[ex] = ggrad
     gres = r.cot[...].astype(f32) + grad_in
     r.gres[...] = gres
     low = gres.astype(bf16)
@@ -573,6 +639,7 @@
             r.branch.at[:, :, pl.ds(pl.multiple_of(256 * ym, 256), 256)], r.brs.at[i - 1],
             ss.br.at[i - 1], rr.br.at[i - 1], to)
     zero = jnp.zeros((64, 256), bf16)
+    to_all(lambda to: r.smallf.at[ex], r.smallf.at[ex], "sf")
     for i in range(1, 4):
         zp, _ = zpeer(4 - i)
         arrive(r.dob.at[zp], rr.dz.at[i - 1])
@@ -581,9 +648,6 @@
     for i in (1, 3, 2):
         zp, to = zpeer(i)
         push(r.wgq.at[zp], r.wgz.at[i - 1], ss.wz.at[i - 1], rr.wz.at[i - 1], to)
-    for i in (1, 3):
-        zp, to = zpeer(i)
-        push(r.normed, r.nall.at[z], ss.na.at[i - 1], rr.na.at[i - 1], to)
     for b in range(4):
         r.dopad[b, 0:64] = zero
         r.dopad[b, 64:128] = r.dob[b]
@@ -592,13 +656,12 @@
         r.delta[b] = jnp.sum(r.dob[b].astype(f32) * r.ot[b], axis=0, keepdims=True)
         r.dq[b] = jnp.zeros((64, 256), f32)
 
-    def load_back(slot, jp):
-        load_keys(slot, jp)
+    def load_back(slot):
         for b in range(4):
             r.kvn[256 * b:256 * b + 256, :] = transposed(r.kvt[slot, b])
             r.kt[:, 256 * b:256 * b + 256] = r.kvt[slot, b, 0:64]
 
-    def backward(tiles, causal):
+    def backward(tiles, weights):
         def gather(b, n, ds, p):
             added = dot(ds, r.qd[b, 0:256]) + dot(p, r.qd[b, 256:512])
             if b == 3:
@@ -609,33 +672,29 @@
 
         held = None
         for b, n in tiles:
-            s = scores(b, n, causal)
             dp = dot(r.kvn[0:n, :], r.dopad[b])
+            p = weights(b, n)
             if held is not None:
                 gather(*held)
-            p = jnp.exp(s - r.lse[b])
             held = (b, n, (p * (dp - r.delta[b])).astype(bf16), p.astype(bf16))
         gather(*held)
 
     def back_chunk(i, carry):
+        slot, xp, jp = geometry(i)
         p = i // 2
-        w = p + (p // 2) * (1 - 2 * (p % 2))
-        g = (2 + d * w + 4) % 4
-        flip = 1 - i % 2
-        odd = g % 2
-        slot = odd * (2 + g // 2 + 2 * flip) + (1 - odd) * (3 * g + flip)
-        xp = (x - d * g + 8) % 4
-        jp = xp * 2 + (c + flip) % 2
-        load_back(slot, jp)
+        load_back(slot)
+
+        def kept(b, n):
+            return r.weights[i, 0:n, 256 * b:256 * b + 256]
 
         @pl.when(jp < j)
         def _():
-            backward([(b, 256 * b + 256) for b in (3, 2, 1, 0)], False)
+            backward([(b, 256 * b + 256) for b in (3, 2, 1, 0)], kept)
 
         @pl.when(jp > j)
         def _():
             r.dkv[768:1024] = jnp.zeros((256, 128), f32)
-            backward([(b, 256 * b) for b in (3, 2, 1)], False)
+            backward([(b, 256 * b) for b in (3, 2, 1)], kept)
 
         @pl.when(i % 2 == 0)
         def _():
@@ -661,7 +720,7 @@
                 r.xs[3] = (r.xs[1 + c].astype(f32) + r.xr[0].astype(f32)).astype(bf16)
                 remote(r.xs.at[3], r.xr.at[2], ss.xs.at[2], rr.xs.at[2], ahead).start()
 
-        @pl.when(i == 3)
+        @pl.when(i == 2)
         def _():
             for k in range(3):
                 arrive(r.wgz.at[k], rr.wz.at[k])
@@ -673,7 +732,7 @@
                 xq, to = xpeer(k)
                 remote(r.wgx.at[xq], r.wgr.at[k - 1], ss.wx.at[k - 1], rr.wx.at[k - 1], to).start()
 
-        @pl.when(i == 4)
+        @pl.when(i == 6)
         def _():
             total = r.branch[:, :, mine].astype(f32)
             for k in range(3):
@@ -681,7 +740,7 @@
                 total = total + r.brs[k].astype(f32)
             r.bs[...] = total.astype(bf16)
 
-        @pl.when(i == 6)
+        @pl.when(i == 5)
         def _():
             total = r.wgx[x].astype(f32)
             for k in range(3):
@@ -695,18 +754,20 @@
         return carry
 
     lax.fori_loop(0, 7, back_chunk, 0)
-    load_back(0, j)
-    backward([(b, 256 * b + 256) for b in (3, 2, 1, 0)], True)
+    load_back(0)
+    load_keys(0, j)
+    backward(
+        [(b, 256 * b + 256) for b in (3, 2, 1, 0)], lambda b, n: jnp.exp(scores(b, n, True) - r.lse[b]))
     for b in range(4):
         r.zs[b, 0:64] = (r.dq[b] * HEAD_DIM ** (-0.5)).astype(bf16)
     for i in (1, 3, 2):
         zp, to = zpeer(i)
         push(r.zs.at[zp, 0:64], r.zr.at[z, 0:64], ss.zq.at[i + 2], rr.zq.at[i + 2], to)
-    to_all(lambda to: r.bs.at[to], r.bret.at[ex], "bb")
-    r.bret[ex] = r.bs[ex]
-    for i in range(1, 4):
+    arrive(r.nall.at[lax.rem(z + 2, 4)], rr.na.at[1])
+    for i in (1, 3):
         zp, _ = zpeer(4 - i)
-        arrive(r.nall.at[zp], rr.na.at[i - 1])
+        arrive(r.nall.at[zp, 0:128], rr.na.at[i - 1])
+        arrive(r.nall.at[zp, 128:256], rr.na.at[i + 2])
 
     def weight_part(first, last, pieces, name):
         wt = dot(r.zs[0, first:last], r.nall[0])
@@ -722,11 +783,11 @@
                 (z * 8 + jt, mp))
 
     def weight_sum(pieces, name):
-        summed = pieces[0][j].astype(f32)
+        total = pieces[0][j].astype(f32)
         for i in range(7):
             arrive(pieces[1].at[i], getattr(rr, name).at[i])
-            summed = summed + pieces[1][i].astype(f32)
-        pieces[2][ex] = summed.astype(bf16)
+            total = total + pieces[1][i].astype(f32)
+        return total.astype(bf16)
 
     weight_part(0, 64, (r.wpq, r.wrq), "wp")
     r.resid[...] = norm_parts(r.tokens[...].astype(f32))[0]
@@ -743,12 +804,14 @@
         push(r.zs.at[zp, 64:192], r.zr.at[z, 64:192], ss.zq.at[i - 1], rr.zq.at[i - 1], to)
     r.zr[z] = r.zs[z]
     weight_part(64, 192, (r.wpk, r.wrk), "wk")
-    for i in range(1, 4):
-        xq, _ = xpeer(4 - i)
-        arrive(r.wgf.at[c, z, xq], rr.wa.at[i - 1])
-    for i in (1, 3, 2):
-        _, to = zpeer(i)
-        push(r.wgf.at[c, z], r.wgf.at[c, z], ss.wb.at[i - 1], rr.wb.at[i - 1], to)
+    r.pieces[0, c, z, x] = weight_sum((r.wpq, r.wrq), "wp")
+    gather_first(0)
+    for k in range(1, 4):
+        xq, _ = xpeer(4 - k)
+        arrive(r.wgf.at[c, z, xq], rr.wa.at[k - 1])
+    for k in (1, 3, 2):
+        _, to = zpeer(k)
+        push(r.wgf.at[c, z], r.wgf.at[c, z], ss.wb.at[k - 1], rr.wb.at[k - 1], to)
 
     def heads(first):
         return transposed(jnp.concatenate([r.zr[h, first:first + 64] for h in range(4)], axis=0))
@@ -770,10 +833,22 @@
     for i in (1, 3, 2):
         ym, to = ypeer(i)
         push(r.gnp.at[ym], r.ry.at[i - 1], ss.ry.at[i - 1], rr.ry.at[i - 1], to)
-    weight_sum((r.wpq, r.wrq, r.pieceq), "wp")
-    spread(r.pieceq, "pa", "pb")
-    weight_sum((r.wpk, r.wrk, r.piecek), "wk")
-    spread(r.piecek, "pc", "pd")
+    gather_second(0)
+    both = weight_sum((r.wpk, r.wrk), "wk")
+    r.pieces[1, c, z, x] = both[0:64]
+    r.pieces[2, c, z, x] = both[64:128]
+    gather_first(1)
+    gather_first(2)
+    for i in range(3):
+        arrive(r.smally.at[i], rr.sy.at[i])
+        one_gain = one_gain + r.smally[i]
+    r.smalle[ex] = one_gain
+    to_all(lambda to: r.smalle.at[ex], r.smalle.at[ex], "se")
+    gather_second(1)
+    gather_second(2)
+    to_all(lambda to: r.bs.at[to], r.bret.at[ex], "bb")
+    r.bret[ex] = r.bs[ex]
+    gather_third(0)
     grad = r.gnp[mp].astype(f32)
     for i in range(3):
         arrive(r.ry.at[i], rr.ry.at[i])
@@ -785,15 +860,8 @@
     for i in (1, 3, 2):
         ym, to = ypeer(i)
         push(r.igrad.at[here, :], r.igrad.at[here, :], ss.ay.at[i - 1], rr.ay.at[i - 1], to)
-    for i in range(3):
-        arrive(r.smally.at[i], rr.sy.at[i])
-        one_gain = one_gain + r.smally[i]
-    r.smalle[ex, 0:1] = one_gain
-    r.smalle[ex, 1:2] = r.ggrad[...]
-    to_all(lambda to: r.smalle.at[ex], r.smalle.at[ex], "se")
-    from_all(r.bs.at[ex], lambda source: r.bret.at[source], "bb")
-    rows = dot(slot_matrix(r.chosen[...]), r.bret[...].reshape(512, 256), 0, 0)
-    r.out[...] = (r.rescol[...] + rows).astype(bf16)
+    gather_third(1)
+    gather_third(2)
     for i in range(1, 4):
         zp, _ = zpeer(4 - i)
         arrive(r.wgf.at[c, zp], rr.wb.at[i - 1])
@@ -802,19 +870,18 @@
     for k in range(16):
         for core in range(2):
             r.wout_out[16 * k:16 * k + 16, 512 * core:512 * core + 512] = r.wgf[core, k // 4, k % 4]
-    pass_on(r.pieceq, "pa", "pb")
-    pass_on(r.piecek, "pc", "pd")
-    passed(r.pieceq, "pb")
-    passed(r.piecek, "pd")
     for k in range(3):
-        source, first = (r.pieceq, 0) if k == 0 else (r.piecek, 64 * k - 64)
+        arrive(r.pieces.at[k, 1 - c], rr.pc.at[k])
         for row in range(8):
-            block = jnp.concatenate([source[8 * h + row, first:first + 64] for h in range(4)], axis=0)
+            block = jnp.concatenate([r.pieces[k, row % 2, h, row // 2] for h in range(4)], axis=0)
             r.qkv_out[k, 128 * row:128 * row + 128] = transposed(block)
     from_all(r.smalle.at[ex], lambda source: r.smalle.at[source], "se")
-    both = jnp.sum(r.smalle[...], axis=0)
-    r.gain1_out[...] = both[0:1]
-    r.gain2_out[...] = both[1:2]
+    from_all(r.smallf.at[ex], lambda source: r.smallf.at[source], "sf")
+    r.gain1_out[...] = jnp.sum(r.smalle[...], axis=0)
+    r.gain2_out[...] = jnp.sum(r.smallf[...], axis=0)
+    from_all(r.bs.at[ex], lambda source: r.bret.at[source], "bb")
+    rows = dot(r.placer[...], r.bret[...].reshape(512, 256), 0, 0)
+    r.out[...] = (r.rescol[...] + rows).astype(bf16)
     for i in range(1, 4):
         ym, _ = ypeer(4 - i)
         there = pl.ds(pl.multiple_of(64 * ym, 64), 64)

time: 142 us -> 139 us (0.979)
  Pallas kernels: 141 us -> 138 us
    pallas_call x1, Pallas kernels: 133 us -> 130 us  [layer(): pl.pallas_call(layer_kernel, out_shape=[pltpu.VMEM(s, t) for s, t in OUTS...]
where the time goes in v5:
time: 139 us
  Pallas kernels  138 us (99%)
    pallas_call x1, Pallas kernels, layer(): pl.pallas_call(layer_kernel, out_shape=[pltpu.VMEM(s, t) for s, t in OUTS...  130 us
    pallas_call x1, Pallas kernels, finish(): pl.pallas_call(finish_kernel, out_shape=[jax.ShapeDtypeStruct(s, t) for s...  7.8 us

profile of v5, /device:TPU:1, one launch (start us, length us, event | category | flops | bytes accessed | tf_op | source)
XLA Modules:
  0.0 138.8 jit_solution(10304473348025397911)
XLA Ops:
  0.6 130.2 %layer.1 = (bf16[2,256,1024]{2,1,0:T(8,128)(2,1)S(1)}, bf16[2,256,1024]{2,1,0:T(8,128)(2,1)S(1)}, bf16[2,256,1024]{2,1,0:T(8,128)(2,1)S(1)}, bf16[2,256,1024]{2,...) custom-call(s32[9]{0:T(128)} %refs_0_.1, ...), custom_call_target="tpu_custom_call" | custom-call | tf_op jit(solution)/shard_map/layer/pallas_call | solution.py:904
  130.8 7.8 %finish.1 = (f32[2,1024,1024]{2,1,0:T(8,128)}, f32[2,1024,1024]{2,1,0:T(8,128)}, f32[3,1024,256]{2,1,0:T(8,128)}, f32[256,1024]{1,0:T(8,128)}, bf16[256,256]{1,0...) custom-call(bf16[2,256,1024]{2,1,0:T(8,128)(2,1)S(1)} %get-tuple-element.26.x, ...), custom_call_target="tpu_custom_call" | custom-call | flops 2147483648 | bytes 29360128 | tf_op jit(solution)/shard_map/finish/pallas_call | solution.py:946

commit v6 on v5

--- a/solution.py
+++ b/solution.py
@@ -161,13 +161,12 @@
     "smally": ((3, 1, 1024), f32), "smalle": ((32, 1, 1024), f32), "smallf": ((32, 1, 1024), f32),
 }
 LOCAL = {"load": (5,)}
-SENT = {
-    "az": (6,), "ag": (28,), "wf": (3,), "wd": (3,), "co": (31,), "cy": (3,), "na": (6,), "oz": (3,), "oy": (12,),
-    "di": (31,), "rs": (6,), "ba": (31,), "bc": (31,), "gb": (3,), "gy": (6,), "dz": (3,), "br": (3,), "bb": (31,), "sb": (4,), "xs": (3,),
-    "wg": (1,), "wz": (3,), "wx": (3,), "wa": (3,), "wb": (3,), "wc": (1,), "zq": (6,), "wp": (7,), "wk": (7,), "pa": (9,), "pb": (9,), "pc": (3,),
-    "ry": (3,), "ay": (3,), "sy": (3,), "se": (31,), "sf": (31,),
-}
-TAKEN = dict(SENT, ag=(32,))
+SENT = dict.fromkeys(
+    ("az", "aq", "ag", "wf", "wd", "co", "cy", "na", "oz", "oy", "di", "rs", "ba", "bc", "gb", "gy", "dz", "br", "bb", "sb",
+     "xs", "wg", "wz", "wx", "wa", "wb", "wc", "zd", "zq", "wp", "wk", "ry", "ay", "sy", "se", "sf"),
+    (1,))
+SENT.update(pa=(3,), pb=(3,), pc=(3,))
+TAKEN = dict(SENT, az=(3,), ag=(16,), oz=(3,), sb=(4,), xs=(3,))
 
 
 class Refs:
@@ -187,7 +186,6 @@
     sib = (ex + d, mp)
     ahead = (z * 8 + lax.rem(x + d + 4, 4) * 2 + c, mp)
     behind = (z * 8 + lax.rem(x - d + 4, 4) * 2 + c, mp)
-    pending = []
 
     def zpeer(i):
         zp = lax.rem(z + i, 4)
@@ -207,7 +205,6 @@
 
     def push(src, dst, ssem, rsem, device):
         remote(src, dst, ssem, rsem, device).start()
-        pending.append((src, ssem))
 
     def arrive(dst, rsem):
         remote(dst, dst, rsem, rsem, sib).wait_recv()
@@ -218,15 +215,7 @@
     def to_all(src_of, dst, name):
         def one(k, carry):
             to = lax.rem(ex + k, EX)
-            remote(src_of(to), dst, getattr(ss, name).at[k - 1], getattr(rr, name).at[k - 1], (to, mp)).start()
-            return carry
-
-        lax.fori_loop(1, EX, one, 0)
-
-    def from_all(src, dst_of, name):
-        def one(k, carry):
-            left(src, getattr(ss, name).at[k - 1])
-            arrive(dst_of(lax.rem(ex + EX - k, EX)), getattr(rr, name).at[k - 1])
+            remote(src_of(to), dst, getattr(ss, name).at[0], getattr(rr, name).at[0], (to, mp)).start()
             return carry
 
         lax.fori_loop(1, EX, one, 0)
@@ -235,29 +224,17 @@
         for i in (1, 3, 2):
             _, to = xpeer(i) if part == 1 else zpeer(i)
             own = r.pieces.at[part, c, z, x]
-            push(own, own, ss.pa.at[3 * part + i - 1], rr.pa.at[3 * part + i - 1], to)
+            push(own, own, ss.pa.at[part], rr.pa.at[part], to)
 
     def gather_second(part):
-        for i in range(1, 4):
-            if part == 1:
-                xq, _ = xpeer(4 - i)
-                arrive(r.pieces.at[part, c, z, xq], rr.pa.at[3 * part + i - 1])
-            else:
-                zp, _ = zpeer(4 - i)
-                arrive(r.pieces.at[part, c, zp, x], rr.pa.at[3 * part + i - 1])
+        arrive(r.pieces.at[part, 0, 0, 0:3], rr.pa.at[part])
         row = r.pieces.at[part, c, z] if part == 1 else r.pieces.at[part, c, :, x]
         for i in (1, 3, 2):
             _, to = zpeer(i) if part == 1 else xpeer(i)
-            push(row, row, ss.pb.at[3 * part + i - 1], rr.pb.at[3 * part + i - 1], to)
+            push(row, row, ss.pb.at[part], rr.pb.at[part], to)
 
     def gather_third(part):
-        for i in range(1, 4):
-            if part == 1:
-                zp, _ = zpeer(4 - i)
-                arrive(r.pieces.at[part, c, zp], rr.pb.at[3 * part + i - 1])
-            else:
-                xq, _ = xpeer(4 - i)
-                arrive(r.pieces.at[part, c, :, xq], rr.pb.at[3 * part + i - 1])
+        arrive(r.pieces.at[part, 0, 0:3], rr.pb.at[part])
         push(r.pieces.at[part, c], r.pieces.at[part, c], ss.pc.at[part], rr.pc.at[part], sib)
 
     bar = greet(ex, mp)
@@ -283,41 +260,44 @@
     greeted(bar)
     for i in (1, 3, 2):
         zp, to = zpeer(i)
-        push(r.kv_s.at[zp], r.kvt.at[0, z], ss.az.at[i - 1], rr.az.at[i - 1], to)
+        push(r.kv_s.at[zp], r.kvt.at[0, z], ss.az.at[0], rr.az.at[i - 1], to)
     r.kvt[0, z] = r.kv_s[z]
 
     def own_piece(k):
         zq = lax.rem(z + 4 - k, 4)
-        remote(r.kvt.at[0, zq], r.kvt.at[2, zq], ss.ag.at[4 * 1 + k], rr.ag.at[4 * 2 + k], ahead).start()
-        remote(r.kvt.at[0, zq], r.kvt.at[3, zq], ss.ag.at[4 * 2 + k], rr.ag.at[4 * 3 + k], behind).start()
-        remote(r.kvt.at[0, zq], r.kvt.at[1, zq], ss.ag.at[k], rr.ag.at[4 * 1 + k], sib).start()
+        remote(r.kvt.at[0, zq], r.kvt.at[2, zq], ss.ag.at[0], rr.ag.at[4 + k], ahead).start()
+        remote(r.kvt.at[0, zq], r.kvt.at[3, zq], ss.ag.at[0], rr.ag.at[8 + k], behind).start()
+        remote(r.kvt.at[0, zq], r.kvt.at[1, zq], ss.ag.at[0], rr.ag.at[0], sib).start()
 
     def came(slot, k):
-        arrive(r.kvt.at[slot, lax.rem(z + 4 - k, 4)], rr.ag.at[4 * slot + k])
+        arrive(r.kvt.at[slot, lax.rem(z + 4 - k, 4)], rr.ag.at[{2: 4, 3: 8, 6: 12}[slot] + k])
+
+    def came_whole(slot):
+        arrive(r.kvt.at[slot], rr.ag.at[{1: 0, 4: 1, 5: 2, 7: 3}[slot]])
 
     def from_sides(k):
         zq = lax.rem(z + 4 - k, 4)
         came(2, k)
-        remote(r.kvt.at[2, zq], r.kvt.at[6, zq], ss.ag.at[4 * 3 + k], rr.ag.at[4 * 6 + k], ahead).start()
-        remote(r.kvt.at[2, zq], r.kvt.at[5, zq], ss.ag.at[4 * 4 + k], rr.ag.at[4 * 5 + k], sib).start()
+        remote(r.kvt.at[2, zq], r.kvt.at[6, zq], ss.ag.at[0], rr.ag.at[12 + k], ahead).start()
+        remote(r.kvt.at[2, zq], r.kvt.at[5, zq], ss.ag.at[0], rr.ag.at[2], sib).start()
         came(3, k)
-        remote(r.kvt.at[3, zq], r.kvt.at[4, zq], ss.ag.at[4 * 5 + k], rr.ag.at[4 * 4 + k], sib).start()
+        remote(r.kvt.at[3, zq], r.kvt.at[4, zq], ss.ag.at[0], rr.ag.at[1], sib).start()
 
     def from_far(k):
         zq = lax.rem(z + 4 - k, 4)
         came(6, k)
-        remote(r.kvt.at[6, zq], r.kvt.at[7, zq], ss.ag.at[4 * 6 + k], rr.ag.at[4 * 7 + k], sib).start()
+        remote(r.kvt.at[6, zq], r.kvt.at[7, zq], ss.ag.at[0], rr.ag.at[3], sib).start()
 
     own_piece(0)
     for i in (1, 3, 2):
         zp, to = zpeer(i)
-        push(r.q_s.at[zp], r.q.at[z], ss.az.at[i + 2], rr.az.at[i + 2], to)
+        push(r.q_s.at[zp], r.q.at[z], ss.aq.at[0], rr.aq.at[0], to)
     r.q[z] = r.q_s[z]
     loads[1].wait()
     half = pl.ds(pl.multiple_of(128 * c, 128), 128)
     for i in range(1, 4):
         ym, to = ypeer(i)
-        push(r.wfull.at[mp, half, :], r.wfull.at[mp, half, :], ss.wf.at[i - 1], rr.wf.at[i - 1], to)
+        push(r.wfull.at[mp, half, :], r.wfull.at[mp, half, :], ss.wf.at[0], rr.wf.at[0], to)
     r.vt1[64:80, :] = jnp.ones((16, 1024), bf16)
     ends = doc_ends(r.lengths)
     feature = lax.broadcasted_iota(jnp.int32, (64, 256), 0)
@@ -334,10 +314,9 @@
     arrive(r.kvt.at[0, lax.rem(z + 2, 4)], rr.az.at[1])
     own_piece(2)
     zp, to = zpeer(2)
-    push(r.normed, r.nall.at[z], ss.na.at[1], rr.na.at[1], to)
+    push(r.normed, r.nall.at[z], ss.na.at[0], rr.na.at[0], to)
     r.nall[z] = r.normed[...]
-    for i in range(1, 4):
-        arrive(r.q.at[lax.rem(z + 4 - i, 4)], rr.az.at[i + 2])
+    arrive(r.q.at[0:3], rr.aq.at[0])
     for b in range(4):
         docs = doc_row(ends, (b * 8 + j) * 256, 256)
         r.qaug[b, 0:64] = r.q[b]
@@ -393,8 +372,7 @@
         def _():
             from_sides(1)
             from_far(0)
-            for k in range(4):
-                came(1, k)
+            came_whole(1)
 
         @pl.when(i == 2)
         def _():
@@ -409,24 +387,21 @@
         @pl.when(i == 4)
         def _():
             from_far(2)
-            for k in range(4):
-                came(4, k)
+            came_whole(4)
             to_all(lambda to: r.cotq_s.at[to], r.cotq.at[mp, ex], "co")
 
         @pl.when(i == 5)
         def _():
-            for k in range(4):
-                came(5, k)
+            came_whole(5)
+            arrive(r.wfull.at[0:3, 0:128, :], rr.wf.at[0])
             for i in range(1, 4):
                 ym, to = ypeer(4 - i)
-                arrive(r.wfull.at[ym, half, :], rr.wf.at[i - 1])
                 remote(
-                    r.wfull.at[ym, half, :], r.wfull.at[ym, half, :], ss.wd.at[i - 1], rr.wd.at[i - 1], sib).start()
+                    r.wfull.at[ym, half, :], r.wfull.at[ym, half, :], ss.wd.at[0], rr.wd.at[0], sib).start()
 
         @pl.when(i == 7)
         def _():
-            for k in range(4):
-                came(7, k)
+            came_whole(7)
 
         load_chunk(i, jp)
 
@@ -449,40 +424,34 @@
         r.o_s[b] = ot.astype(bf16)
     for i in (1, 3, 2):
         zp, to = zpeer(i)
-        push(r.o_s.at[zp], r.att.at[mp, z], ss.oz.at[i - 1], rr.oz.at[i - 1], to)
+        push(r.o_s.at[zp], r.att.at[mp, z], ss.oz.at[0], rr.oz.at[i - 1], to)
     r.att[mp, z] = r.o_s[z]
     def normed_half(part):
         rows = pl.ds(128 * part, 128)
         for i in (1, 3):
             zp, to = zpeer(i)
             push(
-                r.normed.at[rows, :], r.nall.at[z, rows, :], ss.na.at[i - 1 + 3 * part],
-                rr.na.at[i - 1 + 3 * part], to)
+                r.normed.at[rows, :], r.nall.at[z, rows, :], ss.na.at[0],
+                rr.na.at[0], to)
 
     def attended_piece(k):
         zq = lax.rem(z + 4 - k, 4)
         for i in (1, 3, 2):
             ym, to = ypeer(i)
             push(
-                r.att.at[mp, zq], r.att.at[mp, zq], ss.oy.at[3 * k + i - 1], rr.oy.at[3 * k + i - 1], to)
+                r.att.at[mp, zq], r.att.at[mp, zq], ss.oy.at[0], rr.oy.at[0], to)
 
     attended_piece(0)
     for k in (1, 3, 2):
         arrive(r.att.at[mp, lax.rem(z + 4 - k, 4)], rr.oz.at[k - 1])
         attended_piece(k)
     normed_half(0)
-    from_all(r.cotq_s.at[ex], lambda source: r.cotq.at[mp, source], "co")
-    other = pl.ds(pl.multiple_of(128 - 128 * c, 128), 128)
-    for i in range(1, 4):
-        ym, _ = ypeer(4 - i)
-        arrive(r.wfull.at[ym, other, :], rr.wd.at[i - 1])
-    for k in (0, 1, 3, 2):
-        for i in range(1, 4):
-            ym, _ = ypeer(4 - i)
-            arrive(r.att.at[ym, lax.rem(z + 4 - k, 4)], rr.oy.at[3 * k + i - 1])
+    arrive(r.cotq.at[0, 0:31], rr.co.at[0])
+    arrive(r.wfull.at[0:3, 0:128, :], rr.wd.at[0])
+    arrive(r.att.at[0:3], rr.oy.at[0])
     for i in (1, 3, 2):
         ym, to = ypeer(i)
-        push(r.cotq.at[mp], r.cotq.at[mp], ss.cy.at[i - 1], rr.cy.at[i - 1], to)
+        push(r.cotq.at[mp], r.cotq.at[mp], ss.cy.at[0], rr.cy.at[0], to)
     def geometry(i):
         p = i // 2
         w = p + (p // 2) * (1 - 2 * (p % 2))
@@ -527,7 +496,7 @@
         def dispatch(k, carry):
             to = plane * 8 + lax.rem(j + k, 8)
             remote(
-                r.outgoing.at[to], r.arrived.at[ex], ss.di.at[8 * step + k - 1], rr.di.at[8 * step + k - 1],
+                r.outgoing.at[to], r.arrived.at[ex], ss.di.at[0], rr.di.at[0],
                 (to, mp)).start()
             return carry
 
@@ -535,22 +504,13 @@
     r.arrived[ex] = r.outgoing[ex]
     lax.fori_loop(4, 7, softmax, 0)
     loads[3].wait()
-    for i in range(1, 4):
-        ym, _ = ypeer(4 - i)
-        arrive(r.cotq.at[ym], rr.cy.at[i - 1])
+    arrive(r.cotq.at[0:3], rr.cy.at[0])
     for le in range(2):
         rows = jnp.concatenate([one_expert(r.cotq[k], le) for k in range(4)], axis=1)
         r.crows[le] = rows
         r.gh[le] = dot(rows, r.weights[2 + le], 1, 1)
     loads[4].wait()
-
-    def dispatched(k, carry):
-        left(r.outgoing.at[ex], ss.di.at[k - 1])
-        source = lax.rem(z + 4 - k // 8, 4) * 8 + lax.rem(j + 8 - k % 8, 8)
-        arrive(r.arrived.at[source], rr.di.at[k - 1])
-        return carry
-
-    lax.fori_loop(1, EX, dispatched, 0)
+    arrive(r.arrived.at[0:31], rr.di.at[0])
     def expert_rows(le):
         rows = one_expert(r.arrived[...], le)
         r.xrows[le] = rows
@@ -570,7 +530,7 @@
             r.gh[le, :, 128 * k:128 * k + 128] = product[:, 128:256]
         for i in (1, 3, 2):
             ym, to = ypeer(i)
-            push(r.part.at[le, ym], r.rs.at[le, i - 1], ss.rs.at[3 * le + i - 1], rr.rs.at[3 * le + i - 1], to)
+            push(r.part.at[le, ym], r.rs.at[le, i - 1], ss.rs.at[0], rr.rs.at[0], to)
 
     first, second = expert_rows(0), expert_rows(1)
     gpre = activate(0, first)
@@ -582,42 +542,39 @@
     first = dot(r.hid[0], r.weights[2])
     r.branch[...] = both_experts(first, dot(r.hid[1], r.weights[3]))
     lax.fori_loop(0, 4, softmax, 0)
+    arrive(r.rs, rr.rs.at[0])
     sums = []
     for le in range(2):
         total = r.part[le, mp].astype(f32)
         for i in range(3):
-            arrive(r.rs.at[le, i], rr.rs.at[3 * le + i])
             total = total + r.rs[le, i].astype(f32)
         sums.append(total)
     r.back_s[...] = both_experts(sums[0], sums[1])
     to_all(lambda to: r.back_s.at[to], r.back.at[ex], "ba")
     r.back[ex] = r.back_s[ex]
-    from_all(r.wide_s.at[ex], lambda source: r.wide.at[source], "bc")
+    arrive(r.wide.at[0:31], rr.bc.at[0])
     rows = dot(r.placer[...], r.wide[...].reshape(512, 512), 0, 0).astype(bf16)
     for k in range(4):
         r.gb[k] = rows[:, 128 * k:128 * k + 128]
     for i in (1, 3, 2):
         ym, to = ypeer(i)
-        push(r.gb.at[ym], r.gbr.at[i - 1], ss.gb.at[i - 1], rr.gb.at[i - 1], to)
-    from_all(r.back_s.at[ex], lambda source: r.back.at[source], "ba")
+        push(r.gb.at[ym], r.gbr.at[i - 1], ss.gb.at[0], rr.gb.at[0], to)
+    arrive(r.back.at[0:31], rr.ba.at[0])
     r.gn[0, mp] = dot(r.placer[...], r.back[...].reshape(512, 128), 0, 0).astype(bf16)
     for i in (1, 3, 2):
         ym, to = ypeer(i)
-        push(r.gn.at[0, mp], r.gn.at[0, mp], ss.gy.at[i - 1], rr.gy.at[i - 1], to)
+        push(r.gn.at[0, mp], r.gn.at[0, mp], ss.gy.at[0], rr.gy.at[0], to)
     normed_half(1)
     total = r.gb[mp].astype(f32)
+    arrive(r.gbr, rr.gb.at[0])
     for i in range(3):
-        arrive(r.gbr.at[i], rr.gb.at[i])
         total = total + r.gbr[i].astype(f32)
     r.gn[1, mp] = total.astype(bf16)
     for i in (1, 3, 2):
         ym, to = ypeer(i)
-        push(r.gn.at[1, mp], r.gn.at[1, mp], ss.gy.at[i + 2], rr.gy.at[i + 2], to)
+        push(r.gn.at[1, mp], r.gn.at[1, mp], ss.gy.at[0], rr.gy.at[0], to)
     unit, inverse = norm_parts(r.resid[...])
-    for i in range(1, 4):
-        ym, _ = ypeer(4 - i)
-        arrive(r.gn.at[0, ym], rr.gy.at[i - 1])
-        arrive(r.gn.at[1, ym], rr.gy.at[i + 2])
+    arrive(r.gn.at[:, 0:3], rr.gy.at[0])
     grad = jnp.concatenate([r.gn[k % 2, k // 2] for k in range(8)], axis=1).astype(f32)
     grad_in, ggrad = norm_back(grad, r.gain2[...], unit, inverse)
     r.smallf[ex] = ggrad
@@ -627,7 +584,7 @@
     r.dheads[...] = dot(r.wfull[mp], low, 1, 1).astype(bf16).reshape(4, 64, 256)
     for i in (1, 3, 2):
         zp, to = zpeer(i)
-        push(r.dheads.at[zp], r.dob.at[z], ss.dz.at[i - 1], rr.dz.at[i - 1], to)
+        push(r.dheads.at[zp], r.dob.at[z], ss.dz.at[0], rr.dz.at[0], to)
     r.dob[z] = r.dheads[z]
     wgrad = dot(r.att[mp].reshape(256, 256), low).astype(bf16)
     r.wgp[0] = wgrad[:, 0:512].reshape(4, 4, 16, 512)
@@ -637,17 +594,15 @@
         ym, to = ypeer(i)
         push(
             r.branch.at[:, :, pl.ds(pl.multiple_of(256 * ym, 256), 256)], r.brs.at[i - 1],
-            ss.br.at[i - 1], rr.br.at[i - 1], to)
+            ss.br.at[0], rr.br.at[0], to)
     zero = jnp.zeros((64, 256), bf16)
     to_all(lambda to: r.smallf.at[ex], r.smallf.at[ex], "sf")
-    for i in range(1, 4):
-        zp, _ = zpeer(4 - i)
-        arrive(r.dob.at[zp], rr.dz.at[i - 1])
+    arrive(r.dob.at[0:3], rr.dz.at[0])
     arrive(r.wgs, rr.wg.at[0])
     r.wgq[...] = (r.wgp[c].astype(f32) + r.wgs[...].astype(f32)).astype(bf16)
     for i in (1, 3, 2):
         zp, to = zpeer(i)
-        push(r.wgq.at[zp], r.wgz.at[i - 1], ss.wz.at[i - 1], rr.wz.at[i - 1], to)
+        push(r.wgq.at[zp], r.wgz.at[i - 1], ss.wz.at[0], rr.wz.at[0], to)
     for b in range(4):
         r.dopad[b, 0:64] = zero
         r.dopad[b, 64:128] = r.dob[b]
@@ -699,7 +654,7 @@
         @pl.when(i % 2 == 0)
         def _():
             r.sb[p] = r.dkv[...].astype(bf16)
-            remote(r.sb.at[p], r.sr.at[p], ss.sb.at[p], rr.sb.at[p], sib).start()
+            remote(r.sb.at[p], r.sr.at[p], ss.sb.at[0], rr.sb.at[p], sib).start()
 
         @pl.when(i % 2 == 1)
         def _():
@@ -712,44 +667,43 @@
 
             @pl.when(p == 2 - c)
             def _():
-                remote(r.xs.at[p], r.xr.at[1], ss.xs.at[1], rr.xs.at[1], behind).start()
+                remote(r.xs.at[p], r.xr.at[1], ss.xs.at[0], rr.xs.at[1], behind).start()
 
             @pl.when(p == 2)
             def _():
                 arrive(r.xr.at[0], rr.xs.at[0])
                 r.xs[3] = (r.xs[1 + c].astype(f32) + r.xr[0].astype(f32)).astype(bf16)
-                remote(r.xs.at[3], r.xr.at[2], ss.xs.at[2], rr.xs.at[2], ahead).start()
+                remote(r.xs.at[3], r.xr.at[2], ss.xs.at[0], rr.xs.at[2], ahead).start()
 
         @pl.when(i == 2)
         def _():
-            for k in range(3):
-                arrive(r.wgz.at[k], rr.wz.at[k])
+            arrive(r.wgz, rr.wz.at[0])
             total = r.wgq[z].astype(f32)
             for k in range(3):
                 total = total + r.wgz[k].astype(f32)
             r.wgx[...] = total.astype(bf16)
             for k in (1, 3, 2):
                 xq, to = xpeer(k)
-                remote(r.wgx.at[xq], r.wgr.at[k - 1], ss.wx.at[k - 1], rr.wx.at[k - 1], to).start()
+                remote(r.wgx.at[xq], r.wgr.at[k - 1], ss.wx.at[0], rr.wx.at[0], to).start()
 
         @pl.when(i == 6)
         def _():
             total = r.branch[:, :, mine].astype(f32)
+            arrive(r.brs, rr.br.at[0])
             for k in range(3):
-                arrive(r.brs.at[k], rr.br.at[k])
                 total = total + r.brs[k].astype(f32)
             r.bs[...] = total.astype(bf16)
 
         @pl.when(i == 5)
         def _():
             total = r.wgx[x].astype(f32)
+            arrive(r.wgr, rr.wx.at[0])
             for k in range(3):
-                arrive(r.wgr.at[k], rr.wx.at[k])
                 total = total + r.wgr[k].astype(f32)
             r.wgf[c, z, x] = total.astype(bf16)
             for k in (1, 3, 2):
                 _, to = xpeer(k)
-                remote(r.wgf.at[c, z, x], r.wgf.at[c, z, x], ss.wa.at[k - 1], rr.wa.at[k - 1], to).start()
+                remote(r.wgf.at[c, z, x], r.wgf.at[c, z, x], ss.wa.at[0], rr.wa.at[0], to).start()
 
         return carry
 
@@ -762,12 +716,8 @@
         r.zs[b, 0:64] = (r.dq[b] * HEAD_DIM ** (-0.5)).astype(bf16)
     for i in (1, 3, 2):
         zp, to = zpeer(i)
-        push(r.zs.at[zp, 0:64], r.zr.at[z, 0:64], ss.zq.at[i + 2], rr.zq.at[i + 2], to)
-    arrive(r.nall.at[lax.rem(z + 2, 4)], rr.na.at[1])
-    for i in (1, 3):
-        zp, _ = zpeer(4 - i)
-        arrive(r.nall.at[zp, 0:128], rr.na.at[i - 1])
-        arrive(r.nall.at[zp, 128:256], rr.na.at[i + 2])
+        push(r.zs.at[zp, 0:64], r.zr.at[z, 0:64], ss.zd.at[0], rr.zd.at[0], to)
+    arrive(r.nall.at[0:3], rr.na.at[0])
 
     def weight_part(first, last, pieces, name):
         wt = dot(r.zs[0, first:last], r.nall[0])
@@ -779,13 +729,13 @@
         for i in range(1, 8):
             jt = lax.rem(j + i, 8)
             push(
-                pieces[0].at[jt], pieces[1].at[i - 1], getattr(ss, name).at[i - 1], getattr(rr, name).at[i - 1],
+                pieces[0].at[jt], pieces[1].at[i - 1], getattr(ss, name).at[0], getattr(rr, name).at[0],
                 (z * 8 + jt, mp))
 
     def weight_sum(pieces, name):
         total = pieces[0][j].astype(f32)
+        arrive(pieces[1], getattr(rr, name).at[0])
         for i in range(7):
-            arrive(pieces[1].at[i], getattr(rr, name).at[i])
             total = total + pieces[1][i].astype(f32)
         return total.astype(bf16)
 
@@ -801,46 +751,40 @@
         r.zs[b, 64:192] = transposed(low[256 * b:256 * b + 256])
     for i in (1, 3, 2):
         zp, to = zpeer(i)
-        push(r.zs.at[zp, 64:192], r.zr.at[z, 64:192], ss.zq.at[i - 1], rr.zq.at[i - 1], to)
+        push(r.zs.at[zp, 64:192], r.zr.at[z, 64:192], ss.zq.at[0], rr.zq.at[0], to)
     r.zr[z] = r.zs[z]
     weight_part(64, 192, (r.wpk, r.wrk), "wk")
     r.pieces[0, c, z, x] = weight_sum((r.wpq, r.wrq), "wp")
     gather_first(0)
-    for k in range(1, 4):
-        xq, _ = xpeer(4 - k)
-        arrive(r.wgf.at[c, z, xq], rr.wa.at[k - 1])
+    arrive(r.wgf.at[0, 0, 0:3], rr.wa.at[0])
     for k in (1, 3, 2):
         _, to = zpeer(k)
-        push(r.wgf.at[c, z], r.wgf.at[c, z], ss.wb.at[k - 1], rr.wb.at[k - 1], to)
+        push(r.wgf.at[c, z], r.wgf.at[c, z], ss.wb.at[0], rr.wb.at[0], to)
 
     def heads(first):
         return transposed(jnp.concatenate([r.zr[h, first:first + 64] for h in range(4)], axis=0))
 
-    for i in range(1, 4):
-        zp, _ = zpeer(4 - i)
-        arrive(r.zr.at[zp, 0:64], rr.zq.at[i + 2])
+    arrive(r.zr.at[0:3, 0:64], rr.zd.at[0])
     part = dot(heads(0), r.wqkv[0], 1, 1)
-    for i in range(1, 4):
-        zp, _ = zpeer(4 - i)
-        arrive(r.zr.at[zp, 64:192], rr.zq.at[i - 1])
+    arrive(r.zr.at[0:3, 64:192], rr.zq.at[0])
     part = part + dot(heads(64), r.wqkv[1], 1, 1) + dot(heads(128), r.wqkv[2], 1, 1)
     r.gnp[...] = part.astype(bf16).reshape(4, 64, 1024)
     one_gain = jnp.sum(part * r.resid[...], axis=0, keepdims=True)
     r.small[...] = one_gain
     for i in (1, 3, 2):
         ym, to = ypeer(i)
-        push(r.small, r.smally.at[i - 1], ss.sy.at[i - 1], rr.sy.at[i - 1], to)
+        push(r.small, r.smally.at[i - 1], ss.sy.at[0], rr.sy.at[0], to)
     for i in (1, 3, 2):
         ym, to = ypeer(i)
-        push(r.gnp.at[ym], r.ry.at[i - 1], ss.ry.at[i - 1], rr.ry.at[i - 1], to)
+        push(r.gnp.at[ym], r.ry.at[i - 1], ss.ry.at[0], rr.ry.at[0], to)
     gather_second(0)
     both = weight_sum((r.wpk, r.wrk), "wk")
     r.pieces[1, c, z, x] = both[0:64]
     r.pieces[2, c, z, x] = both[64:128]
     gather_first(1)
     gather_first(2)
+    arrive(r.smally, rr.sy.at[0])
     for i in range(3):
-        arrive(r.smally.at[i], rr.sy.at[i])
         one_gain = one_gain + r.smally[i]
     r.smalle[ex] = one_gain
     to_all(lambda to: r.smalle.at[ex], r.smalle.at[ex], "se")
@@ -850,8 +794,8 @@
     r.bret[ex] = r.bs[ex]
     gather_third(0)
     grad = r.gnp[mp].astype(f32)
+    arrive(r.ry, rr.ry.at[0])
     for i in range(3):
-        arrive(r.ry.at[i], rr.ry.at[i])
         grad = grad + r.ry[i].astype(f32)
     here = pl.ds(pl.multiple_of(64 * mp, 64), 64)
     unit, inverse = norm_parts(r.tokens[here, :].astype(f32))
@@ -859,12 +803,10 @@
     r.igrad[here, :] = (r.gres[here, :] + grad_in).astype(bf16)
     for i in (1, 3, 2):
         ym, to = ypeer(i)
-        push(r.igrad.at[here, :], r.igrad.at[here, :], ss.ay.at[i - 1], rr.ay.at[i - 1], to)
+        push(r.igrad.at[here, :], r.igrad.at[here, :], ss.ay.at[0], rr.ay.at[0], to)
     gather_third(1)
     gather_third(2)
-    for i in range(1, 4):
-        zp, _ = zpeer(4 - i)
-        arrive(r.wgf.at[c, zp], rr.wb.at[i - 1])
+    arrive(r.wgf.at[0, 0:3], rr.wb.at[0])
     push(r.wgf.at[c], r.wgf.at[c], ss.wc.at[0], rr.wc.at[0], sib)
     arrive(r.wgf.at[1 - c], rr.wc.at[0])
     for k in range(16):
@@ -875,29 +817,30 @@
         for row in range(8):
             block = jnp.concatenate([r.pieces[k, row % 2, h, row // 2] for h in range(4)], axis=0)
             r.qkv_out[k, 128 * row:128 * row + 128] = transposed(block)
-    from_all(r.smalle.at[ex], lambda source: r.smalle.at[source], "se")
-    from_all(r.smallf.at[ex], lambda source: r.smallf.at[source], "sf")
+    arrive(r.smalle.at[0:31], rr.se.at[0])
+    arrive(r.smallf.at[0:31], rr.sf.at[0])
     r.gain1_out[...] = jnp.sum(r.smalle[...], axis=0)
     r.gain2_out[...] = jnp.sum(r.smallf[...], axis=0)
-    from_all(r.bs.at[ex], lambda source: r.bret.at[source], "bb")
+    arrive(r.bret.at[0:31], rr.bb.at[0])
     rows = dot(r.placer[...], r.bret[...].reshape(512, 256), 0, 0)
     r.out[...] = (r.rescol[...] + rows).astype(bf16)
-    for i in range(1, 4):
-        ym, _ = ypeer(4 - i)
-        there = pl.ds(pl.multiple_of(64 * ym, 64), 64)
-        arrive(r.igrad.at[there, :], rr.ay.at[i - 1])
-    for src, ssem in pending:
-        left(src, ssem)
-    for k in range(28):
-        left(r.kvt.at[0, 0], ss.ag.at[k])
-    for k in range(3):
-        left(r.wfull.at[0, half, :], ss.wd.at[k])
-    for p in range(4):
-        left(r.sb.at[p], ss.sb.at[p])
-    for p in range(3):
-        left(r.xs.at[p], ss.xs.at[p])
-        left(r.wgx.at[0], ss.wx.at[p])
-        left(r.wgf.at[c, z, x], ss.wa.at[p])
+    arrive(r.igrad.at[0:192, :], rr.ay.at[0])
+    sent = {
+        "az": r.kv_s.at[0:3], "aq": r.q_s.at[0:3], "ag": r.kvt.at[0:7], "wf": r.wfull.at[0:3, 0:128, :],
+        "wd": r.wfull.at[0:3, 0:128, :], "co": r.cotq_s.at[0:31], "cy": r.cotq.at[0:3], "na": r.nall.at[0:3],
+        "oz": r.o_s.at[0:3], "oy": r.att.at[0:3], "di": r.outgoing.at[0:31], "rs": r.rs, "ba": r.back_s.at[0:31],
+        "bc": r.wide_s.at[0:31], "gb": r.gb.at[0:3], "gy": r.gn.at[:, 0:3], "dz": r.dheads.at[0:3], "br": r.brs,
+        "bb": r.bs.at[0:31], "sb": r.sb, "xs": r.xs.at[0:3], "wg": r.wgs, "wz": r.wgq.at[0:3], "wx": r.wgr,
+        "wa": r.wgr, "wb": r.wgf.at[0, 0:3], "wc": r.wgf.at[0], "zd": r.zs.at[0:3, 0:64], "zq": r.zs.at[0:3, 64:192],
+        "wp": r.wrq, "wk": r.wrk, "ry": r.ry, "ay": r.ry, "sy": r.smally, "se": r.smalle.at[0:31],
+        "sf": r.smallf.at[0:31],
+    }
+    for name, ref in sent.items():
+        left(ref, getattr(ss, name).at[0])
+    for part in range(3):
+        left(r.pieces.at[0, 0, 0, 0:3], ss.pa.at[part])
+        left(r.pieces.at[0, 0, 0:3], ss.pb.at[part])
+        left(r.pieces.at[0, 0], ss.pc.at[part])
 
 
 def layer(*args):

time: 139 us -> 132 us (0.950)
  Pallas kernels: 138 us -> 131 us
    pallas_call x1, Pallas kernels: 130 us -> 123 us  [layer(): pl.pallas_call(layer_kernel, out_shape=[pltpu.VMEM(s, t) for s, t in OUTS...]
where the time goes in v6:
time: 132 us
  Pallas kernels  131 us (99%)
    pallas_call x1, Pallas kernels, layer(): pl.pallas_call(layer_kernel, out_shape=[pltpu.VMEM(s, t) for s, t in OUTS...  123 us
    pallas_call x1, Pallas kernels, finish(): pl.pallas_call(finish_kernel, out_shape=[jax.ShapeDtypeStruct(s, t) for s...  7.8 us

profile of v6, /device:TPU:1, one launch (start us, length us, event | category | flops | bytes accessed | tf_op | source)
XLA Modules:
  0.0 131.6 jit_solution(15851845378750413378)
XLA Ops:
  0.6 123.0 %layer.1 = (bf16[2,256,1024]{2,1,0:T(8,128)(2,1)S(1)}, bf16[2,256,1024]{2,1,0:T(8,128)(2,1)S(1)}, bf16[2,256,1024]{2,1,0:T(8,128)(2,1)S(1)}, bf16[2,256,1024]{2,...) custom-call(s32[9]{0:T(128)} %refs_0_.1, ...), custom_call_target="tpu_custom_call" | custom-call | tf_op jit(solution)/shard_map/layer/pallas_call | solution.py:847
  123.6 7.8 %finish.1 = (f32[2,1024,1024]{2,1,0:T(8,128)}, f32[2,1024,1024]{2,1,0:T(8,128)}, f32[3,1024,256]{2,1,0:T(8,128)}, f32[256,1024]{1,0:T(8,128)}, bf16[256,256]{1,0...) custom-call(bf16[2,256,1024]{2,1,0:T(8,128)(2,1)S(1)} %get-tuple-element.26.x, ...), custom_call_target="tpu_custom_call" | custom-call | flops 2147483648 | bytes 29360128 | tf_op jit(solution)/shard_map/finish/pallas_call | solution.py:889

commit v7 on v6

--- a/solution.py
+++ b/solution.py
@@ -139,7 +139,7 @@
     "vt1": ((80, 1024), bf16), "acc": ((4, 80, 256), f32), "peak": ((4, 1, 256), f32),
     "ot": ((4, 64, 256), f32), "lse": ((4, 1, 256), f32), "o_s": ((4, 64, 256), bf16),
     "att": ((4, 4, 64, 256), bf16), "cotq_s": ((32, 16, 256), bf16), "cotq": ((4, 32, 16, 256), bf16),
-    "outgoing": ((32, 16, 1024), bf16), "arrived": ((32, 16, 1024), bf16),
+    "slots": ((64, 16, 1024), bf16),
     "gh": (ROWS, f32),
     "part": ((2, 4, 256, 128), bf16), "rs": ((2, 3, 256, 128), bf16), "back_s": ((32, 16, 128), bf16),
     "back": ((32, 16, 128), bf16), "wide_s": ((32, 16, 512), bf16), "wide": ((32, 16, 512), bf16),
@@ -166,7 +166,7 @@
      "xs", "wg", "wz", "wx", "wa", "wb", "wc", "zd", "zq", "wp", "wk", "ry", "ay", "sy", "se", "sf"),
     (1,))
 SENT.update(pa=(3,), pb=(3,), pc=(3,))
-TAKEN = dict(SENT, az=(3,), ag=(16,), oz=(3,), sb=(4,), xs=(3,))
+TAKEN = dict(SENT, ry=(2,), az=(3,), ag=(16,), oz=(3,), sb=(4,), xs=(3,))
 
 
 class Refs:
@@ -252,9 +252,7 @@
     loads[0].wait()
     kt = transposed(dot(normed, r.wqkv[1]).astype(bf16))
     vt = transposed(dot(normed, r.wqkv[2]).astype(bf16))
-    qt = transposed((dot(normed, r.wqkv[0]).astype(bf16) * HEAD_DIM ** (-0.5)).astype(bf16))
     for h in range(4):
-        r.q_s[h] = qt[64 * h:64 * h + 64]
         r.kv_s[h, 0:64] = kt[64 * h:64 * h + 64]
         r.kv_s[h, 64:128] = vt[64 * h:64 * h + 64]
     greeted(bar)
@@ -289,6 +287,9 @@
         remote(r.kvt.at[6, zq], r.kvt.at[7, zq], ss.ag.at[0], rr.ag.at[3], sib).start()
 
     own_piece(0)
+    qt = transposed((dot(normed, r.wqkv[0]).astype(bf16) * HEAD_DIM ** (-0.5)).astype(bf16))
+    for h in range(4):
+        r.q_s[h] = qt[64 * h:64 * h + 64]
     for i in (1, 3, 2):
         zp, to = zpeer(i)
         push(r.q_s.at[zp], r.q.at[z], ss.aq.at[0], rr.aq.at[0], to)
@@ -490,18 +491,18 @@
     normed = (unit * r.gain2[...]).astype(bf16)
     for step in (1, 3, 2, 0):
         plane = lax.rem(z + step, 4)
-        r.outgoing[pl.ds(8 * plane, 8)] = dot(
+        r.slots[pl.ds(8 * plane, 8)] = dot(
             r.placer[pl.ds(pl.multiple_of(128 * plane, 128), 128), :], normed).astype(bf16).reshape(8, 16, 1024)
 
         def dispatch(k, carry):
             to = plane * 8 + lax.rem(j + k, 8)
             remote(
-                r.outgoing.at[to], r.arrived.at[ex], ss.di.at[0], rr.di.at[0],
+                r.slots.at[to], r.slots.at[32 + ex], ss.di.at[0], rr.di.at[0],
                 (to, mp)).start()
             return carry
 
         lax.fori_loop(0 if step else 1, 8, dispatch, 0)
-    r.arrived[ex] = r.outgoing[ex]
+    r.slots[32 + ex] = r.slots[ex]
     lax.fori_loop(4, 7, softmax, 0)
     loads[3].wait()
     arrive(r.cotq.at[0:3], rr.cy.at[0])
@@ -510,9 +511,9 @@
         r.crows[le] = rows
         r.gh[le] = dot(rows, r.weights[2 + le], 1, 1)
     loads[4].wait()
-    arrive(r.arrived.at[0:31], rr.di.at[0])
+    arrive(r.slots.at[32:63], rr.di.at[0])
     def expert_rows(le):
-        rows = one_expert(r.arrived[...], le)
+        rows = one_expert(r.slots[32:64], le)
         r.xrows[le] = rows
         return dot(rows, r.weights[le])
 
@@ -574,6 +575,12 @@
         ym, to = ypeer(i)
         push(r.gn.at[1, mp], r.gn.at[1, mp], ss.gy.at[0], rr.gy.at[0], to)
     unit, inverse = norm_parts(r.resid[...])
+    left(r.slots.at[0:31], ss.di.at[0])
+    load_keys(0, j)
+    for b in (3, 2, 1, 0):
+        n = 256 * b + 256
+        own = jnp.exp(scores(b, n, True) - r.lse[b]).astype(bf16)
+        r.slots[0:n // 16, :, 256 * b:256 * b + 256] = own.reshape(n // 16, 16, 256)
     arrive(r.gn.at[:, 0:3], rr.gy.at[0])
     grad = jnp.concatenate([r.gn[k % 2, k // 2] for k in range(8)], axis=1).astype(f32)
     grad_in, ggrad = norm_back(grad, r.gain2[...], unit, inverse)
@@ -709,9 +716,9 @@
 
     lax.fori_loop(0, 7, back_chunk, 0)
     load_back(0)
-    load_keys(0, j)
     backward(
-        [(b, 256 * b + 256) for b in (3, 2, 1, 0)], lambda b, n: jnp.exp(scores(b, n, True) - r.lse[b]))
+        [(b, 256 * b + 256) for b in (3, 2, 1, 0)],
+        lambda b, n: r.slots[0:n // 16, :, 256 * b:256 * b + 256].reshape(n, 256))
     for b in range(4):
         r.zs[b, 0:64] = (r.dq[b] * HEAD_DIM ** (-0.5)).astype(bf16)
     for i in (1, 3, 2):
@@ -774,53 +781,59 @@
     for i in (1, 3, 2):
         ym, to = ypeer(i)
         push(r.small, r.smally.at[i - 1], ss.sy.at[0], rr.sy.at[0], to)
-    for i in (1, 3, 2):
-        ym, to = ypeer(i)
-        push(r.gnp.at[ym], r.ry.at[i - 1], ss.ry.at[0], rr.ry.at[0], to)
-    gather_second(0)
+    for first in (0, 32):
+        rows = pl.ds(first, 32)
+        for i in (1, 3, 2):
+            ym, to = ypeer(i)
+            push(r.gnp.at[ym, rows, :], r.ry.at[i - 1, rows, :], ss.ry.at[0], rr.ry.at[first // 32], to)
     both = weight_sum((r.wpk, r.wrk), "wk")
     r.pieces[1, c, z, x] = both[0:64]
     r.pieces[2, c, z, x] = both[64:128]
     gather_first(1)
     gather_first(2)
+    gather_second(0)
+    arrive(r.wgf.at[0, 0:3], rr.wb.at[0])
+    push(r.wgf.at[c], r.wgf.at[c], ss.wc.at[0], rr.wc.at[0], sib)
+    def norm_rows(first):
+        grad = r.gnp[mp, first:first + 32].astype(f32)
+        arrive(r.ry.at[:, first:first + 32], rr.ry.at[first // 32])
+        for i in range(3):
+            grad = grad + r.ry[i, first:first + 32].astype(f32)
+        here = pl.ds(pl.multiple_of(64 * mp + first, 32), 32)
+        unit, inverse = norm_parts(r.tokens[here, :].astype(f32))
+        grad_in, _ = norm_back(grad, r.gain1[...], unit, inverse)
+        r.igrad[here, :] = (r.gres[here, :] + grad_in).astype(bf16)
+        for i in (1, 3, 2):
+            ym, to = ypeer(i)
+            push(r.igrad.at[here, :], r.igrad.at[here, :], ss.ay.at[0], rr.ay.at[0], to)
+
+    gather_second(1)
+    gather_second(2)
     arrive(r.smally, rr.sy.at[0])
     for i in range(3):
         one_gain = one_gain + r.smally[i]
     r.smalle[ex] = one_gain
     to_all(lambda to: r.smalle.at[ex], r.smalle.at[ex], "se")
-    gather_second(1)
-    gather_second(2)
+    norm_rows(0)
+    gather_third(0)
+    norm_rows(32)
     to_all(lambda to: r.bs.at[to], r.bret.at[ex], "bb")
     r.bret[ex] = r.bs[ex]
-    gather_third(0)
-    grad = r.gnp[mp].astype(f32)
-    arrive(r.ry, rr.ry.at[0])
-    for i in range(3):
-        grad = grad + r.ry[i].astype(f32)
-    here = pl.ds(pl.multiple_of(64 * mp, 64), 64)
-    unit, inverse = norm_parts(r.tokens[here, :].astype(f32))
-    grad_in, _ = norm_back(grad, r.gain1[...], unit, inverse)
-    r.igrad[here, :] = (r.gres[here, :] + grad_in).astype(bf16)
-    for i in (1, 3, 2):
-        ym, to = ypeer(i)
-        push(r.igrad.at[here, :], r.igrad.at[here, :], ss.ay.at[0], rr.ay.at[0], to)
-    gather_third(1)
-    gather_third(2)
-    arrive(r.wgf.at[0, 0:3], rr.wb.at[0])
-    push(r.wgf.at[c], r.wgf.at[c], ss.wc.at[0], rr.wc.at[0], sib)
     arrive(r.wgf.at[1 - c], rr.wc.at[0])
     for k in range(16):
         for core in range(2):
             r.wout_out[16 * k:16 * k + 16, 512 * core:512 * core + 512] = r.wgf[core, k // 4, k % 4]
+    gather_third(1)
+    gather_third(2)
+    arrive(r.smalle.at[0:31], rr.se.at[0])
+    arrive(r.smallf.at[0:31], rr.sf.at[0])
+    r.gain1_out[...] = jnp.sum(r.smalle[...], axis=0)
+    r.gain2_out[...] = jnp.sum(r.smallf[...], axis=0)
     for k in range(3):
         arrive(r.pieces.at[k, 1 - c], rr.pc.at[k])
         for row in range(8):
             block = jnp.concatenate([r.pieces[k, row % 2, h, row // 2] for h in range(4)], axis=0)
             r.qkv_out[k, 128 * row:128 * row + 128] = transposed(block)
-    arrive(r.smalle.at[0:31], rr.se.at[0])
-    arrive(r.smallf.at[0:31], rr.sf.at[0])
-    r.gain1_out[...] = jnp.sum(r.smalle[...], axis=0)
-    r.gain2_out[...] = jnp.sum(r.smallf[...], axis=0)
     arrive(r.bret.at[0:31], rr.bb.at[0])
     rows = dot(r.placer[...], r.bret[...].reshape(512, 256), 0, 0)
     r.out[...] = (r.rescol[...] + rows).astype(bf16)
@@ -828,7 +841,7 @@
     sent = {
         "az": r.kv_s.at[0:3], "aq": r.q_s.at[0:3], "ag": r.kvt.at[0:7], "wf": r.wfull.at[0:3, 0:128, :],
         "wd": r.wfull.at[0:3, 0:128, :], "co": r.cotq_s.at[0:31], "cy": r.cotq.at[0:3], "na": r.nall.at[0:3],
-        "oz": r.o_s.at[0:3], "oy": r.att.at[0:3], "di": r.outgoing.at[0:31], "rs": r.rs, "ba": r.back_s.at[0:31],
+        "oz": r.o_s.at[0:3], "oy": r.att.at[0:3], "rs": r.rs, "ba": r.back_s.at[0:31],
         "bc": r.wide_s.at[0:31], "gb": r.gb.at[0:3], "gy": r.gn.at[:, 0:3], "dz": r.dheads.at[0:3], "br": r.brs,
         "bb": r.bs.at[0:31], "sb": r.sb, "xs": r.xs.at[0:3], "wg": r.wgs, "wz": r.wgq.at[0:3], "wx": r.wgr,
         "wa": r.wgr, "wb": r.wgf.at[0, 0:3], "wc": r.wgf.at[0], "zd": r.zs.at[0:3, 0:64], "zq": r.zs.at[0:3, 64:192],

time: 132 us -> 130 us (0.985)
  Pallas kernels: 131 us -> 129 us
    pallas_call x1, Pallas kernels: 123 us -> 121 us  [layer(): pl.pallas_call(layer_kernel, out_shape=[pltpu.VMEM(s, t) for s, t in OUTS...]
where the time goes in v7:
time: 130 us
  Pallas kernels  129 us (99%)
    pallas_call x1, Pallas kernels, layer(): pl.pallas_call(layer_kernel, out_shape=[pltpu.VMEM(s, t) for s, t in OUTS...  121 us
    pallas_call x1, Pallas kernels, finish(): pl.pallas_call(finish_kernel, out_shape=[jax.ShapeDtypeStruct(s, t) for s...  7.79 us

profile of v7, /device:TPU:1, one launch (start us, length us, event | category | flops | bytes accessed | tf_op | source)
XLA Modules:
  0.0 130.1 jit_solution(5539918739606651965)
XLA Ops:
  0.6 121.5 %layer.1 = (bf16[2,256,1024]{2,1,0:T(8,128)(2,1)S(1)}, bf16[2,256,1024]{2,1,0:T(8,128)(2,1)S(1)}, bf16[2,256,1024]{2,1,0:T(8,128)(2,1)S(1)}, bf16[2,256,1024]{2,...) custom-call(s32[9]{0:T(128)} %refs_0_.1, ...), custom_call_target="tpu_custom_call" | custom-call | tf_op jit(solution)/shard_map/layer/pallas_call | solution.py:860
  122.1 7.8 %finish.1 = (f32[2,1024,1024]{2,1,0:T(8,128)}, f32[2,1024,1024]{2,1,0:T(8,128)}, f32[3,1024,256]{2,1,0:T(8,128)}, f32[256,1024]{1,0:T(8,128)}, bf16[256,256]{1,0...) custom-call(bf16[2,256,1024]{2,1,0:T(8,128)(2,1)S(1)} %get-tuple-element.26.x, ...), custom_call_target="tpu_custom_call" | custom-call | flops 2147483648 | bytes 29360128 | tf_op jit(solution)/shard_map/finish/pallas_call | solution.py:902

commit v8 on v7

--- a/solution.py
+++ b/solution.py
@@ -149,7 +149,7 @@
     "wgz": ((3, 4, 16, 512), bf16), "wgx": ((4, 16, 512), bf16), "wgr": ((3, 16, 512), bf16),
     "wgf": ((2, 4, 4, 16, 512), bf16),
     "dheads": ((4, 64, 256), bf16), "dob": ((4, 64, 256), bf16), "brs": ((3, 32, 16, 256), bf16),
-    "bs": ((32, 16, 256), bf16), "bret": ((32, 16, 256), bf16), "dopad": ((4, 128, 256), bf16),
+    "bs": ((32, 16, 256), bf16), "bz": ((4, 8, 16, 256), bf16), "bret": ((4, 8, 16, 256), bf16), "dopad": ((4, 128, 256), bf16),
     "qd": ((4, 512, 128), bf16), "delta": ((4, 1, 256), f32), "kvn": ((1024, 128), bf16),
     "kt": ((64, 1024), bf16), "dkv": ((1024, 128), f32), "dq": ((4, 64, 256), f32),
     "sb": ((4, 1024, 128), bf16), "sr": ((4, 1024, 128), bf16), "xs": ((4, 1024, 128), bf16),
@@ -158,12 +158,12 @@
     "wpk": ((8, 128, 128), bf16), "wrk": ((7, 128, 128), bf16),
     "pieces": ((3, 2, 4, 4, 64, 128), bf16),
     "gnp": ((4, 64, 1024), bf16), "ry": ((3, 64, 1024), bf16), "small": ((1, 1024), f32),
-    "smally": ((3, 1, 1024), f32), "smalle": ((32, 1, 1024), f32), "smallf": ((32, 1, 1024), f32),
+    "smally": ((3, 1, 1024), f32), "gsum": ((2, 1024), f32), "gz": ((3, 2, 1024), f32), "gps": ((2, 1024), f32), "gp": ((7, 2, 1024), f32),
 }
 LOCAL = {"load": (5,)}
 SENT = dict.fromkeys(
     ("az", "aq", "ag", "wf", "wd", "co", "cy", "na", "oz", "oy", "di", "rs", "ba", "bc", "gb", "gy", "dz", "br", "bb", "sb",
-     "xs", "wg", "wz", "wx", "wa", "wb", "wc", "zd", "zq", "wp", "wk", "ry", "ay", "sy", "se", "sf"),
+     "xs", "wg", "wz", "wx", "wa", "wb", "wc", "zd", "zq", "wp", "wk", "ry", "ay", "sy", "se", "sf", "bp"),
     (1,))
 SENT.update(pa=(3,), pb=(3,), pc=(3,))
 TAKEN = dict(SENT, ry=(2,), az=(3,), ag=(16,), oz=(3,), sb=(4,), xs=(3,))
@@ -584,7 +584,7 @@
     arrive(r.gn.at[:, 0:3], rr.gy.at[0])
     grad = jnp.concatenate([r.gn[k % 2, k // 2] for k in range(8)], axis=1).astype(f32)
     grad_in, ggrad = norm_back(grad, r.gain2[...], unit, inverse)
-    r.smallf[ex] = ggrad
+    r.gsum[1:2] = ggrad
     gres = r.cot[...].astype(f32) + grad_in
     r.gres[...] = gres
     low = gres.astype(bf16)
@@ -603,7 +603,6 @@
             r.branch.at[:, :, pl.ds(pl.multiple_of(256 * ym, 256), 256)], r.brs.at[i - 1],
             ss.br.at[0], rr.br.at[0], to)
     zero = jnp.zeros((64, 256), bf16)
-    to_all(lambda to: r.smallf.at[ex], r.smallf.at[ex], "sf")
     arrive(r.dob.at[0:3], rr.dz.at[0])
     arrive(r.wgs, rr.wg.at[0])
     r.wgq[...] = (r.wgp[c].astype(f32) + r.wgs[...].astype(f32)).astype(bf16)
@@ -700,6 +699,11 @@
             for k in range(3):
                 total = total + r.brs[k].astype(f32)
             r.bs[...] = total.astype(bf16)
+            for k in (1, 3, 2):
+                zp, to = zpeer(k)
+                remote(
+                    r.bs.at[pl.ds(8 * zp, 8)], r.bz.at[z], ss.bb.at[0], rr.bb.at[0], to).start()
+            r.bz[z] = r.bs[pl.ds(8 * z, 8)]
 
         @pl.when(i == 5)
         def _():
@@ -809,44 +813,54 @@
 
     gather_second(1)
     gather_second(2)
+    arrive(r.bz.at[0:3], rr.bb.at[0])
+    for i in range(1, 8):
+        jt = lax.rem(j + i, 8)
+        push(r.bz.at[:, jt], r.bret.at[:, j], ss.bp.at[0], rr.bp.at[0], (z * 8 + jt, mp))
+    for b in range(4):
+        r.bret[b, j] = r.bz[b, j]
     arrive(r.smally, rr.sy.at[0])
     for i in range(3):
         one_gain = one_gain + r.smally[i]
-    r.smalle[ex] = one_gain
-    to_all(lambda to: r.smalle.at[ex], r.smalle.at[ex], "se")
+    r.gsum[0:1] = one_gain
+    for i in (1, 3, 2):
+        _, to = zpeer(i)
+        push(r.gsum, r.gz.at[i - 1], ss.se.at[0], rr.se.at[0], to)
     norm_rows(0)
     gather_third(0)
     norm_rows(32)
-    to_all(lambda to: r.bs.at[to], r.bret.at[ex], "bb")
-    r.bret[ex] = r.bs[ex]
+    arrive(r.gz, rr.se.at[0])
+    r.gps[...] = r.gsum[...] + r.gz[0] + r.gz[1] + r.gz[2]
+    for i in range(1, 8):
+        jt = lax.rem(j + i, 8)
+        push(r.gps, r.gp.at[i - 1], ss.sf.at[0], rr.sf.at[0], (z * 8 + jt, mp))
     arrive(r.wgf.at[1 - c], rr.wc.at[0])
     for k in range(16):
         for core in range(2):
             r.wout_out[16 * k:16 * k + 16, 512 * core:512 * core + 512] = r.wgf[core, k // 4, k % 4]
     gather_third(1)
     gather_third(2)
-    arrive(r.smalle.at[0:31], rr.se.at[0])
-    arrive(r.smallf.at[0:31], rr.sf.at[0])
-    r.gain1_out[...] = jnp.sum(r.smalle[...], axis=0)
-    r.gain2_out[...] = jnp.sum(r.smallf[...], axis=0)
     for k in range(3):
         arrive(r.pieces.at[k, 1 - c], rr.pc.at[k])
         for row in range(8):
             block = jnp.concatenate([r.pieces[k, row % 2, h, row // 2] for h in range(4)], axis=0)
             r.qkv_out[k, 128 * row:128 * row + 128] = transposed(block)
-    arrive(r.bret.at[0:31], rr.bb.at[0])
+    arrive(r.bret.at[:, 0:7], rr.bp.at[0])
     rows = dot(r.placer[...], r.bret[...].reshape(512, 256), 0, 0)
     r.out[...] = (r.rescol[...] + rows).astype(bf16)
+    arrive(r.gp, rr.sf.at[0])
+    both = r.gps[...] + jnp.sum(r.gp[...], axis=0)
+    r.gain1_out[...] = both[0:1]
+    r.gain2_out[...] = both[1:2]
     arrive(r.igrad.at[0:192, :], rr.ay.at[0])
     sent = {
         "az": r.kv_s.at[0:3], "aq": r.q_s.at[0:3], "ag": r.kvt.at[0:7], "wf": r.wfull.at[0:3, 0:128, :],
         "wd": r.wfull.at[0:3, 0:128, :], "co": r.cotq_s.at[0:31], "cy": r.cotq.at[0:3], "na": r.nall.at[0:3],
         "oz": r.o_s.at[0:3], "oy": r.att.at[0:3], "rs": r.rs, "ba": r.back_s.at[0:31],
         "bc": r.wide_s.at[0:31], "gb": r.gb.at[0:3], "gy": r.gn.at[:, 0:3], "dz": r.dheads.at[0:3], "br": r.brs,
-        "bb": r.bs.at[0:31], "sb": r.sb, "xs": r.xs.at[0:3], "wg": r.wgs, "wz": r.wgq.at[0:3], "wx": r.wgr,
+        "bb": r.bz.at[0:3], "bp": r.bret.at[:, 0:7], "sb": r.sb, "xs": r.xs.at[0:3], "wg": r.wgs, "wz": r.wgq.at[0:3], "wx": r.wgr,
         "wa": r.wgr, "wb": r.wgf.at[0, 0:3], "wc": r.wgf.at[0], "zd": r.zs.at[0:3, 0:64], "zq": r.zs.at[0:3, 64:192],
-        "wp": r.wrq, "wk": r.wrk, "ry": r.ry, "ay": r.ry, "sy": r.smally, "se": r.smalle.at[0:31],
-        "sf": r.smallf.at[0:31],
+        "wp": r.wrq, "wk": r.wrk, "ry": r.ry, "ay": r.ry, "sy": r.smally, "se": r.gz, "sf": r.gp,
     }
     for name, ref in sent.items():
         left(ref, getattr(ss, name).at[0])

time: 130 us -> 129 us (level)
    pallas_call x1, Pallas kernels: 121 us -> 120 us  [layer(): pl.pallas_call(layer_kernel, out_shape=[pltpu.VMEM(s, t) for s, t in OUTS...]
where the time goes in v8:
time: 129 us
  Pallas kernels  128 us (99%)
    pallas_call x1, Pallas kernels, layer(): pl.pallas_call(layer_kernel, out_shape=[pltpu.VMEM(s, t) for s, t in OUTS...  120 us
    pallas_call x1, Pallas kernels, finish(): pl.pallas_call(finish_kernel, out_shape=[jax.ShapeDtypeStruct(s, t) for s...  7.81 us

profile of v8, /device:TPU:1, one launch (start us, length us, event | category | flops | bytes accessed | tf_op | source)
XLA Modules:
  0.0 128.5 jit_solution(3140102765127547707)
XLA Ops:
  0.6 119.9 %layer.1 = (bf16[2,256,1024]{2,1,0:T(8,128)(2,1)S(1)}, bf16[2,256,1024]{2,1,0:T(8,128)(2,1)S(1)}, bf16[2,256,1024]{2,1,0:T(8,128)(2,1)S(1)}, bf16[2,256,1024]{2,...) custom-call(s32[9]{0:T(128)} %refs_0_.1, ...), custom_call_target="tpu_custom_call" | custom-call | tf_op jit(solution)/shard_map/layer/pallas_call | solution.py:874
  120.5 7.8 %finish.1 = (f32[2,1024,1024]{2,1,0:T(8,128)}, f32[2,1024,1024]{2,1,0:T(8,128)}, f32[3,1024,256]{2,1,0:T(8,128)}, f32[256,1024]{1,0:T(8,128)}, bf16[256,256]{1,0...) custom-call(bf16[2,256,1024]{2,1,0:T(8,128)(2,1)S(1)} %get-tuple-element.26.x, ...), custom_call_target="tpu_custom_call" | custom-call | flops 2147483648 | bytes 29360128 | tf_op jit(solution)/shard_map/finish/pallas_call | solution.py:916

commit v9 on v8

--- a/solution.py
+++ b/solution.py
@@ -124,13 +124,14 @@
 DMA = pltpu.SemaphoreType.DMA
 ROWS = (2, 256, 1024)
 
-ARGS = ["lengths", "tokens", "gain1", "gain2", "chosen", "wqkv_hbm", "wout_hbm", "cot_hbm", "win_hbm", "wex_hbm"]
+ARGS = ["lengths", "tokens_hbm", "gain1", "gain2", "chosen", "wqkv_hbm", "wout_hbm", "cot_hbm", "win_hbm", "wex_hbm"]
 OUTS = {
     "xrows": (ROWS, bf16), "crows": (ROWS, bf16), "hid": (ROWS, bf16), "gpre": (ROWS, bf16),
     "out": ((256, 256), bf16), "igrad": ((256, 1024), bf16), "gain1_out": ((1, 1024), f32), "gain2_out": ((1, 1024), f32),
     "qkv_out": ((3, 1024, 256), bf16), "wout_out": ((256, 1024), bf16),
 }
 BUFFERS = {
+    "tokens": ((256, 1024), bf16),
     "wqkv": ((3, 1024, 256), bf16), "cot": ((256, 1024), bf16),
     "weights": ((7, 1024, 1024), bf16), "placer": ((512, 256), bf16), "normed": ((256, 1024), bf16),
     "nall": ((4, 256, 1024), bf16), "wfull": ((4, 256, 1024), bf16),
@@ -160,7 +161,7 @@
     "gnp": ((4, 64, 1024), bf16), "ry": ((3, 64, 1024), bf16), "small": ((1, 1024), f32),
     "smally": ((3, 1, 1024), f32), "gsum": ((2, 1024), f32), "gz": ((3, 2, 1024), f32), "gps": ((2, 1024), f32), "gp": ((7, 2, 1024), f32),
 }
-LOCAL = {"load": (5,)}
+LOCAL = {"load": (6,)}
 SENT = dict.fromkeys(
     ("az", "aq", "ag", "wf", "wd", "co", "cy", "na", "oz", "oy", "di", "rs", "ba", "bc", "gb", "gy", "dz", "br", "bb", "sb",
      "xs", "wg", "wz", "wx", "wa", "wb", "wc", "zd", "zq", "wp", "wk", "ry", "ay", "sy", "se", "sf", "bp"),
@@ -237,19 +238,20 @@
         arrive(r.pieces.at[part, 0, 0:3], rr.pb.at[part])
         push(r.pieces.at[part, c], r.pieces.at[part, c], ss.pc.at[part], rr.pc.at[part], sib)
 
-    bar = greet(ex, mp)
     loads = [
         pltpu.make_async_copy(src, dst, ls.load.at[i])
         for i, (src, dst) in enumerate([
-            (r.wqkv_hbm, r.wqkv), (r.wout_hbm, r.wfull.at[mp]), (r.cot_hbm, r.cot), (r.wex_hbm, r.weights.at[2:4]),
+            (r.tokens_hbm, r.tokens), (r.wqkv_hbm, r.wqkv), (r.wout_hbm, r.wfull.at[mp]), (r.cot_hbm, r.cot), (r.wex_hbm, r.weights.at[2:4]),
             (r.win_hbm, r.weights.at[0:2])])
     ]
     for copy in loads:
         copy.start()
+    bar = greet(ex, mp)
+    loads[0].wait()
     unit, _ = norm_parts(r.tokens[...].astype(f32))
     normed = (unit * r.gain1[...]).astype(bf16)
     r.normed[...] = normed
-    loads[0].wait()
+    loads[1].wait()
     kt = transposed(dot(normed, r.wqkv[1]).astype(bf16))
     vt = transposed(dot(normed, r.wqkv[2]).astype(bf16))
     for h in range(4):
@@ -294,7 +296,7 @@
         zp, to = zpeer(i)
         push(r.q_s.at[zp], r.q.at[z], ss.aq.at[0], rr.aq.at[0], to)
     r.q[z] = r.q_s[z]
-    loads[1].wait()
+    loads[2].wait()
     half = pl.ds(pl.multiple_of(128 * c, 128), 128)
     for i in range(1, 4):
         ym, to = ypeer(i)
@@ -302,7 +304,7 @@
     r.vt1[64:80, :] = jnp.ones((16, 1024), bf16)
     ends = doc_ends(r.lengths)
     feature = lax.broadcasted_iota(jnp.int32, (64, 256), 0)
-    loads[2].wait()
+    loads[3].wait()
     mine = pl.ds(pl.multiple_of(256 * mp, 256), 256)
     r.placer[...] = slot_matrix(r.chosen[...])
     r.cotq_s[...] = dot(r.placer[...], r.cot[:, mine]).astype(bf16).reshape(EX, 16, 256)
@@ -504,13 +506,13 @@
         lax.fori_loop(0 if step else 1, 8, dispatch, 0)
     r.slots[32 + ex] = r.slots[ex]
     lax.fori_loop(4, 7, softmax, 0)
-    loads[3].wait()
+    loads[4].wait()
     arrive(r.cotq.at[0:3], rr.cy.at[0])
     for le in range(2):
         rows = jnp.concatenate([one_expert(r.cotq[k], le) for k in range(4)], axis=1)
         r.crows[le] = rows
         r.gh[le] = dot(rows, r.weights[2 + le], 1, 1)
-    loads[4].wait()
+    loads[5].wait()
     arrive(r.slots.at[32:63], rr.di.at[0])
     def expert_rows(le):
         rows = one_expert(r.slots[32:64], le)
@@ -874,7 +876,7 @@
     return pl.pallas_call(
         layer_kernel,
         out_shape=[pltpu.VMEM(s, t) for s, t in OUTS.values()],
-        in_specs=[SM, VM, VM, VM, VM, ANY, ANY, ANY, ANY, ANY],
+        in_specs=[SM, ANY, VM, VM, VM, ANY, ANY, ANY, ANY, ANY],
         out_specs=[VM] * len(OUTS),
         scratch_shapes=[pltpu.VMEM(s, t) for s, t in BUFFERS.values()]
         + [DMA(s) for group in (LOCAL, SENT, TAKEN) for s in group.values()],

time: 129 us -> 129 us (level)
  no operation moved by 1% of the time
where the time goes in v9:
time: 129 us; the launch traced here: 128 us
  Pallas kernels  128 us (99%)
    pallas_call x1, Pallas kernels, layer(): pl.pallas_call(layer_kernel, out_shape=[pltpu.VMEM(s, t) for s, t in OUTS...  120 us
    pallas_call x1, Pallas kernels, finish(): pl.pallas_call(finish_kernel, out_shape=[jax.ShapeDtypeStruct(s, t) for s...  7.8 us

profile of v9, /device:TPU:1, one launch (start us, length us, event | category | flops | bytes accessed | tf_op | source)
XLA Modules:
  0.0 128.4 jit_solution(17879691659908659691)
XLA Ops:
  0.6 119.8 %layer.1 = (bf16[2,256,1024]{2,1,0:T(8,128)(2,1)S(1)}, bf16[2,256,1024]{2,1,0:T(8,128)(2,1)S(1)}, bf16[2,256,1024]{2,1,0:T(8,128)(2,1)S(1)}, bf16[2,256,1024]{2,...) custom-call(s32[9]{0:T(128)} %refs_0_.1, ...), custom_call_target="tpu_custom_call" | custom-call | tf_op jit(solution)/shard_map/layer/pallas_call | solution.py:876
  120.4 7.8 %finish.1 = (f32[2,1024,1024]{2,1,0:T(8,128)}, f32[2,1024,1024]{2,1,0:T(8,128)}, f32[3,1024,256]{2,1,0:T(8,128)}, f32[256,1024]{1,0:T(8,128)}, bf16[256,256]{1,0...) custom-call(bf16[2,256,1024]{2,1,0:T(8,128)(2,1)S(1)} %get-tuple-element.26.x, ...), custom_call_target="tpu_custom_call" | custom-call | flops 2147483648 | bytes 29360128 | tf_op jit(solution)/shard_map/finish/pallas_call | solution.py:918
